TPU v7x, 32 devices: a whole 2x2x4 slice. The times are simulated.
32 devices in a mesh: ctx: 8 (over z, x), fsdp: 4 (over y, core).
Axes of the slice: x: 2, y: 2, z: 4, core: 2. Of those that a mesh axis runs over, the one named last changes fastest.
Arguments:
- tokens: bfloat16 [4, 1024, 768], P('fsdp', 'ctx'), may hold values from -6 to 6
- doc_lengths: int32 [4, 4], P('fsdp'), may hold values from 1 to 960, as said below
- routes: int32 [4, 1024, 2], P('fsdp', 'ctx'), may hold values from 0 to 3, all different within a row
- cotangent: bfloat16 [4, 1024, 768], P('fsdp', 'ctx'), may hold values from -6 to 6
- attn_gain: bfloat16 [768], P(('ctx', 'fsdp')), may hold values from 0.25 to 1.75
- w_qkv: bfloat16 [768, 2304], P(('ctx', 'fsdp')), may hold values from -0.21875 to 0.21875
- w_out: bfloat16 [768, 768], P(('ctx', 'fsdp')), may hold values from -2.5 to 2.5
- mlp_gain: bfloat16 [768], P(('ctx', 'fsdp')), may hold values from 0.25 to 1.75
- router: bfloat16 [768, 4], P(('ctx', 'fsdp')), may hold values from -0.15625 to 0.15625
- expert_in: bfloat16 [2048, 4, 2, 768], P(('ctx', 'fsdp')), may hold values from -0.21875 to 0.21875
- expert_out: bfloat16 [2048, 4, 768], P(('ctx', 'fsdp')), may hold values from -0.375 to 0.375
- shared_in: bfloat16 [2048, 2, 768], P(('ctx', 'fsdp')), may hold values from -0.21875 to 0.21875
- shared_out: bfloat16 [2048, 768], P(('ctx', 'fsdp')), may hold values from -0.25 to 0.25
Outputs:
- layer_out: bfloat16 [4, 1024, 768], P('fsdp', 'ctx')
- grad_tokens: float32 [4, 1024, 768], P('fsdp', 'ctx')
- grad_attn_gain: float32 [768], P(('ctx', 'fsdp'))
- grad_w_qkv: float32 [768, 2304], P(('ctx', 'fsdp'))
- grad_w_out: float32 [768, 768], P(('ctx', 'fsdp'))
- grad_mlp_gain: float32 [768], P(('ctx', 'fsdp'))
- grad_router: float32 [768, 4], P(('ctx', 'fsdp'))
- grad_expert_in: float32 [2048, 4, 2, 768], P(('ctx', 'fsdp'))
- grad_expert_out: float32 [2048, 4, 768], P(('ctx', 'fsdp'))
- grad_shared_in: float32 [2048, 2, 768], P(('ctx', 'fsdp'))
- grad_shared_out: float32 [2048, 768], P(('ctx', 'fsdp'))
Inputs may be any that keep to these rules, and one draw needn't show every extreme that they name: `doc_lengths`: in each slot the lengths sum to less than 1024; rows past the sum are padding. Each slot holds one document of exactly 960 rows and at least one of a single row. `routes`: each token names 2 different experts, in order of priority.
All inputs are finite; a program needn't handle non-finite values.
Results may differ from a plain program's by a relative error of at most 0.035.
Values may be sent and summed in bfloat16 or wider, within the bound.
A program may use at most 448 MiB of HBM per device.

v0:
```python
import math

import jax
import jax.numpy as jnp
from jax import lax
from jax.sharding import PartitionSpec as P

HEAD_DIM = 64


EPSILON = 1e-05
ROPE_BASE = 10000.0
MASKED = -1e30
PRECISE = lax.Precision.HIGHEST


def doc_ids(row_index, doc_ends):
    return jnp.sum((row_index[:, None] >= doc_ends[None, :]).astype(jnp.int32), axis=1)


def positions(row_index, lengths):
    doc_ends = jnp.cumsum(lengths)
    doc_starts = doc_ends - lengths
    doc_num = doc_ids(row_index, doc_ends)
    column = jnp.arange(lengths.shape[0], dtype=jnp.int32)
    begins = jnp.sum(jnp.where(doc_num[:, None] == column[None, :], doc_starts[None, :], 0), axis=1)
    return (doc_num, row_index - begins, doc_ends)


def rope_tables(position, head_dim):
    half_dim = head_dim // 2
    inverse = ROPE_BASE ** (-2.0 * jnp.arange(half_dim, dtype=jnp.float32) / head_dim)
    angles = position.astype(jnp.float32)[:, None] * inverse[None, :]
    return (jnp.cos(angles), jnp.sin(angles))


def rotate(values, cosine, sine_tab):
    half_dim = values.shape[-1] // 2
    lower_half = values[..., :half_dim]
    upper_half = values[..., half_dim:]
    cos_b = cosine[:, None, :]
    sin_b = sine_tab[:, None, :]
    return jnp.concatenate(
        [lower_half * cos_b - upper_half * sin_b, upper_half * cos_b + lower_half * sin_b], axis=-1
    )


def placement(route_rows, live_rows, expert_count, capacity):
    tok_count = route_rows.shape[0]
    top_k = route_rows.shape[1]
    expert_of = route_rows.T.reshape(-1)
    token_of = jnp.tile(jnp.arange(tok_count, dtype=jnp.int32), top_k)
    pair_live = jnp.tile(live_rows, top_k)
    expert_raw = expert_of[:, None] == jnp.arange(expert_count, dtype=jnp.int32)[None, :]
    expert_hot = (expert_raw & pair_live[:, None]).astype(jnp.int32)
    earlier = jnp.cumsum(expert_hot, axis=0) - expert_hot
    slot_of = jnp.sum(earlier * expert_hot, axis=1)
    kept_pair = pair_live & (slot_of < capacity)
    flat_slot = expert_of * capacity + slot_of
    slot_ids = jnp.arange(expert_count * capacity, dtype=jnp.int32)
    pair_place = ((flat_slot[:, None] == slot_ids[None, :]) & kept_pair[:, None]).astype(
        jnp.float32
    )
    token_hot = (token_of[:, None] == jnp.arange(tok_count, dtype=jnp.int32)[None, :]).astype(
        jnp.float32
    )
    return (pair_place, token_hot, expert_raw.astype(jnp.float32))


def rms_forward(values, gain):
    inv_rms = lax.rsqrt(jnp.mean(values * values, axis=-1, keepdims=True) + EPSILON)
    return (values * inv_rms * gain, inv_rms)


def rms_backward(values, inv_rms, gain, grad_out):
    weighted = grad_out * gain
    inner = jnp.mean(weighted * values, axis=-1, keepdims=True)
    grad_in = inv_rms * weighted - values * inner * inv_rms**3
    return (grad_in, jnp.sum(grad_out * values * inv_rms, axis=0))


def body(
    tokens,
    doc_lengths,
    routes,
    cotangent,
    attn_gain,
    w_qkv,
    w_out,
    mlp_gain,
    router,
    expert_in,
    expert_out,
    shared_in,
    shared_out,
):
    tok_count = tokens.shape[1]
    model_dim = tokens.shape[2]
    head_count = model_dim // HEAD_DIM
    expert_count = expert_in.shape[1]
    hidden_count = expert_in.shape[0]
    top_k = routes.shape[2]
    capacity = 5 * top_k * tok_count // (4 * expert_count)
    slot_rows = expert_count * capacity
    score_scale = 1.0 / math.sqrt(HEAD_DIM)
    head_shape = (tok_count, head_count, HEAD_DIM)
    row_index = lax.axis_index("ctx") * tok_count + jnp.arange(tok_count, dtype=jnp.int32)
    lengths = doc_lengths[0]
    doc_num, position, doc_ends = positions(row_index, lengths)
    live_rows = doc_num < lengths.shape[0]
    live_mask = live_rows.astype(jnp.float32)[:, None]
    gain_a, weight_qkv, weight_out, gain_m, router_full = (
        lax.all_gather(attn_gain, ("ctx", "fsdp"), axis=0, tiled=True),
        lax.all_gather(w_qkv, ("ctx", "fsdp"), axis=0, tiled=True),
        lax.all_gather(w_out, ("ctx", "fsdp"), axis=0, tiled=True),
        lax.all_gather(mlp_gain, ("ctx", "fsdp"), axis=0, tiled=True),
        lax.all_gather(router, ("ctx", "fsdp"), axis=0, tiled=True),
    )
    inputs = tokens[0].astype(jnp.float32)
    normed, inv_attn = rms_forward(inputs, gain_a.astype(jnp.float32))
    normed_b = normed.astype(jnp.bfloat16)
    proj_qkv = jnp.dot(normed_b, weight_qkv, preferred_element_type=jnp.float32)
    cosine, sine_tab = rope_tables(position, HEAD_DIM)
    query_b = rotate(proj_qkv[:, :model_dim].reshape(head_shape), cosine, sine_tab).astype(
        jnp.bfloat16
    )
    key_b = rotate(
        proj_qkv[:, model_dim : 2 * model_dim].reshape(head_shape), cosine, sine_tab
    ).astype(jnp.bfloat16)
    value_b = proj_qkv[:, 2 * model_dim :].reshape(head_shape).astype(jnp.bfloat16)

    def allowed_mask(query_index, key_index):
        same_doc = doc_ids(query_index, doc_ends)[:, None] == doc_ids(key_index, doc_ends)[None, :]
        return (same_doc & (key_index[None, :] <= query_index[:, None]))[None]

    start_state = (
        jnp.full((head_count, tok_count), MASKED, jnp.float32),
        jnp.zeros((head_count, tok_count), jnp.float32),
        jnp.zeros(head_shape, jnp.float32),
    )
    keys_part = lax.all_gather(key_b, "ctx", axis=0, tiled=True)
    values_part = lax.all_gather(value_b, "ctx", axis=0, tiled=True)
    width = math.gcd(keys_part.shape[0], 512)

    def attend_key_step(number, loop_state):
        run_max, run_sum, accumulated = loop_state
        begin_at = number * width
        key_blk = lax.dynamic_slice_in_dim(keys_part, begin_at, width, 0)
        value_blk = lax.dynamic_slice_in_dim(values_part, begin_at, width, 0)
        allowed = allowed_mask(row_index, begin_at + jnp.arange(width, dtype=jnp.int32))
        scores = (
            jnp.einsum("qhd,khd->hqk", query_b, key_blk, preferred_element_type=jnp.float32)
            * score_scale
        )
        scores = jnp.where(allowed, scores, MASKED)
        new_max = jnp.maximum(run_max, jnp.max(scores, axis=-1))
        expo_vals = jnp.where(allowed, jnp.exp(scores - new_max[:, :, None]), 0.0)
        factor = jnp.exp(run_max - new_max)
        run_sum = run_sum * factor + jnp.sum(expo_vals, axis=-1)
        accumulated = accumulated * factor.T[:, :, None] + jnp.einsum(
            "hqk,khd->qhd",
            expo_vals.astype(jnp.bfloat16),
            value_blk,
            preferred_element_type=jnp.float32,
        )
        return (new_max, run_sum, accumulated)

    run_max, run_sum, accumulated = lax.fori_loop(
        0, keys_part.shape[0] // width, attend_key_step, start_state
    )
    attn_heads = accumulated / run_sum.T[:, :, None]
    log_heads = run_max + jnp.log(run_sum)
    attn_b = attn_heads.reshape(tok_count, model_dim).astype(jnp.bfloat16)
    resid = inputs + jnp.dot(attn_b, weight_out, preferred_element_type=jnp.float32)
    mixed, inv_mlp = rms_forward(resid, gain_m.astype(jnp.float32))
    mixed_b = mixed.astype(jnp.bfloat16)
    logits = jnp.dot(mixed_b, router_full, preferred_element_type=jnp.float32)
    shifted = jnp.exp(logits - jnp.max(logits, axis=-1, keepdims=True))
    router_probs = shifted / jnp.sum(shifted, axis=-1, keepdims=True)
    pair_place, token_hot, expert_raw = placement(routes[0], live_rows, expert_count, capacity)
    gate_pair = jnp.sum(jnp.dot(token_hot, router_probs, precision=PRECISE) * expert_raw, axis=1)
    dispatch = jnp.dot(pair_place.T, token_hot, precision=PRECISE)
    combine = jnp.dot(pair_place.T, token_hot * gate_pair[:, None], precision=PRECISE)
    slot_in = (
        jnp.dot(dispatch.astype(jnp.bfloat16), mixed_b, preferred_element_type=jnp.float32)
        .astype(jnp.bfloat16)
        .reshape(expert_count, capacity, model_dim)
    )

    def expert_pre(part_in):
        gate_e = jnp.einsum(
            "ecd,fed->ecf", slot_in, part_in[:, :, 0, :], preferred_element_type=jnp.float32
        )
        up_e = jnp.einsum(
            "ecd,fed->ecf", slot_in, part_in[:, :, 1, :], preferred_element_type=jnp.float32
        )
        return (gate_e, up_e)

    def shared_pre(part_sin):
        gate_s = jnp.einsum(
            "td,fd->tf", mixed_b, part_sin[:, 0, :], preferred_element_type=jnp.float32
        )
        up_s = jnp.einsum(
            "td,fd->tf", mixed_b, part_sin[:, 1, :], preferred_element_type=jnp.float32
        )
        return (gate_s, up_s)

    group_in, group_out, group_sin, group_sout = (
        lax.all_gather(expert_in, "fsdp", axis=0, tiled=True),
        lax.all_gather(expert_out, "fsdp", axis=0, tiled=True),
        lax.all_gather(shared_in, "fsdp", axis=0, tiled=True),
        lax.all_gather(shared_out, "fsdp", axis=0, tiled=True),
    )
    part_in = lax.all_gather(group_in, "ctx", axis=0, tiled=True)
    part_out = lax.all_gather(group_out, "ctx", axis=0, tiled=True)
    part_sin = lax.all_gather(group_sin, "ctx", axis=0, tiled=True)
    part_sout = lax.all_gather(group_sout, "ctx", axis=0, tiled=True)
    gate_e, up_e = expert_pre(part_in)
    hidden_e = (gate_e * jax.nn.sigmoid(gate_e) * up_e).astype(jnp.bfloat16)
    routed_sum = jnp.einsum("ecf,fed->ecd", hidden_e, part_out, preferred_element_type=jnp.float32)
    gate_s, up_s = shared_pre(part_sin)
    hidden_s = (gate_s * jax.nn.sigmoid(gate_s) * up_s).astype(jnp.bfloat16)
    shared_sum = jnp.einsum("tf,fd->td", hidden_s, part_sout, preferred_element_type=jnp.float32)
    expert_flat = routed_sum.reshape(slot_rows, model_dim)
    routed = jnp.dot(combine.T, expert_flat, precision=PRECISE)
    layer_out = (live_mask * (resid + routed + shared_sum)).astype(jnp.bfloat16)[None]
    gain_a, weight_qkv, weight_out, gain_m, router_full = (
        lax.all_gather(attn_gain, ("ctx", "fsdp"), axis=0, tiled=True),
        lax.all_gather(w_qkv, ("ctx", "fsdp"), axis=0, tiled=True),
        lax.all_gather(w_out, ("ctx", "fsdp"), axis=0, tiled=True),
        lax.all_gather(mlp_gain, ("ctx", "fsdp"), axis=0, tiled=True),
        lax.all_gather(router, ("ctx", "fsdp"), axis=0, tiled=True),
    )
    grad_top = cotangent[0].astype(jnp.float32) * live_mask
    grad_ye_b = (
        jnp.dot(combine, grad_top, precision=PRECISE)
        .astype(jnp.bfloat16)
        .reshape(expert_count, capacity, model_dim)
    )
    grad_sh_b = grad_top.astype(jnp.bfloat16)
    routed_grad = jnp.dot(dispatch, grad_top, precision=PRECISE)
    grad_slot_gate = jnp.sum(expert_flat * routed_grad, axis=1)
    grad_pair = jnp.dot(pair_place, grad_slot_gate, precision=PRECISE)
    grad_probs = jnp.dot(token_hot.T, expert_raw * grad_pair[:, None], precision=PRECISE)
    grad_logits = router_probs * (
        grad_probs - jnp.sum(router_probs * grad_probs, axis=-1, keepdims=True)
    )
    grad_logits_b = grad_logits.astype(jnp.bfloat16)
    grad_router = jnp.einsum(
        "td,te->de", mixed_b, grad_logits_b, preferred_element_type=jnp.float32
    )
    grad_mixed = jnp.einsum(
        "te,de->td", grad_logits_b, router_full, preferred_element_type=jnp.float32
    )
    again_in, again_out, again_sin, again_sout = (
        lax.all_gather(expert_in, "fsdp", axis=0, tiled=True),
        lax.all_gather(expert_out, "fsdp", axis=0, tiled=True),
        lax.all_gather(shared_in, "fsdp", axis=0, tiled=True),
        lax.all_gather(shared_out, "fsdp", axis=0, tiled=True),
    )
    part_in = lax.all_gather(again_in, "ctx", axis=0, tiled=True)
    part_out = lax.all_gather(again_out, "ctx", axis=0, tiled=True)
    part_sin = lax.all_gather(again_sin, "ctx", axis=0, tiled=True)
    part_sout = lax.all_gather(again_sout, "ctx", axis=0, tiled=True)
    gate_e, up_e = expert_pre(part_in)
    sig_e = jax.nn.sigmoid(gate_e)
    hidden_e = (gate_e * sig_e * up_e).astype(jnp.bfloat16)
    grad_hid = jnp.einsum("ecd,fed->ecf", grad_ye_b, part_out, preferred_element_type=jnp.float32)
    grad_gate = (grad_hid * up_e * sig_e * (1.0 + gate_e * (1.0 - sig_e))).astype(jnp.bfloat16)
    grad_up = (grad_hid * gate_e * sig_e).astype(jnp.bfloat16)
    grad_slots = jnp.einsum(
        "ecf,fed->ecd", grad_gate, part_in[:, :, 0, :], preferred_element_type=jnp.float32
    ) + jnp.einsum("ecf,fed->ecd", grad_up, part_in[:, :, 1, :], preferred_element_type=jnp.float32)
    mlp_pre_buffer = jnp.stack([grad_gate, grad_up], axis=2)
    gate_s, up_s = shared_pre(part_sin)
    sig_s = jax.nn.sigmoid(gate_s)
    hidden_s = (gate_s * sig_s * up_s).astype(jnp.bfloat16)
    grad_hs = jnp.einsum("td,fd->tf", grad_sh_b, part_sout, preferred_element_type=jnp.float32)
    grad_gs = (grad_hs * up_s * sig_s * (1.0 + gate_s * (1.0 - sig_s))).astype(jnp.bfloat16)
    grad_us = (grad_hs * gate_s * sig_s).astype(jnp.bfloat16)
    grad_shared_x = jnp.einsum(
        "tf,fd->td", grad_gs, part_sin[:, 0, :], preferred_element_type=jnp.float32
    ) + jnp.einsum("tf,fd->td", grad_us, part_sin[:, 1, :], preferred_element_type=jnp.float32)
    mlp_spre_buffer = jnp.stack([grad_gs, grad_us], axis=1)
    grad_slots, grad_shared_x, pre_buffer, hid_buffer, spre_buffer, shid_buffer = (
        grad_slots,
        grad_shared_x,
        mlp_pre_buffer,
        hidden_e,
        mlp_spre_buffer,
        hidden_s,
    )
    term_in = jnp.einsum(
        "ecgf,ecd->fegd", pre_buffer, slot_in, preferred_element_type=jnp.float32
    ).reshape(lax.axis_size(("ctx", "fsdp")) * hidden_count, -1)
    term_out = jnp.einsum(
        "ecf,ecd->fed", hid_buffer, grad_ye_b, preferred_element_type=jnp.float32
    ).reshape(lax.axis_size(("ctx", "fsdp")) * hidden_count, -1)
    term_sin = jnp.einsum(
        "tgf,td->fgd", spre_buffer, mixed_b, preferred_element_type=jnp.float32
    ).reshape(lax.axis_size(("ctx", "fsdp")) * hidden_count, -1)
    term_sout = jnp.einsum("tf,td->fd", shid_buffer, grad_sh_b, preferred_element_type=jnp.float32)
    mlp_sums = lax.psum_scatter(
        jnp.concatenate([term_in, term_out, term_sin, term_sout], axis=1),
        ("ctx", "fsdp"),
        scatter_dimension=0,
        tiled=True,
    )
    in_width = expert_count * 2 * model_dim
    out_width = expert_count * model_dim
    grad_expert_in = mlp_sums[:, :in_width].reshape(hidden_count, expert_count, 2, model_dim)
    grad_expert_out = mlp_sums[:, in_width : in_width + out_width].reshape(
        hidden_count, expert_count, model_dim
    )
    grad_shared_in = mlp_sums[
        :, in_width + out_width : in_width + out_width + 2 * model_dim
    ].reshape(hidden_count, 2, model_dim)
    grad_shared_out = mlp_sums[:, in_width + out_width + 2 * model_dim :]
    grad_mixed = (
        grad_mixed
        + jnp.dot(dispatch.T, grad_slots.reshape(slot_rows, model_dim), precision=PRECISE)
        + grad_shared_x
    )
    grad_resid_n, grad_gain_m = rms_backward(resid, inv_mlp, gain_m.astype(jnp.float32), grad_mixed)
    grad_resid = grad_top + grad_resid_n
    grad_attn_b = grad_resid.astype(jnp.bfloat16)
    grad_w_out = jnp.einsum("ti,to->io", attn_b, grad_attn_b, preferred_element_type=jnp.float32)
    grad_o = jnp.einsum("to,io->ti", grad_attn_b, weight_out, preferred_element_type=jnp.float32)
    grad_o_b = grad_o.reshape(head_shape).astype(jnp.bfloat16)
    delta_rows = jnp.sum(grad_o_b.astype(jnp.float32) * attn_heads, axis=-1)
    delta_heads = delta_rows.T
    log_rows = log_heads.T
    query_keys_part = lax.all_gather(key_b, "ctx", axis=0, tiled=True)
    query_values_part = lax.all_gather(value_b, "ctx", axis=0, tiled=True)
    query_width = math.gcd(query_keys_part.shape[0], 512)

    def query_key_step(number, grad_query):
        begin_at = number * query_width
        key_blk = lax.dynamic_slice_in_dim(query_keys_part, begin_at, query_width, 0)
        value_blk = lax.dynamic_slice_in_dim(query_values_part, begin_at, query_width, 0)
        allowed = allowed_mask(row_index, begin_at + jnp.arange(query_width, dtype=jnp.int32))
        scores = (
            jnp.einsum("qhd,khd->hqk", query_b, key_blk, preferred_element_type=jnp.float32)
            * score_scale
        )
        probs = jnp.where(allowed, jnp.exp(scores - log_heads[:, :, None]), 0.0)
        grad_p = jnp.einsum("qhd,khd->hqk", grad_o_b, value_blk, preferred_element_type=jnp.float32)
        grad_scores = (probs * (grad_p - delta_heads[:, :, None])).astype(jnp.bfloat16)
        return (
            grad_query
            + jnp.einsum("hqk,khd->qhd", grad_scores, key_blk, preferred_element_type=jnp.float32)
            * score_scale
        )

    grad_query = lax.fori_loop(
        0,
        query_keys_part.shape[0] // query_width,
        query_key_step,
        jnp.zeros(head_shape, jnp.float32),
    )
    kv_start = (jnp.zeros(head_shape, jnp.float32), jnp.zeros(head_shape, jnp.float32))
    query_part = lax.all_gather(query_b, "ctx", axis=0, tiled=True)
    grad_o_part = lax.all_gather(grad_o_b, "ctx", axis=0, tiled=True)
    log_part = lax.all_gather(log_rows.astype(jnp.bfloat16), "ctx", axis=0, tiled=True).astype(
        jnp.float32
    )
    delta_part = lax.all_gather(delta_rows.astype(jnp.bfloat16), "ctx", axis=0, tiled=True).astype(
        jnp.float32
    )
    key_width = math.gcd(query_part.shape[0], 512)

    def query_step(number, grad_state):
        grad_keys, grad_values = grad_state
        begin_at = number * key_width
        query_blk = lax.dynamic_slice_in_dim(query_part, begin_at, key_width, 0)
        grad_o_blk = lax.dynamic_slice_in_dim(grad_o_part, begin_at, key_width, 0)
        log_blk = lax.dynamic_slice_in_dim(log_part, begin_at, key_width, 0)
        delta_blk = lax.dynamic_slice_in_dim(delta_part, begin_at, key_width, 0)
        allowed = allowed_mask(begin_at + jnp.arange(key_width, dtype=jnp.int32), row_index)
        scores = (
            jnp.einsum("qhd,khd->hqk", query_blk, key_b, preferred_element_type=jnp.float32)
            * score_scale
        )
        probs = jnp.where(allowed, jnp.exp(scores - log_blk.T[:, :, None]), 0.0)
        grad_values = grad_values + jnp.einsum(
            "hqk,qhd->khd",
            probs.astype(jnp.bfloat16),
            grad_o_blk,
            preferred_element_type=jnp.float32,
        )
        grad_p = jnp.einsum("qhd,khd->hqk", grad_o_blk, value_b, preferred_element_type=jnp.float32)
        grad_scores = (probs * (grad_p - delta_blk.T[:, :, None])).astype(jnp.bfloat16)
        grad_keys = (
            grad_keys
            + jnp.einsum("hqk,qhd->khd", grad_scores, query_blk, preferred_element_type=jnp.float32)
            * score_scale
        )
        return (grad_keys, grad_values)

    grad_keys, grad_values = lax.fori_loop(
        0, query_part.shape[0] // key_width, query_step, kv_start
    )
    grad_q_raw = rotate(grad_query, cosine, -sine_tab).reshape(tok_count, model_dim)
    grad_k_raw = rotate(grad_keys, cosine, -sine_tab).reshape(tok_count, model_dim)
    grad_proj_b = jnp.concatenate(
        [grad_q_raw, grad_k_raw, grad_values.reshape(tok_count, model_dim)], axis=1
    ).astype(jnp.bfloat16)
    grad_w_qkv = jnp.einsum("ti,to->io", normed_b, grad_proj_b, preferred_element_type=jnp.float32)
    grad_normed = jnp.einsum(
        "to,io->ti", grad_proj_b, weight_qkv, preferred_element_type=jnp.float32
    )
    grad_in_n, grad_gain_a = rms_backward(inputs, inv_attn, gain_a.astype(jnp.float32), grad_normed)
    grad_inputs = (grad_resid + grad_in_n)[None]
    summed = (
        lax.psum_scatter(grad_gain_a, ("ctx", "fsdp"), scatter_dimension=0, tiled=True),
        lax.psum_scatter(grad_w_qkv, ("ctx", "fsdp"), scatter_dimension=0, tiled=True),
        lax.psum_scatter(grad_w_out, ("ctx", "fsdp"), scatter_dimension=0, tiled=True),
        lax.psum_scatter(grad_gain_m, ("ctx", "fsdp"), scatter_dimension=0, tiled=True),
        lax.psum_scatter(grad_router, ("ctx", "fsdp"), scatter_dimension=0, tiled=True),
    )
    return (
        layer_out,
        grad_inputs,
        summed[0],
        summed[1],
        summed[2],
        summed[3],
        summed[4],
        grad_expert_in,
        grad_expert_out,
        grad_shared_in,
        grad_shared_out,
    )


def solution(mesh):
    placed = (
        P("fsdp", "ctx", None),
        P("fsdp", None),
        P("fsdp", "ctx", None),
        P("fsdp", "ctx", None),
        P(("ctx", "fsdp")),
        P(("ctx", "fsdp"), None),
        P(("ctx", "fsdp"), None),
        P(("ctx", "fsdp")),
        P(("ctx", "fsdp"), None),
        P(("ctx", "fsdp"), None, None, None),
        P(("ctx", "fsdp"), None, None),
        P(("ctx", "fsdp"), None, None),
        P(("ctx", "fsdp"), None),
    )
    return jax.shard_map(
        body,
        mesh=mesh,
        in_specs=placed,
        out_specs=(
            P("fsdp", "ctx", None),
            P("fsdp", "ctx", None),
            P(("ctx", "fsdp")),
            P(("ctx", "fsdp"), None),
            P(("ctx", "fsdp"), None),
            P(("ctx", "fsdp")),
            P(("ctx", "fsdp"), None),
            P(("ctx", "fsdp"), None, None, None),
            P(("ctx", "fsdp"), None, None),
            P(("ctx", "fsdp"), None, None),
            P(("ctx", "fsdp"), None),
        ),
        check_vma=False,
    )
```

profile of v0, /device:TPU:0, one launch (start us, length us, event | category | flops | bytes accessed | tf_op | source)
XLA Modules:
  0.0 2332.3 jit_solution(9675972499210958833)
XLA Ops:
  12.6 42.1 %all-reduce.6 = (bf16[768]{0:T(1024)(128)(2,1)S(1)}, bf16[768]{0:T(1024)(128)(2,1)S(1)}) all-reduce(bf16[768]{0:T(1024)(128)(2,1)S(1)} %dynamic-update-slice, bf16[768]{0:T(1024)(128)(2,1)S(1)} %dynamic-update-slice.1), channel_id=1, replica_groups=mesh['ctx'=8,'fsdp'=4] {'ctx','fsdp'}, use_global_device_ids=true, to_apply=%add | all-reduce | flops 1536 | bytes 6144
  55.4 18.6 all-gather.14.cloned.1.call-done
  80.6 13.1 all_gather.83
  93.8 9.6 all_gather.85
  108.9 20.6 all-gather.26.cloned.1.call-done
  131.2 40.6 %all-gather = bf16[32,24,4]{1,2,0:T(4,128)(2,1)S(1)} all-gather(bf16[1,24,4]{1,2,0:T(4,128)(2,1)S(1)} %bitcast.302), channel_id=1, replica_groups=mesh['ctx'=8,'fsdp'=4] {'ctx','fsdp'}, dimensions={0}, use_global_device_ids=true | all-gather | bytes 6336 | tf_op jit(solution)/shard_map/all_gather | solution.py:117
  177.4 46.0 %all-gather.16.cloned.1.call-done = bf16[1024,12,64]{0,2,1:T(8,128)(2,1)} async-done(((bf16[128,12,64]{0,2,1:T(8,128)(2,1)}), bf16[1024,12,64]{0,2,1:T(8,128)(2,1)}) %all-gather.16.cloned.1.call-update) | async-done | bytes 1572880 | tf_op jit(solution)/shard_map/all_gather | solution.py:141
  223.4 8.8 while.48
  232.4 46.1 %all-gather.20.cloned.1.call-done = bf16[768,768]{1,0:T(8,128)(2,1)} async-done(((bf16[24,768]{1,0:T(8,128)(2,1)}), bf16[768,768]{1,0:T(8,128)(2,1)}) %all-gather.20.cloned.1.call-update) | async-done | bytes 1179664 | tf_op jit(solution)/shard_map/all_gather | solution.py:115
  284.1 94.6 %all-gather.30.cloned.1.call-done = bf16[2048,2,768]{2,0,1:T(8,128)(2,1)} async-done(((bf16[256,2,768]{2,0,1:T(8,128)(2,1)}), bf16[2048,2,768]{2,0,1:T(8,128)(2,1)}) %all-gather.30.cloned.1.call-update) | async-done | bytes 6291472 | tf_op jit(solution)/shard_map/all_gather | solution.py:216
  384.7 54.8 %all-gather.32.cloned.1.call-done = bf16[2048,768]{1,0:T(8,128)(2,1)} async-done(((bf16[256,768]{1,0:T(8,128)(2,1)}), bf16[2048,768]{1,0:T(8,128)(2,1)}) %all-gather.32.cloned.1.call-update) | async-done | bytes 3145744 | tf_op jit(solution)/shard_map/all_gather | solution.py:217
  446.5 6.3 fusion.93
  452.8 12.7 copy.99
  471.3 448.9 %all-gather.24.cloned.1.call-done = bf16[2048,4,2,768]{3,0,1,2:T(8,128)(2,1)} async-done(((bf16[256,4,2,768]{3,0,1,2:T(8,128)(2,1)}), bf16[2048,4,2,768]{3,0,1,2:T(8,128)(2,1)}) %all-gather.24.cloned.1.call-update) | async-done | bytes 25165840 | tf_op jit(solution)/shard_map/all_gather | solution.py:214
  920.2 7.0 fusion.77
  927.2 11.0 fusion.75
  938.2 160.4 %all-gather.28.cloned.1.call-done = bf16[2048,4,768]{2,0,1:T(8,128)(2,1)} async-done(((bf16[256,4,768]{2,0,1:T(8,128)(2,1)}), bf16[2048,4,768]{2,0,1:T(8,128)(2,1)}) %all-gather.28.cloned.1.call-update) | async-done | bytes 12582928 | tf_op jit(solution)/shard_map/all_gather | solution.py:215
  1098.7 11.0 multiply_convert_fusion.1
  1109.6 7.2 fusion.172
  1134.9 10.4 fusion.174
  1145.3 24.8 %copy.98 = f32[2048,3072]{1,0:T(8,128)} copy(f32[2048,3072]{0,1:T(8,128)} %bitcast.266) | data formatting | bytes 50331648 | tf_op jit(solution)/shard_map/reshape | solution.py:298
  1170.1 20.4 fusion.82
  1190.5 49.0 %copy.97 = f32[2048,6144]{1,0:T(8,128)} copy(f32[2048,6144]{0,1:T(8,128)} %bitcast.265) | data formatting | bytes 100663296 | tf_op jit(solution)/shard_map/reshape | solution.py:295
  1239.6 77.1 %pad_maximum_fusion = f32[2048,11520]{1,0:T(8,128)} fusion(f32[2048,768]{1,0:T(8,128)} %fusion.136, f32[2048,1536]{1,0:T(8,128)} %copy.99, f32[2048,3072]{1,0:T(8,128)} %copy.98, f32[2048,6144]{1,0:T(8,128)} %copy.97), kind=kLoop, calls=%fused_computation.84 | loop fusion | flops 70778880 | bytes 188743680 | tf_op jit(solution)/shard_map/concatenate | solution.py:304
  1318.0 26.0 %all_gather.88 = bf16[1024,12]{0,1:T(8,128)(2,1)S(1)} all-gather(bf16[128,12]{0,1:T(8,128)(2,1)S(1)} %get-tuple-element.746), channel_id=1, replica_groups=mesh['ctx'=8,'fsdp'=4] {'ctx'}, dimensions={0}, use_global_device_ids=true | all-gather | bytes 27648 | tf_op jit(solution)/shard_map/all_gather | solution.py:364
  1345.6 26.0 %all_gather.90 = bf16[1024,12]{0,1:T(8,128)(2,1)S(1)} all-gather(bf16[128,12]{0,1:T(8,128)(2,1)S(1)} %convert_element_type.236), channel_id=1, replica_groups=mesh['ctx'=8,'fsdp'=4] {'ctx'}, dimensions={0}, use_global_device_ids=true | all-gather | bytes 27648 | tf_op jit(solution)/shard_map/all_gather | solution.py:367
  1374.2 14.1 while.49
  1388.4 25.5 %while.50 = (s32[]{:T(128)}, f32[128,12,64]{0,2,1:T(8,128)}, f32[128,12,64]{0,2,1:T(8,128)}, bf16[1024,12,64]{0,2,1:T(8,128)(2,1)}, s32[4]{0:T(128)S(1)}, /*inde...) while((s32[]{:T(128)}, f32[128,12,64]{0,2,1:T(8,128)}, ...), condition=%wide.region_28.29_spmd.clone, body=%wide.region_25.28_spmd.clone.sunk | while | flops 411213312 | bytes 14956801 | solution.py:400
  1429.6 39.5 %all-reduce.5 = (f32[768]{0:T(1024)S(1)}, f32[768]{0:T(1024)S(1)}, f32[768,4]{0,1:T(4,128)S(1)}) all-reduce(f32[768]{0:T(1024)S(1)} %get-tuple-element.677, f32[768]{0:T(1024)S(1)} %copy-done.50, f32[768,4]{0,1:T(4,128)S(1)} %fusion.170), channel_id=2, replica_groups=mesh['ctx'=8,'fsdp'=4] {'ctx','fsdp'}, use_global_device_ids=true, to_apply=%region_31.32.clone | all-reduce | flops 4608 | bytes 36864
  1471.8 624.6 %reduce-scatter.9.cloned.1.call-done = f32[64,11520]{1,0:T(8,128)} async-done(((f32[2048,11520]{1,0:T(8,128)}), f32[64,11520]{1,0:T(8,128)}) %reduce-scatter.9.cloned.1.call-update) | async-done | bytes 2949136 | tf_op jit(solution)/shard_map/reduce_scatter | solution.py:303
  2103.9 97.2 %reduce-scatter.7.cloned.1.call-done = f32[24,768]{1,0:T(8,128)} async-done(((f32[768,768]{1,0:T(8,128)}), f32[24,768]{1,0:T(8,128)}) %reduce-scatter.7.cloned.1.call-update) | async-done | bytes 73744 | tf_op jit(solution)/shard_map/reduce_scatter | solution.py:417
  2201.1 124.3 %reduce-scatter.5.cloned.1.call-done = f32[24,2304]{1,0:T(8,128)} async-done(((f32[768,2304]{1,0:T(8,128)}), f32[24,2304]{1,0:T(8,128)}) %reduce-scatter.5.cloned.1.call-update) | async-done | bytes 221200 | tf_op jit(solution)/shard_map/reduce_scatter | solution.py:416
  (341 shorter events, 146.5 us)
Async XLA Ops:
  7.2 47.5 %copy-start.10 = (bf16[1,128,768]{2,1,0:T(8,128)(2,1)S(1)}, bf16[1,128,768]{2,1,0:T(8,128)(2,1)}, u32[]{:S(2)}) copy-start(bf16[1,128,768]{2,1,0:T(8,128)(2,1)} %param.19) | copy-start | bytes 589828
  7.2 66.7 %all-gather.14.cloned.1.call-start = ((), (), s32[]{:S(2)}) async-start(), calls=%async_computation.3 | async-start | bytes 3649536 | tf_op jit(solution)/shard_map/all_gather | solution.py:114
  7.9 100.9 %all-gather.22.cloned.1.call-start = ((), (), s32[]{:S(2)}) async-start(), calls=%async_computation.7 | async-start | bytes 3932160 | tf_op jit(solution)/shard_map/all_gather | solution.py:209
  10.2 119.4 %all-gather.26.cloned.1.call-start = ((), (), s32[]{:S(2)}) async-start(), calls=%async_computation.9 | async-start | bytes 1966080 | tf_op jit(solution)/shard_map/all_gather | solution.py:210
  12.0 65.5 %copy-start.69 = (s32[1,4]{1,0:T(1,128)S(1)}, s32[1,4]{1,0:T(1,128)}, u32[]{:S(2)}) copy-start(s32[1,4]{1,0:T(1,128)} %param.20) | copy-start | bytes 52
  12.0 165.4 %all-gather.18.cloned.1.call-start = ((), (), s32[]{:S(2)}) async-start(), calls=%async_computation.5 | async-start | bytes 1769472 | tf_op jit(solution)/shard_map/all_gather | solution.py:142
  77.5 145.9 %all-gather.16.cloned.1.call-start = ((), (), s32[]{:S(2)}) async-start(), calls=%async_computation.4 | async-start | bytes 1769472 | tf_op jit(solution)/shard_map/all_gather | solution.py:141
  79.9 198.6 %all-gather.20.cloned.1.call-start = ((), (), s32[]{:S(2)}) async-start(), calls=%async_computation.6 | async-start | bytes 1216512 | tf_op jit(solution)/shard_map/all_gather | solution.py:115
  80.5 298.2 %all-gather.30.cloned.1.call-start = ((), (), s32[]{:S(2)}) async-start(), calls=%async_computation.11 | async-start | bytes 7077888 | tf_op jit(solution)/shard_map/all_gather | solution.py:216
  93.7 345.8 %all-gather.32.cloned.1.call-start = ((), (), s32[]{:S(2)}) async-start(), calls=%async_computation.12 | async-start | bytes 3538944 | tf_op jit(solution)/shard_map/all_gather | solution.py:217
  103.4 816.7 %all-gather.24.cloned.1.call-start = ((), (), s32[]{:S(2)}) async-start(), calls=%async_computation.8 | async-start | bytes 28311552 | tf_op jit(solution)/shard_map/all_gather | solution.py:214
  108.9 989.8 %all-gather.28.cloned.1.call-start = ((), (), s32[]{:S(2)}) async-start(), calls=%async_computation.10 | async-start | bytes 14155776 | tf_op jit(solution)/shard_map/all_gather | solution.py:215
  129.5 1258.8 %all-gather.34.cloned.1.call-start = ((), (), s32[]{:S(2)}) async-start(), calls=%async_computation.13 | async-start | bytes 1769472 | tf_op jit(solution)/shard_map/all_gather | solution.py:362
  129.6 1003.7 %copy-start.51 = (f32[128]{0:T(128)}, f32[128]{0:T(128)S(1)}, u32[]{:S(2)}) copy-start(f32[128]{0:T(128)S(1)} %get-tuple-element.779) | copy-start | bytes 1540
  172.0 108.9 %copy-start.70 = (s32[256]{0:T(256)}, s32[256]{0:T(256)S(1)}, u32[]{:S(2)}) copy-start(s32[256]{0:T(256)S(1)} %iota_bitcast_fusion) | copy-start | bytes 3076
  172.5 109.1 %copy-start.25 = (f32[320,128]{1,0:T(8,128)}, f32[320,128]{1,0:T(8,128)S(1)}, u32[]{:S(2)}) copy-start(f32[320,128]{1,0:T(8,128)S(1)} %fusion.112) | copy-start | bytes 491524
  173.2 1215.1 %all-gather.36.cloned.1.call-start = ((), (), s32[]{:S(2)}) async-start(), calls=%async_computation.14 | async-start | bytes 1769472 | tf_op jit(solution)/shard_map/all_gather | solution.py:363
  232.3 146.4 %copy-start.45 = (s32[4]{0:T(128)}, s32[4]{0:T(128)S(1)}, u32[]{:S(2)}) copy-start(s32[4]{0:T(128)S(1)} %get-tuple-element.1162) | copy-start | bytes 52
  232.3 49.9 %copy-start.18 = (bf16[1,128,768]{2,1,0:T(8,128)(2,1)S(1)}, bf16[1,128,768]{2,1,0:T(8,128)(2,1)}, u32[]{:S(2)}) copy-start(bf16[1,128,768]{2,1,0:T(8,128)(2,1)} %param.22) | copy-start | bytes 589828
  232.4 47.9 %copy-start.21 = (bf16[128,12,64]{0,2,1:T(8,128)(2,1)}, bf16[128,12,64]{0,2,1:T(8,128)(2,1)S(1)}, u32[]{:S(2)}) copy-start(bf16[128,12,64]{0,2,1:T(8,128)(2,1)S(1)} %fusion.129) | copy-start | bytes 589828
  280.2 853.1 %copy-start.1 = (f32[128,768]{1,0:T(8,128)}, f32[128,768]{1,0:T(8,128)S(1)}, u32[]{:S(2)}) copy-start(f32[128,768]{1,0:T(8,128)S(1)} %get-tuple-element.782) | copy-start | bytes 1179652
  280.4 166.1 %copy-start.4 = (bf16[128,768]{1,0:T(8,128)(2,1)}, bf16[128,768]{1,0:T(8,128)(2,1)S(1)}, u32[]{:S(2)}) copy-start(bf16[128,768]{1,0:T(8,128)(2,1)S(1)} %multiply_convert_fusion.7) | copy-start | bytes 589828
  280.5 839.1 %copy-start.48 = (f32[128,4]{0,1:T(4,128)}, f32[128,4]{0,1:T(4,128)S(1)}, u32[]{:S(2)}) copy-start(f32[128,4]{0,1:T(4,128)S(1)} %get-tuple-element.784) | copy-start | bytes 6148
  280.6 839.1 %copy-start.54 = (f32[128]{0:T(128)}, f32[128]{0:T(128)S(1)}, u32[]{:S(2)}) copy-start(f32[128]{0:T(128)S(1)} %get-tuple-element.783) | copy-start | bytes 1540
  280.6 839.0 %copy-start.60 = (f32[128]{0:T(128)}, f32[128]{0:T(128)S(1)}, u32[]{:S(2)}) copy-start(f32[128]{0:T(128)S(1)} %fusion.159) | copy-start | bytes 1540
  1133.5 238.8 %copy-start.8 = (f32[128,768]{1,0:T(8,128)}, f32[128,768]{1,0:T(8,128)S(1)}, u32[]{:S(2)}) copy-start(f32[128,768]{1,0:T(8,128)S(1)} %fusion.107) | copy-start | bytes 1179652
  1239.5 856.9 %reduce-scatter.9.cloned.1.call-start = ((), (), s32[]{:S(2)}) async-start(), calls=%async_computation.17 | async-start | bytes 97320960 | tf_op jit(solution)/shard_map/reduce_scatter | solution.py:303
  1316.7 55.6 %copy-start.22 = (bf16[128,12,64]{0,2,1:T(8,128)(2,1)S(1)}, bf16[128,12,64]{0,2,1:T(8,128)(2,1)}, u32[]{:S(2)}) copy-start(bf16[128,12,64]{0,2,1:T(8,128)(2,1)} %copy-done.21) | copy-start | bytes 589828
  1316.7 57.5 %copy-start = (bf16[128,12,64]{0,2,1:T(8,128)(2,1)S(1)}, bf16[128,12,64]{0,2,1:T(8,128)(2,1)}, u32[]{:S(2)}) copy-start(bf16[128,12,64]{0,2,1:T(8,128)(2,1)} %get-tuple-element.1134) | copy-start | bytes 589828
  1316.7 57.5 %copy-start.46 = (s32[4]{0:T(128)S(1)}, s32[4]{0:T(128)}, u32[]{:S(2)}) copy-start(s32[4]{0:T(128)} %copy-done.45) | copy-start | bytes 52
  1316.7 884.4 %reduce-scatter.7.cloned.1.call-start = ((), (), s32[]{:S(2)}) async-start(), calls=%async_computation.16 | async-start | bytes 2433024 | tf_op jit(solution)/shard_map/reduce_scatter | solution.py:417
  1388.3 937.1 %reduce-scatter.5.cloned.1.call-start = ((), (), s32[]{:S(2)}) async-start(), calls=%async_computation.15 | async-start | bytes 7299072 | tf_op jit(solution)/shard_map/reduce_scatter | solution.py:416
  (58 other events, 708.5 us)
Sparse Core Ops, SparseCore 0:
  11.0 62.9 all-gather.13
  76.1 32.7 all-gather.21
  111.0 18.4 all-gather.25
  132.0 45.3 all-gather.17
  179.9 43.4 all-gather.15
  226.2 52.2 all-gather.19
  280.7 97.9 all-gather.29
  380.9 58.6 all-gather.31
  441.1 479.0 all-gather.23
  922.2 176.3 all-gather.27
  1101.3 43.4 all-gather.33
  1239.6 43.5 all-gather.35
  1316.8 779.5 reduce-scatter.8
  2103.0 98.0 reduce-scatter.6
  2207.2 118.1 reduce-scatter.4
where the time goes:
time: 2340 us; the launch traced here: 2330 us
  waiting for transfers between devices  1750 us (75%)
  blocking collectives  197 us (8%)
  matrix products  168 us (7%)
  local copies, waits for them, and re-layouts  109 us (5%)
  other arithmetic  95.1 us (4%)
    reduce_scatter x1, waiting for transfers between devices, body(): lax.psum_scatter(jnp.concatenate([term_in, term_out, term_sin, term_sout]...  625 us
    all_gather x1, waiting for transfers between devices, body(): part_in = lax.all_gather(group_in, 'ctx', axis=0, tiled=True)  449 us
    all_gather x1, waiting for transfers between devices, body(): part_out = lax.all_gather(group_out, 'ctx', axis=0, tiled=True)  160 us
    reduce_scatter x1, waiting for transfers between devices, body(): lax.psum_scatter(grad_w_qkv, ('ctx', 'fsdp'), scatter_dimension=0, tiled=...  124 us
    reduce_scatter x1, waiting for transfers between devices, body(): lax.psum_scatter(grad_w_out, ('ctx', 'fsdp'), scatter_dimension=0, tiled=...  97.2 us
    all_gather x1, waiting for transfers between devices, body(): part_sin = lax.all_gather(group_sin, 'ctx', axis=0, tiled=True)  94.6 us
    unnamed x2, blocking collectives  81.6 us
    concatenate x1, other arithmetic, body(): jnp.concatenate([term_in, term_out, term_sin, term_sout], axis=1)  77.1 us
  transfers between devices with their start and end apart: 15, of which 13 were waited for; matrix products, arithmetic and copies ran while one was open for 16% of the time, Pallas kernels for 0%

commit v1 on v0

v1 whole, which is shorter than its diff:
```python
import functools
import math

import jax
import jax.numpy as jnp
from jax import lax
from jax.experimental import pallas as pl
from jax.experimental.pallas import tpu as pltpu
from jax.sharding import PartitionSpec as P

HEAD_DIM = 64
EPSILON = 1e-05
ROPE_BASE = 10000.0
MASKED = -1e30
GROUPS = 4
MESH = pl.DeviceIdType.MESH
DMA = pltpu.SemaphoreType.DMA
BF = jnp.bfloat16
F32 = jnp.float32


class Place:
    def __init__(self, columns):
        ctx, fsdp = lax.axis_index("ctx"), lax.axis_index("fsdp")
        self.columns = columns
        self.a, self.b = ctx // 2, ctx % 2
        self.y, self.c = fsdp // 2, fsdp % 2
        flip_b = (1 - self.b, self.y)
        flip_y = (self.b, 1 - self.y)
        core = self.c == 0
        self.first = tuple(jnp.where(core, p, q) for p, q in zip(flip_b, flip_y))
        self.second = tuple(jnp.where(core, q, p) for p, q in zip(flip_b, flip_y))
        self.plane = [(self.b, self.y), self.first, self.second, (1 - self.b, 1 - self.y)]
        self.sib_plane = [(self.b, self.y), self.second, self.first, (1 - self.b, 1 - self.y)]

    def at(self, step):
        return lax.rem(self.a + step, self.columns)

    def device(self, a=None, plane=None, c=None):
        b, y = plane if plane is not None else (self.b, self.y)
        a = self.a if a is None else a
        c = self.c if c is None else c
        return {"ctx": a * 2 + b, "fsdp": y * 2 + c}

    def column(self, step):
        return self.device(a=self.at(step))

    def flip_b(self):
        return self.device(plane=(1 - self.b, self.y))

    def flip_y(self):
        return self.device(plane=(self.b, 1 - self.y))

    def sibling(self):
        return self.device(c=1 - self.c)

    def chunk(self, step, plane, c):
        return (self.at(step) * 2 + plane[0]) * 4 + plane[1] * 2 + c


def greet(devices):
    barrier = pltpu.get_barrier_semaphore()
    for device in devices:
        pl.semaphore_signal(barrier, inc=1, device_id=device, device_id_type=MESH)
    pl.semaphore_wait(barrier, len(devices))


def remote(src, dst, send, recv, device):
    return pltpu.make_async_remote_copy(
        src_ref=src, dst_ref=dst, send_sem=send, recv_sem=recv, device_id=device, device_id_type=MESH
    )


class Sends:
    def __init__(self, sems):
        self.sems, self.made = sems, []

    def start(self, src, dst, recv, device):
        copy = remote(src, dst, self.sems.at[len(self.made)], recv, device)
        copy.start()
        self.made.append(copy)

    def finish(self):
        for copy in self.made:
            copy.wait_send()


def arrived(dst, recv, device):
    remote(dst, dst, recv, recv, device).wait_recv()


def gather_ctx(pos, src, out, sends, recv, local):
    n = pos.columns
    me = pos.a * 2 + pos.b
    own = pltpu.make_async_copy(src, out.at[me], local)
    own.start()
    for k in range(1, n):
        sends.start(src, out.at[me], recv.at[k], pos.column(k))
    sends.start(src, out.at[me], recv.at[n], pos.flip_b())
    yield
    for k in range(1, n):
        slot = pos.at(n - k) * 2 + pos.b
        arrived(out.at[slot], recv.at[k], pos.column(k))
        sends.start(out.at[slot], out.at[slot], recv.at[n + k], pos.flip_b())
        yield
    for k in range(n):
        slot = pos.at(n - k) * 2 + 1 - pos.b
        arrived(out.at[slot], recv.at[n + k], pos.flip_b())
        yield
    own.wait()


def gather_ctx_sems(n):
    return [DMA((2 * n,)), DMA((2 * n,)), DMA]


def gather_fsdp(pos, src, out, sends, recv, local):
    parts = src.shape[0]
    me = pos.y * 2 + pos.c
    other = (1 - pos.y) * 2 + pos.c
    own = []
    for p in range(parts):
        own.append(pltpu.make_async_copy(src.at[p], out.at[p, me], local.at[p]))
        own[-1].start()
        sends.start(src.at[p], out.at[p, me], recv.at[p], pos.flip_y())
    for p in range(parts):
        sends.start(src.at[p], out.at[p, me], recv.at[parts + p], pos.sibling())
    yield
    for p in range(parts):
        arrived(out.at[p, other], recv.at[p], pos.flip_y())
        sends.start(out.at[p, other], out.at[p, other], recv.at[2 * parts + p], pos.sibling())
        yield
    for p in range(parts):
        arrived(out.at[p, pos.y * 2 + 1 - pos.c], recv.at[parts + p], pos.sibling())
        arrived(out.at[p, (1 - pos.y) * 2 + 1 - pos.c], recv.at[2 * parts + p], pos.sibling())
        own[p].wait()


def gather_fsdp_sems(parts):
    return [DMA((3 * parts,)), DMA((3 * parts,)), DMA((parts,))]


def gather_all(pos, src, out, sends, recv, local, group_of=None):
    n = pos.columns
    me = pos.chunk(0, pos.plane[0], pos.c)
    part = (lambda a: src) if group_of is None else (lambda a: src.at[group_of(a)])
    mine = part(pos.a)
    own = pltpu.make_async_copy(mine, out.at[me], local)
    own.start()
    first, second = pos.device(plane=pos.first), pos.device(plane=pos.second)
    sibling = pos.sibling()
    for k in range(1, n):
        sends.start(part(pos.at(k)), out.at[me], recv.at[k], pos.column(k))
    sends.start(mine, out.at[me], recv.at[n], first)
    sends.start(mine, out.at[me], recv.at[2 * n], second)
    sends.start(mine, out.at[me], recv.at[4 * n], sibling)
    yield
    for k in range(1, n):
        slot = pos.chunk(n - k, pos.plane[0], pos.c)
        arrived(out.at[slot], recv.at[k], first)
        sends.start(out.at[slot], out.at[slot], recv.at[n + k], first)
        sends.start(out.at[slot], out.at[slot], recv.at[2 * n + k], second)
        sends.start(out.at[slot], out.at[slot], recv.at[4 * n + k], sibling)
        yield
    for k in range(n):
        slot = pos.chunk(n - k, pos.first, pos.c)
        arrived(out.at[slot], recv.at[n + k], first)
        sends.start(out.at[slot], out.at[slot], recv.at[3 * n + k], second)
        sends.start(out.at[slot], out.at[slot], recv.at[5 * n + k], sibling)
        yield
    for r in range(2):
        for k in range(n):
            slot = pos.chunk(n - k, pos.plane[2 + r], pos.c)
            arrived(out.at[slot], recv.at[(2 + r) * n + k], second)
            sends.start(out.at[slot], out.at[slot], recv.at[(6 + r) * n + k], sibling)
            yield
    own.wait()
    for r in range(4):
        for k in range(n):
            slot = pos.chunk(n - k, pos.sib_plane[r], 1 - pos.c)
            arrived(out.at[slot], recv.at[(4 + r) * n + k], sibling)


def gather_all_sems(n):
    return [DMA((8 * n,)), DMA((8 * n,)), DMA]


def drive(streams):
    streams = list(streams)
    while streams:
        for stream in list(streams):
            if next(stream, streams) is streams:
                streams.remove(stream)


def all_partners(pos):
    return [pos.column(k) for k in range(1, pos.columns)] + [pos.flip_b(), pos.flip_y(), pos.sibling()]


def gather_start_kernel(columns, group_of, tokens, wq, wo, ffn, cot, o_tokens, o_wq, o_wo, o_ffn, o_cot, *sems):
    pos = Place(columns)
    greet(all_partners(pos))
    s = [Sends(sems[3 * i]) for i in range(5)]
    r = lambda i: (sems[3 * i + 1], sems[3 * i + 2])
    streams = [
        gather_ctx(pos, tokens, o_tokens, s[0], *r(0)),
        gather_all(pos, wq, o_wq, s[1], *r(1), group_of=group_of),
        gather_all(pos, wo, o_wo, s[2], *r(2)),
        gather_fsdp(pos, ffn, o_ffn, s[3], *r(3)),
    ]
    drive(streams)
    drive([gather_ctx(pos, cot, o_cot, s[4], *r(4))])
    for x in s:
        x.finish()


def call(kernel, collective_id, ins, outs, scratch, name, space=pl.ANY, in_space=None):
    return pl.pallas_call(
        kernel,
        out_shape=outs,
        in_specs=[pl.BlockSpec(memory_space=in_space or space)] * len(ins),
        out_specs=jax.tree.map(lambda _: pl.BlockSpec(memory_space=space), outs),
        scratch_shapes=scratch,
        compiler_params=pltpu.CompilerParams(
            collective_id=collective_id, has_side_effects=True, vmem_limit_bytes=60 << 20
        ),
        name=name,
    )(*ins)


def shaped(shape, dtype=BF):
    return jax.ShapeDtypeStruct(tuple(shape), dtype)


def gather_start(nc, tokens, wq, wo, ffn, cot):
    n = nc // 2
    group_of = lambda a: a // (n // GROUPS)
    sems = gather_ctx_sems(n) + gather_all_sems(n) * 2 + gather_fsdp_sems(ffn.shape[0]) + gather_ctx_sems(n)
    outs = (
        shaped((nc,) + tokens.shape),
        shaped((nc * 4,) + wq.shape[1:]),
        shaped((nc * 4,) + wo.shape),
        shaped((ffn.shape[0], 4) + ffn.shape[1:]),
        shaped((nc,) + cot.shape),
    )
    return call(functools.partial(gather_start_kernel, n, group_of), 1, (tokens, wq, wo, ffn, cot), outs, sems, "gather_start")


def gather_ctx_kernel(columns, src, out, send, recv, local):
    pos = Place(columns)
    greet([pos.column(k) for k in range(1, columns)] + [pos.flip_b()])
    s = Sends(send)
    drive([gather_ctx(pos, src, out, s, recv, local)])
    s.finish()


def gather_rows(nc, src, collective_id):
    n = nc // 2
    return call(functools.partial(gather_ctx_kernel, n), collective_id, (src,), shaped((nc,) + src.shape), gather_ctx_sems(n), "gather_rows")


def swap_kernel(nc, src, out, send, recv, local):
    per = nc // GROUPS
    ctx = lax.axis_index("ctx")
    group, place = ctx // per, ctx % per
    peer = lambda k: lax.rem(group + k, GROUPS)
    device = lambda k: {"ctx": peer(k) * per + place}
    greet([device(k) for k in range(1, GROUPS)])
    own = pltpu.make_async_copy(src.at[group], out.at[group], local)
    own.start()
    copies = []
    for k in range(1, GROUPS):
        copies.append(remote(src.at[peer(k)], out.at[group], send.at[k], recv.at[k], device(k)))
        copies[-1].start()
    for k in range(1, GROUPS):
        arrived(out.at[peer(GROUPS - k)], recv.at[k], device(k))
    own.wait()
    for copy in copies:
        copy.wait_send()


def swap(nc, src, collective_id):
    return call(functools.partial(swap_kernel, nc), collective_id, (src,), shaped(src.shape), [DMA((GROUPS,)), DMA((GROUPS,)), DMA], "swap")


def add(acc, *others):
    total = acc[...].astype(F32)
    for other in others:
        total = total + other[...].astype(F32)
    acc[...] = total.astype(acc.dtype)


def scatter_ctx(pos, part, out, acc, from_b, from_col, sends, recv, local):
    n = pos.columns
    loads = []
    for k in range(n):
        loads.append(pltpu.make_async_copy(part.at[pos.at(k) * 2 + pos.b], acc.at[k], local.at[k]))
        loads[-1].start()
    for k in [*range(1, n), 0]:
        sends.start(part.at[pos.at(k) * 2 + 1 - pos.b], from_b.at[k], recv.at[k], pos.flip_b())
    yield
    for k in [*range(1, n), 0]:
        loads[k].wait()
        arrived(from_b.at[k], recv.at[k], pos.flip_b())
        if k:
            add(acc.at[k], from_b.at[k])
            sends.start(acc.at[k], from_col.at[k], recv.at[n + k], pos.column(k))
            yield
    total = acc[0].astype(F32) + from_b[0].astype(F32)
    for k in range(1, n):
        arrived(from_col.at[k], recv.at[n + k], pos.column(k))
        total = total + from_col[k].astype(F32)
        yield
    out[...] = total.astype(out.dtype)


def scatter_ctx_scratch(n, shape):
    v = lambda m: pltpu.VMEM((m,) + tuple(shape), BF)
    return [v(n), v(n), v(n), DMA((2 * n,)), DMA((2 * n,)), DMA((n,))]


def scatter_ctx_kernel(columns, part, out, acc, from_b, from_col, send, recv, local):
    pos = Place(columns)
    greet([pos.column(k) for k in range(1, columns)] + [pos.flip_b()])
    s = Sends(send)
    drive([scatter_ctx(pos, part, out, acc, from_b, from_col, s, recv, local)])
    s.finish()


def scatter_rows(nc, part, collective_id):
    n = nc // 2
    return pl.pallas_call(
        functools.partial(scatter_ctx_kernel, n),
        out_shape=shaped(part.shape[1:], F32),
        in_specs=[pl.BlockSpec(memory_space=pl.ANY)],
        out_specs=pl.BlockSpec(memory_space=pltpu.VMEM),
        scratch_shapes=scatter_ctx_scratch(n, part.shape[1:]),
        compiler_params=pltpu.CompilerParams(collective_id=collective_id, has_side_effects=True, vmem_limit_bytes=60 << 20),
        name="scatter_rows",
    )(part)


def scatter_fsdp(pos, part, out, acc, from_sib, from_y, sends, recv, local):
    parts = part.shape[0]
    loads = []
    mine = [(1 - pos.y) * 2 + pos.c, pos.y * 2 + pos.c]
    his = [(1 - pos.y) * 2 + 1 - pos.c, pos.y * 2 + 1 - pos.c]
    for t in range(2):
        for p in range(parts):
            i = t * parts + p
            loads.append(pltpu.make_async_copy(part.at[p, mine[t]], acc.at[i], local.at[i]))
            loads[-1].start()
            sends.start(part.at[p, his[t]], from_sib.at[i], recv.at[i], pos.sibling())
    yield
    for p in range(parts):
        loads[p].wait()
        arrived(from_sib.at[p], recv.at[p], pos.sibling())
        add(acc.at[p], from_sib.at[p])
        sends.start(acc.at[p], from_y.at[p], recv.at[2 * parts + p], pos.flip_y())
        yield
    for p in range(parts):
        loads[parts + p].wait()
        arrived(from_sib.at[parts + p], recv.at[parts + p], pos.sibling())
        add(acc.at[parts + p], from_sib.at[parts + p])
        yield
    for p in range(parts):
        arrived(from_y.at[p], recv.at[2 * parts + p], pos.flip_y())
        out[p] = acc[parts + p].astype(F32) + from_y[p].astype(F32)
        yield


def scatter_fsdp_scratch(parts, shape):
    v = lambda m: pltpu.VMEM((m,) + tuple(shape), BF)
    return [v(2 * parts), v(2 * parts), v(parts), DMA((3 * parts,)), DMA((3 * parts,)), DMA((2 * parts,))]


def scatter_all(pos, part, out, acc, from_sib, from_2, from_1, from_col, sends, recv, local, per_group=False):
    n = pos.columns
    sibling = pos.sibling()
    first, second = pos.device(plane=pos.first), pos.device(plane=pos.second)
    loads = {}
    for r in (3, 2, 1, 0):
        for k in range(n):
            i = r * n + k
            loads[i] = pltpu.make_async_copy(part.at[pos.chunk(k, pos.plane[r], pos.c)], acc.at[i], local.at[i])
            loads[i].start()
            sends.start(part.at[pos.chunk(k, pos.sib_plane[r], 1 - pos.c)], from_sib.at[i], recv.at[i], sibling)
    yield
    for r in (3, 2):
        for k in range(n):
            i = r * n + k
            loads[i].wait()
            arrived(from_sib.at[i], recv.at[i], sibling)
            add(acc.at[i], from_sib.at[i])
            j = (r - 2) * n + k
            sends.start(acc.at[i], from_2.at[j], recv.at[4 * n + j], second)
        yield
    for k in range(n):
        i = n + k
        loads[i].wait()
        arrived(from_sib.at[i], recv.at[i], sibling)
        arrived(from_2.at[i], recv.at[4 * n + i], second)
        add(acc.at[i], from_sib.at[i], from_2.at[i])
        sends.start(acc.at[i], from_1.at[k], recv.at[6 * n + k], first)
    yield
    for k in [*range(1, n), 0]:
        loads[k].wait()
        arrived(from_sib.at[k], recv.at[k], sibling)
        arrived(from_2.at[k], recv.at[4 * n + k], second)
        arrived(from_1.at[k], recv.at[6 * n + k], first)
        if k:
            add(acc.at[k], from_sib.at[k], from_2.at[k], from_1.at[k])
            sends.start(acc.at[k], from_col.at[k], recv.at[7 * n + k], pos.column(k))
    total = acc[0].astype(F32) + from_sib[0].astype(F32) + from_2[0].astype(F32) + from_1[0].astype(F32)
    yield
    if not per_group:
        for k in range(1, n):
            arrived(from_col.at[k], recv.at[7 * n + k], pos.column(k))
            total = total + from_col[k].astype(F32)
        out[...] = total
        return
    each = n // GROUPS
    for k in range(1, n):
        arrived(from_col.at[k], recv.at[7 * n + k], pos.column(k))
    out[...] = jnp.zeros_like(out)
    for k in range(n):
        value = total if k == 0 else from_col[k].astype(F32)
        group = pos.at(n - k) // each
        out[group] = out[group] + value


def scatter_all_scratch(n, shape):
    v = lambda m: pltpu.VMEM((m,) + tuple(shape), BF)
    return [v(4 * n), v(4 * n), v(2 * n), v(n), v(n), DMA((8 * n,)), DMA((8 * n,)), DMA((4 * n,))]


def scatter_end_kernel(columns, gn, wq, wo, ffn, yy, o_gn, o_wq, o_wo, o_ffn, o_yy, *scratch):
    pos = Place(columns)
    greet(all_partners(pos))
    c1, a1, a2, f1, c2 = scratch[0:6], scratch[6:14], scratch[14:22], scratch[22:28], scratch[28:34]
    s = [Sends(x[-3]) for x in (c1, a1, a2, f1, c2)]
    drive(
        [
            scatter_ctx(pos, gn, o_gn, *c1[:-3], s[0], *c1[-2:]),
            scatter_fsdp(pos, ffn, o_ffn, *f1[:-3], s[3], *f1[-2:]),
            scatter_all(pos, wq, o_wq, *a1[:-3], s[1], *a1[-2:], per_group=True),
            scatter_all(pos, wo, o_wo, *a2[:-3], s[2], *a2[-2:]),
            scatter_ctx(pos, yy, o_yy, *c2[:-3], s[4], *c2[-2:]),
        ]
    )
    for x in s:
        x.finish()


def scatter_end(nc, gn, wq, wo, ffn, yy):
    n = nc // 2
    scratch = (
        scatter_ctx_scratch(n, gn.shape[1:])
        + scatter_all_scratch(n, wq.shape[1:])
        + scatter_all_scratch(n, wo.shape[1:])
        + scatter_fsdp_scratch(ffn.shape[0], ffn.shape[2:])
        + scatter_ctx_scratch(n, yy.shape[1:])
    )
    outs = (
        shaped(gn.shape[1:], F32),
        shaped((GROUPS,) + wq.shape[1:], F32),
        shaped(wo.shape[1:], F32),
        shaped((ffn.shape[0],) + ffn.shape[2:], F32),
        shaped(yy.shape[1:], F32),
    )
    return call(
        functools.partial(scatter_end_kernel, n), 6, (gn, wq, wo, ffn, yy), outs, scratch, "scatter_end",
        space=pltpu.VMEM, in_space=pl.ANY,
    )


def doc_ids(row_index, doc_ends):
    return jnp.sum((row_index[:, None] >= doc_ends[None, :]).astype(jnp.int32), axis=1)


def positions(row_index, lengths):
    doc_ends = jnp.cumsum(lengths)
    doc_starts = doc_ends - lengths
    doc_num = doc_ids(row_index, doc_ends)
    column = jnp.arange(lengths.shape[0], dtype=jnp.int32)
    begins = jnp.sum(jnp.where(doc_num[:, None] == column[None, :], doc_starts[None, :], 0), axis=1)
    return doc_num, row_index - begins


def rope_tables(position):
    half_dim = HEAD_DIM // 2
    inverse = ROPE_BASE ** (-2.0 * jnp.arange(half_dim, dtype=F32) / HEAD_DIM)
    angles = position.astype(F32)[:, None] * inverse[None, :]
    return jnp.cos(angles), jnp.sin(angles)


def rotate(values, cosine, sine):
    half_dim = values.shape[-1] // 2
    lower, upper = values[..., :half_dim], values[..., half_dim:]
    cosine, sine = cosine[:, None, :], sine[:, None, :]
    return jnp.concatenate([lower * cosine - upper * sine, upper * cosine + lower * sine], axis=-1)


def kept_rows(route_rows, live_rows, experts, capacity):
    count, top = route_rows.shape
    hot = (route_rows[:, :, None] == jnp.arange(experts, dtype=jnp.int32)) & live_rows[:, None, None]
    hot = hot.astype(F32)
    before = jnp.tril(jnp.ones((count, count), F32), -1)
    kept = jnp.zeros((count, experts), F32)
    base = jnp.zeros((1, experts), F32)
    for k in range(top):
        earlier = base + jnp.dot(before, hot[:, k])
        kept = kept + hot[:, k] * (earlier < capacity)
        base = base + jnp.sum(hot[:, k], axis=0, keepdims=True)
    return kept


def dot(a, b, dims):
    return lax.dot_general(a, b, (dims, ((), ())), preferred_element_type=F32)


def pad_rows(x, rows):
    return jnp.pad(x, [(0, rows - x.shape[0])] + [(0, 0)] * (x.ndim - 1))


def body(tokens, doc_lengths, routes, cotangent, attn_gain, w_qkv, w_out, mlp_gain, router, expert_in, expert_out, shared_in, shared_out):
    nc = lax.axis_size("ctx")
    nf = lax.axis_size("fsdp")
    rows, width = tokens.shape[1:]
    heads = width // HEAD_DIM
    experts = expert_in.shape[1]
    hidden = expert_in.shape[0]
    top = routes.shape[2]
    capacity = 5 * top * rows // (4 * experts)
    per = nc // GROUPS
    ctx = lax.axis_index("ctx")
    group, place = ctx // per, ctx % per
    slot = nc * rows
    mine = heads // GROUPS
    share = mine * HEAD_DIM
    scale = 1.0 / math.sqrt(HEAD_DIM)
    owned = w_out.shape[0]
    padded = -(-(owned + 2 + experts) // 16) * 16

    wq_send = w_qkv.reshape(owned, 3, GROUPS, share).transpose(2, 0, 1, 3).reshape(GROUPS, owned, 3 * share)
    wq_send = jnp.pad(wq_send, ((0, 0), (0, padded - owned), (0, 0)))
    small = jnp.concatenate([attn_gain[None], mlp_gain[None], router.T], axis=0)
    wo_send = pad_rows(jnp.concatenate([w_out, jnp.pad(small, ((0, 0), (0, width - owned)))], axis=0), padded)
    gate_up = jnp.concatenate([expert_in.transpose(2, 1, 0, 3), shared_in.transpose(1, 0, 2)[:, None]], axis=1)
    down = jnp.concatenate([expert_out.transpose(1, 0, 2), shared_out[None]], axis=0)
    ffn_send = jnp.concatenate([gate_up, down[None]], axis=0).reshape(3, (experts + 1) * hidden, width)

    x_all, wq_all, wo_all, ffn_all, cot_all = gather_start(nc, tokens[0], wq_send, wo_send, ffn_send, cotangent[0])
    units = nf * (experts + 1) * hidden
    w_gate, w_up, w_down = (ffn_all[p].reshape(units, width) for p in range(3))
    wq = wq_all[:, :owned].reshape(width, 3 * share)
    wo = wo_all[:, :owned].reshape(width, width)
    small = wo_all[:, owned : owned + 2 + experts, :owned].transpose(1, 0, 2).reshape(2 + experts, width)
    gain_a, gain_m = small[0].astype(F32), small[1].astype(F32)
    router_t = small[2:]

    all_rows = jnp.arange(slot, dtype=jnp.int32)
    doc_num, position = positions(all_rows, doc_lengths[0])
    cosine, sine = rope_tables(position)
    live_all = (doc_num < doc_lengths.shape[1]).astype(F32)[:, None]
    x_slot = x_all.reshape(slot, width).astype(F32)
    inv_attn = lax.rsqrt(jnp.mean(x_slot * x_slot, axis=-1, keepdims=True) + EPSILON)
    normed = (x_slot * inv_attn * gain_a).astype(BF)

    def queries(v):
        return lax.dynamic_index_in_dim(v.reshape((GROUPS, per, rows) + v.shape[1:]), place, 1, False).reshape((GROUPS * rows,) + v.shape[1:])

    normed_q = queries(normed)
    cos_q, sin_q = queries(cosine), queries(sine)
    q = rotate(dot(normed_q, wq[:, :share], ((1,), (0,))).reshape(-1, mine, HEAD_DIM), cos_q, sin_q).astype(BF)
    k = rotate(dot(normed, wq[:, share : 2 * share], ((1,), (0,))).reshape(slot, mine, HEAD_DIM), cosine, sine).astype(BF)
    v = dot(normed, wq[:, 2 * share :], ((1,), (0,))).reshape(slot, mine, HEAD_DIM).astype(BF)
    rows_q, doc_q = queries(all_rows), queries(doc_num)
    allowed = (doc_q[:, None] == doc_num[None, :]) & (all_rows[None, :] <= rows_q[:, None])
    scores = jnp.einsum("qhd,khd->hqk", q, k, preferred_element_type=F32) * scale
    scores = jnp.where(allowed[None], scores, MASKED)
    expo = jnp.exp(scores - jnp.max(scores, axis=-1, keepdims=True))
    prob = expo / jnp.sum(expo, axis=-1, keepdims=True)
    prob_b = prob.astype(BF)
    o = jnp.einsum("hqk,khd->qhd", prob_b, v, preferred_element_type=F32).astype(BF)

    o_own = swap(nc, o.reshape(GROUPS, rows, share), 2)
    attn = o_own.transpose(1, 0, 2).reshape(rows, width)

    row_index = ctx * rows + jnp.arange(rows, dtype=jnp.int32)
    doc_own, _ = positions(row_index, doc_lengths[0])
    live_rows = doc_own < doc_lengths.shape[1]
    live = live_rows.astype(F32)[:, None]
    x = tokens[0].astype(F32)
    resid = x + dot(attn, wo, ((1,), (0,)))
    inv_mlp = lax.rsqrt(jnp.mean(resid * resid, axis=-1, keepdims=True) + EPSILON)
    mixed = (resid * inv_mlp * gain_m).astype(BF)
    logits = dot(mixed, router_t, ((1,), (1,)))
    router_prob = jax.nn.softmax(logits, axis=-1)
    kept = kept_rows(routes[0], live_rows, experts, capacity)
    weight = router_prob * kept
    high = weight.astype(BF)
    low = (weight - high.astype(F32)).astype(BF)
    extra = pad_rows(jnp.pad(jnp.concatenate([high, low], axis=1).T, ((0, 0), (0, width - rows))), 16)
    mixed_all = gather_rows(nc, jnp.concatenate([mixed, extra], axis=0), 3)

    weights = mixed_all[:, rows : rows + 2 * experts, :rows].astype(F32)
    weights = (weights[:, :experts] + weights[:, experts:]).transpose(0, 2, 1).reshape(slot, experts)
    mix = mixed_all[:, :rows].reshape(slot, width)
    g = (cot_all.reshape(slot, width) * live_all.astype(BF)).astype(BF)
    unit_weight = jnp.concatenate([weights, jnp.ones((slot, 1), F32)], axis=1)
    unit_weight = jnp.tile(jnp.repeat(unit_weight, hidden, axis=1), (1, nf))
    gate = dot(mix, w_gate, ((1,), (1,)))
    up = dot(mix, w_up, ((1,), (1,)))
    sig = jax.nn.sigmoid(gate)
    hid = gate * sig * up
    hid_w = (hid * unit_weight).astype(BF)
    y_part = dot(hid_w, w_down, ((1,), (0,))).astype(BF)
    back = dot(g, w_down, ((1,), (1,)))
    pair = (hid * back).reshape(slot, nf, experts + 1, hidden).sum(axis=(1, 3))[:, :experts]
    back_w = back * unit_weight
    d_gate = (back_w * up * sig * (1.0 + gate * (1.0 - sig))).astype(BF)
    d_up = (back_w * gate * sig).astype(BF)
    gm_part = (dot(d_gate, w_gate, ((1,), (0,))) + dot(d_up, w_up, ((1,), (0,)))).astype(BF)
    d_w = jnp.stack([dot(d_gate, mix, ((0,), (0,))), dot(d_up, mix, ((0,), (0,))), dot(hid_w, g, ((0,), (0,)))]).astype(BF)
    pair_t = pair.reshape(nc, rows, experts).transpose(0, 2, 1)
    pair_t = jnp.pad(pair_t, ((0, 0), (0, 16 - experts), (0, width - rows))).astype(BF)
    gm_all = scatter_rows(nc, jnp.concatenate([gm_part.reshape(nc, rows, width), pair_t], axis=1), 4)

    grad_prob = gm_all[rows : rows + experts, :rows].T * kept
    grad_logits = (router_prob * (grad_prob - jnp.sum(router_prob * grad_prob, axis=-1, keepdims=True))).astype(BF)
    grad_router_t = dot(grad_logits, mixed, ((0,), (0,)))
    grad_mixed = gm_all[:rows] + dot(grad_logits, router_t, ((1,), (0,)))
    grad_top = cotangent[0].astype(F32) * live
    w = grad_mixed * gain_m
    grad_resid = grad_top + inv_mlp * w - resid * jnp.mean(w * resid, axis=-1, keepdims=True) * inv_mlp**3
    grad_gain_m = jnp.sum(grad_mixed * resid * inv_mlp, axis=0)
    grad_resid_b = grad_resid.astype(BF)
    grad_wo = dot(attn, grad_resid_b, ((0,), (0,)))
    grad_attn = dot(grad_resid_b, wo, ((1,), (1,))).astype(BF)
    do = swap(nc, grad_attn.reshape(rows, GROUPS, share).transpose(1, 0, 2), 5).reshape(GROUPS * rows, mine, HEAD_DIM)

    grad_p = jnp.einsum("qhd,khd->hqk", do, v, preferred_element_type=F32)
    delta = jnp.sum(prob * grad_p, axis=-1, keepdims=True)
    grad_s = (prob * (grad_p - delta)).astype(BF)
    dq = jnp.einsum("hqk,khd->qhd", grad_s, k, preferred_element_type=F32) * scale
    dk = jnp.einsum("hqk,qhd->khd", grad_s, q, preferred_element_type=F32) * scale
    dv = jnp.einsum("hqk,qhd->khd", prob_b, do, preferred_element_type=F32)
    dq = rotate(dq, cos_q, -sin_q).reshape(GROUPS * rows, share).astype(BF)
    dk = rotate(dk, cosine, -sine).reshape(slot, share)
    dkv = jnp.concatenate([dk, dv.reshape(slot, share)], axis=1).astype(BF)
    grad_wq = jnp.concatenate([dot(normed_q, dq, ((0,), (0,))), dot(normed, dkv, ((0,), (0,)))], axis=1)
    gn_q = dot(dq, wq[:, :share], ((1,), (1,))).reshape(GROUPS, 1, rows, width)
    here = (jnp.arange(per) == place).astype(F32)[None, :, None, None]
    gn = dot(dkv, wq[:, share:], ((1,), (1,))).reshape(GROUPS, per, rows, width) + gn_q * here
    gn_part = gn.reshape(nc, rows, width).astype(BF)

    gn_full = gn.reshape(slot, width)
    grad_gain_a = jnp.sum(gn_full * x_slot * inv_attn, axis=0)
    small = jnp.concatenate([grad_gain_a[None], grad_gain_m[None], grad_router_t], axis=0)
    small = small.reshape(2 + experts, nc * nf, owned).transpose(1, 0, 2)
    wo_part = jnp.concatenate([grad_wo.reshape(nc * nf, owned, width), jnp.pad(small, ((0, 0), (0, 0), (0, width - owned)))], axis=1)
    wo_part = jnp.pad(wo_part, ((0, 0), (0, padded - wo_part.shape[1]), (0, 0))).astype(BF)
    wq_part = jnp.pad(grad_wq.reshape(nc * nf, owned, 3 * share), ((0, 0), (0, padded - owned), (0, 0))).astype(BF)
    ffn_part = d_w.reshape(3, nf, (experts + 1) * hidden, width)
    gn_own, wq_own, wo_own, ffn_own, y_own = scatter_end(nc, gn_part, wq_part, wo_part, ffn_part, y_part.reshape(nc, rows, width))

    layer_out = (live * (resid + y_own)).astype(BF)[None]
    inv = lax.rsqrt(jnp.mean(x * x, axis=-1, keepdims=True) + EPSILON)
    w = gn_own * gain_a
    grad_tokens = (grad_resid + inv * w - x * jnp.mean(w * x, axis=-1, keepdims=True) * inv**3)[None]
    grad_w_qkv = wq_own[:, :owned].reshape(GROUPS, owned, 3, share).transpose(1, 2, 0, 3).reshape(owned, 3 * width)
    small = wo_own[owned : owned + 2 + experts, :owned]
    out = ffn_own.reshape(3, experts + 1, hidden, width)
    return (
        layer_out,
        grad_tokens,
        small[0],
        grad_w_qkv,
        wo_own[:owned],
        small[1],
        small[2:].T,
        out[:2, :experts].transpose(2, 1, 0, 3),
        out[2, :experts].transpose(1, 0, 2),
        out[:2, experts].transpose(1, 0, 2),
        out[2, experts],
    )


def solution(mesh):
    rows = P("fsdp", "ctx", None)
    flat = ("ctx", "fsdp")
    weights = (P(flat), P(flat, None), P(flat, None), P(flat), P(flat, None))
    ffn = (P(flat, None, None, None), P(flat, None, None), P(flat, None, None), P(flat, None))
    return jax.shard_map(
        body,
        mesh=mesh,
        in_specs=(rows, P("fsdp", None), rows, rows) + weights + ffn,
        out_specs=(rows, rows) + weights + ffn,
        check_vma=False,
    )
```

time: 2340 us -> 462 us (0.20)
  waiting for transfers between devices: 1750 us -> 0 us
  Pallas kernels: 0 us -> 239 us
  blocking collectives: 197 us -> 0 us
  matrix products: 168 us -> 90.5 us
  other arithmetic: 95.1 us -> 43.9 us
  local copies, waits for them, and re-layouts: 109 us -> 82.3 us
    all_gather x12 -> x0, waiting for transfers between devices: 899 us -> none  [the longest x1 449 us: body(): part_in = lax.all_gather(group_in, 'ctx', axis=0, tiled=True)]
    reduce_scatter x3 -> x0, waiting for transfers between devices: 846 us -> none  [the longest x1 625 us: body(): lax.psum_scatter(jnp.concatenate([term_in, term_out, term_sin, term_sout]...]
    pallas_call x0 -> x6, Pallas kernels: none -> 239 us  [the longest x5 211 us: call(): pl.pallas_call(kernel, out_shape=outs, in_specs=[pl.BlockSpec(memory_spac...]
    all_gather x5 -> x0, blocking collectives: 115 us -> none  [the longest x1 40.6 us: body(): lax.all_gather(router, ('ctx', 'fsdp'), axis=0, tiled=True)]
    reshape x6 -> x9, local copies, waits for them, and re-layouts: 91.2 us -> 3.32 us  [the longest x2 1.05 us: body(): wq_own[:, :owned].reshape(GROUPS, owned, 3, share).transpose(1, 2, 0, 3)]
    dot_general x49 -> x29, matrix products: 168 us -> 84.3 us  [the longest x22 58.5 us: dot(): return lax.dot_general(a, b, (dims, ((), ())), preferred_element_type=F32)]
    unnamed x2 -> x0, blocking collectives: 81.6 us -> none
    concatenate x4 -> x10, other arithmetic: 78.6 us -> 11.6 us  [the longest x1 2.76 us: body(): jnp.concatenate([gm_part.reshape(nc, rows, width), pair_t], axis=1)]
  transfers between devices with their start and end apart: 15 -> 0, of which waited for: 13 -> 0; matrix products, arithmetic and copies ran while one was open for 16% -> 0% of each run, Pallas kernels for 0% -> 0%
where the time goes in v1:
time: 462 us; the launch traced here: 457 us
  Pallas kernels  239 us (52%)
  matrix products  90.5 us (20%)
  local copies, waits for them, and re-layouts  82.3 us (18%)
  other arithmetic  43.9 us (10%)
    pallas_call x5, Pallas kernels, call(): pl.pallas_call(kernel, out_shape=outs, in_specs=[pl.BlockSpec(memory_spac...  211 us
    dot_general x22, matrix products, dot(): return lax.dot_general(a, b, (dims, ((), ())), preferred_element_type=F32)  58.5 us
    pallas_call x1, Pallas kernels, scatter_rows(): pl.pallas_call(functools.partial(scatter_ctx_kernel, n), out_shape=shaped...  27.4 us
    dot_general x5, local copies, waits for them, and re-layouts, dot(): return lax.dot_general(a, b, (dims, ((), ())), preferred_element_type=F32)  15.4 us
    dot_general x1, matrix products, body(): jnp.einsum('hqk,khd->qhd', prob_b, v, preferred_element_type=F32).astype(BF)  15 us
    unnamed x160, local copies, waits for them, and re-layouts  12.2 us

profile of v1, /device:TPU:0, one launch (start us, length us, event | category | flops | bytes accessed | tf_op | source)
XLA Modules:
  0.0 457.3 jit_solution(6240285566638158252)
XLA Ops:
  0.7 2.6 pad_maximum_fusion.2
  7.1 93.8 %gather_start.1 = (bf16[8,128,768]{2,1,0:T(8,128)(2,1)}, bf16[32,32,576]{2,1,0:T(8,128)(2,1)}, bf16[32,32,768]{2,1,0:T(8,128)(2,1)}, bf16[3,4,320,768]{3,2,1,0:T(8,128)(2,1)}, bf16[8,128,768]{2,1,0:T(8,128)(2,1)}) custom-call(bf16[128,768]{1,0:T(8,128)(2,1)} %bitcast.274, bf16[4,32,576]{2,1,0:T(8,128)(2,1)} %pad.41.wq, bf16[32,768]{1,0:T(8,128)(2,1)} %fusion.62.wo, ...), custom_call_target="tpu_custom_call" | custom-call | tf_op jit(solution)/shard_map/gather_start/pallas_call | solution.py:218
  119.5 6.3 %fusion.107 = (f32[3,512]{1,0:T(4,128)S(1)}, f32[3,512,1024]{2,1,0:T(8,128)}) fusion(pred[512,1024]{1,0:T(8,128)(4,1)} %fusion.15, bf16[1024,3,32]{0,2,1:T(8,128)(2,1)} %get-tuple-element.95, bf16[1024,3,32]{0,2,1:T(8,128)(2,1)} %get-tuple-element.94, bf16[512,3,32]{0,2,1:T(8,128)(2,1)} %get-tuple-element.102, bf16[512,3,32]{0,2,1:T(8,128)(2,1)} %get-tuple-element.101), kind=kOutput, calls=%fused_computation.226 | convolution fusion | flops 208798720 | bytes 7411712 | tf_op jit(solution)/shard_map/sub | solution.py:582
  128.3 15.0 %fusion.32 = bf16[512,3,64]{0,2,1:T(8,128)(2,1)S(1)} fusion(bf16[1024,3,64]{0,2,1:T(8,128)(2,1)S(1)} %convolution_convert_fusion.3, f32[3,512,1024]{2,1,0:T(8,128)} %get-tuple-element.121, f32[3,512]{1,0:T(4,128)S(1)} %get-tuple-element.120), kind=kOutput, calls=%fused_computation.64 | convolution fusion | flops 204570624 | bytes 6887424 | tf_op jit(solution)/shard_map/hqk,khd->qhd/dot_general | solution.py:585
  144.2 11.9 %swap.2 = bf16[4,128,192]{2,1,0:T(8,128)(2,1)} custom-call(bf16[4,128,192]{2,1,0:T(8,128)(2,1)} %copy.114.src), custom_call_target="tpu_custom_call" | custom-call | tf_op jit(solution)/shard_map/swap/pallas_call | solution.py:218
  169.1 29.0 %gather_rows.1 = bf16[8,144,768]{2,1,0:T(8,128)(2,1)} custom-call(bf16[144,768]{1,0:T(8,128)(2,1)} %fusion.51.src), custom_call_target="tpu_custom_call" | custom-call | tf_op jit(solution)/shard_map/gather_rows/pallas_call | solution.py:218
  199.6 5.7 %fusion.105 = (bf16[1,4,320,768]{3,2,1,0:T(8,128)(2,1)S(1)}, bf16[1,4,320,768]{3,2,1,0:T(8,128)(2,1)}, bf16[1,4,320,768]{3,2,1,0:T(8,128)(2,1)}) fusion(bf16[3,4,320,768]{3,2,1,0:T(8,128)(2,1)} %get-tuple-element.25), kind=kLoop, calls=%fused_computation.224 | loop fusion | bytes 11796480 | tf_op jit(solution)/shard_map/slice | solution.py:555
  205.3 4.6 %fusion.112 = f32[1024,1280]{1,0:T(8,128)} fusion(bf16[1024,768]{1,0:T(8,128)(2,1)S(1)} %bitcast.298, bf16[1280,768]{1,0:T(8,128)(2,1)S(1)} %bitcast.289), kind=kOutput, calls=%fused_computation.231 | convolution fusion | flops 2013265920 | bytes 8781824 | tf_op jit(solution)/shard_map/dot_general | solution.py:519
  210.8 2.9 tile.11
  213.7 5.9 %copy.117 = f32[1024,1280]{1,0:T(8,128)} copy(f32[1024,1280]{0,1:T(8,128)} %bitcast.261) | data formatting | bytes 10485760 | tf_op jit(solution)/shard_map/tile | solution.py:612
  224.8 9.5 %multiply_convert_fusion.1 = (bf16[1024,1280]{1,0:T(8,128)(2,1)}, bf16[1024,1280]{1,0:T(8,128)(2,1)}, f32[1024,1280]{1,0:T(8,128)}, bf16[1024,1280]{1,0:T(8,128)(2,1)}) fusion(f32[1024,1280]{1,0:T(8,128)S(1)} %bitcast.270, f32[1024,1280]{1,0:T(8,128)} %fusion.112, f32[1024,1280]{1,0:T(8,128)S(1)} %fusion.111, bf16[1024,768]{1,0:T(8,128)(2,1)S(1)} %bitcast.301, ...), kind=kOutput, calls=%fused_computation.6 | convolution fusion | flops 2038169600 | bytes 32374784 | tf_op jit(solution)/shard_map/dot_general | solution.py:519
  234.3 4.5 copy.129
  238.8 5.7 %convert_bitcast_fusion.1 = bf16[1,4,320,768]{3,2,1,0:T(8,128)(2,1)} fusion(bf16[4,320,1024]{2,1,0:T(8,128)(2,1)} %bitcast.284, bf16[1024,768,1]{1,0,2:T(8,128)(2,1)} %bitcast.299), kind=kOutput, calls=%fused_computation.37 | convolution fusion | flops 2014248960 | bytes 6160384 | tf_op jit(solution)/shard_map/dot_general | solution.py:519
  244.5 4.5 copy.128
  248.9 5.7 %convert_bitcast_fusion.2 = bf16[1,4,320,768]{3,2,1,0:T(8,128)(2,1)} fusion(bf16[4,320,1024]{2,1,0:T(8,128)(2,1)} %bitcast.282, bf16[1024,768,1]{1,0,2:T(8,128)(2,1)} %bitcast.300), kind=kOutput, calls=%fused_computation.38 | convolution fusion | flops 2014248960 | bytes 6160384 | tf_op jit(solution)/shard_map/dot_general | solution.py:519
  254.6 4.5 copy.131
  259.1 4.5 convert_bitcast_fusion
  263.7 3.6 pad_maximum_fusion.ffn
  270.5 3.3 add_convert_fusion
  273.8 6.0 %copy.118 = f32[1024,1280]{0,1:T(8,128)} copy(f32[1024,1280]{1,0:T(8,128)} %get-tuple-element.85) | data formatting | bytes 10485760 | tf_op jit(solution)/shard_map/mul | solution.py:620
  279.8 2.9 reduce_sum.155
  282.8 2.8 fusion.16.part
  285.5 27.4 %scatter_rows.1 = f32[144,768]{1,0:T(8,128)} custom-call(bf16[8,144,768]{2,1,0:T(8,128)(2,1)} %fusion.16.part), custom_call_target="tpu_custom_call" | custom-call | tf_op jit(solution)/shard_map/scatter_rows/pallas_call | solution.py:332
  324.4 7.9 %swap.3 = bf16[4,128,192]{2,1,0:T(8,128)(2,1)} custom-call(bf16[4,128,192]{2,1,0:T(8,128)(2,1)} %bitcast.309), custom_call_target="tpu_custom_call" | custom-call | tf_op jit(solution)/shard_map/swap/pallas_call | solution.py:218
  333.5 3.7 multiply_reduce_fusion
  337.2 3.5 multiply_convert_fusion
  342.6 4.3 fusion.25
  351.6 5.2 %fusion.6 = (bf16[768]{0:T(1024)(128)(2,1)S(1)}, bf16[1024,768]{1,0:T(8,128)(2,1)}, f32[1024,768]{1,0:T(8,128)}) fusion(bf16[8,128,768]{2,1,0:T(8,128)(2,1)S(1)} %copy-done, f32[1024]{0:T(1024)S(1)} %bitcast.326, f32[1024]{0:T(1024)S(1)} %copy-done.55, f32[4,128,768]{2,1,0:T(8,128)S(1)} %fusion.49, f32[768]{0:T(1024)S(1)} %reshape.578, ...), kind=kOutput, calls=%fused_computation.19 | convolution fusion | flops 612629760 | bytes 9253376 | tf_op jit(solution)/shard_map/dot_general | solution.py:519
  366.4 3.6 fusion.10.gn
  370.0 3.4 convolution_convert_fusion
  373.4 68.6 %scatter_end.1 = (f32[128,768]{1,0:T(8,128)}, f32[4,32,576]{2,1,0:T(8,128)}, f32[32,768]{1,0:T(8,128)}, f32[3,320,768]{2,1,0:T(8,128)}, f32[128,768]{1,0:T(8,128)}) custom-call(bf16[8,128,768]{2,1,0:T(8,128)(2,1)} %fusion.10.gn, bf16[32,32,576]{2,1,0:T(8,128)(2,1)} %pad.47.wq, bf16[32,32,768]{2,1,0:T(8,128)(2,1)} %pad.49.wo, ...), custom_call_target="tpu_custom_call" | custom-call | tf_op jit(solution)/shard_map/scatter_end/pallas_call | solution.py:218
  443.5 2.4 copy.133
  (289 shorter events, 90.3 us)
Async XLA Ops:
  100.9 4.8 %copy-start = (bf16[8,128,768]{2,1,0:T(8,128)(2,1)S(1)}, bf16[8,128,768]{2,1,0:T(8,128)(2,1)}, u32[]{:S(2)}) copy-start(bf16[8,128,768]{2,1,0:T(8,128)(2,1)} %get-tuple-element.21) | copy-start | bytes 4718596
  106.2 4.8 %copy-start.1 = (bf16[4,1,128,768]{3,2,1,0:T(8,128)(2,1)}, bf16[4,1,128,768]{3,2,1,0:T(8,128)(2,1)S(1)}, u32[]{:S(2)}) copy-start(bf16[4,1,128,768]{3,2,1,0:T(8,128)(2,1)S(1)} %fusion.19) | copy-start | bytes 2359300
  119.5 6.3 %copy-start.27 = (bf16[192,768]{0,1:T(8,128)(2,1)S(1)}, bf16[192,768]{0,1:T(8,128)(2,1)}, u32[]{:S(2)}) copy-start(bf16[192,768]{0,1:T(8,128)(2,1)} %get-tuple-element.98) | copy-start | bytes 884740
  125.8 17.5 %copy-start.58 = (f32[3,512]{1,0:T(4,128)}, f32[3,512]{1,0:T(4,128)S(1)}, u32[]{:S(2)}) copy-start(f32[3,512]{1,0:T(4,128)S(1)} %get-tuple-element.120) | copy-start | bytes 18436
  128.3 15.0 %copy-start.75 = (bf16[1024,3,64]{0,2,1:T(8,128)(2,1)}, bf16[1024,3,64]{0,2,1:T(8,128)(2,1)S(1)}, u32[]{:S(2)}) copy-start(bf16[1024,3,64]{0,2,1:T(8,128)(2,1)S(1)} %convolution_convert_fusion.3) | copy-start | bytes 1179652
  143.3 15.4 %copy-start.7 = (bf16[1,128,768]{2,1,0:T(8,128)(2,1)S(1)}, bf16[1,128,768]{2,1,0:T(8,128)(2,1)}, u32[]{:S(2)}) copy-start(bf16[1,128,768]{2,1,0:T(8,128)(2,1)} %param.13) | copy-start | bytes 589828
  157.3 7.3 %copy-start.20 = (bf16[128,4,192]{0,2,1:T(8,128)(2,1)}, bf16[128,4,192]{0,2,1:T(8,128)(2,1)S(1)}, u32[]{:S(2)}) copy-start(bf16[128,4,192]{0,2,1:T(8,128)(2,1)S(1)} %copy.115) | copy-start | bytes 589828
  160.6 38.9 %copy-start.5 = (bf16[128,768]{1,0:T(8,128)(2,1)}, bf16[128,768]{1,0:T(8,128)(2,1)S(1)}, u32[]{:S(2)}) copy-start(bf16[128,768]{1,0:T(8,128)(2,1)S(1)} %multiply_convert_fusion.6) | copy-start | bytes 589828
  165.1 148.5 %copy-start.61 = (f32[128]{0:T(128)}, f32[128]{0:T(128)S(1)}, u32[]{:S(2)}) copy-start(f32[128]{0:T(128)S(1)} %fusion.82) | copy-start | bytes 1540
  168.3 145.3 %copy-start.53 = (f32[128,4]{0,1:T(4,128)}, f32[128,4]{0,1:T(4,128)S(1)}, u32[]{:S(2)}) copy-start(f32[128,4]{0,1:T(4,128)S(1)} %get-tuple-element.126) | copy-start | bytes 6148
  199.6 5.7 %copy-start.25 = (bf16[8,128,768]{2,1,0:T(8,128)(2,1)}, bf16[8,128,768]{2,1,0:T(8,128)(2,1)S(1)}, u32[]{:S(2)}) copy-start(bf16[8,128,768]{2,1,0:T(8,128)(2,1)S(1)} %slice.157) | copy-start | bytes 4718596
  205.3 4.6 %copy-start.16 = (bf16[1,4,320,768]{3,2,1,0:T(8,128)(2,1)}, bf16[1,4,320,768]{3,2,1,0:T(8,128)(2,1)S(1)}, u32[]{:S(2)}) copy-start(bf16[1,4,320,768]{3,2,1,0:T(8,128)(2,1)S(1)} %get-tuple-element.87) | copy-start | bytes 5898244
  259.1 4.6 copy-start.18
  259.1 4.6 copy-start.19
  263.7 4.5 copy-start.17
  282.7 30.2 %copy-start.57 = (f32[128]{0:T(128)S(1)}, f32[128]{0:T(128)}, u32[]{:S(2)}) copy-start(f32[128]{0:T(128)} %copy-done.56) | copy-start | bytes 1540
  282.7 30.9 %copy-start.51 = (bf16[4,768]{1,0:T(4,128)(2,1)S(1)}, bf16[4,768]{1,0:T(4,128)(2,1)}, u32[]{:S(2)}) copy-start(bf16[4,768]{1,0:T(4,128)(2,1)} %slice.149) | copy-start | bytes 18436
  282.7 30.9 %copy-start.64 = (f32[128]{0:T(128)S(1)}, f32[128]{0:T(128)}, u32[]{:S(2)}) copy-start(f32[128]{0:T(128)} %copy-done.63) | copy-start | bytes 1540
  282.7 32.9 %copy-start.65 = (f32[128]{0:T(128)S(1)}, f32[128]{0:T(128)}, u32[]{:S(2)}) copy-start(f32[128]{0:T(128)} %get-tuple-element.116) | copy-start | bytes 1540
  282.8 32.9 %copy-start.70 = (f32[128]{0:T(128)S(1)}, f32[128]{0:T(128)}, u32[]{:S(2)}) copy-start(f32[128]{0:T(128)} %get-tuple-element.118) | copy-start | bytes 1540
  285.5 31.2 %copy-start.21 = (bf16[128,4,192]{0,2,1:T(8,128)(2,1)S(1)}, bf16[128,4,192]{0,2,1:T(8,128)(2,1)}, u32[]{:S(2)}) copy-start(bf16[128,4,192]{0,2,1:T(8,128)(2,1)} %copy-done.20) | copy-start | bytes 589828
  285.5 32.7 %copy-start.6 = (bf16[128,768]{1,0:T(8,128)(2,1)S(1)}, bf16[128,768]{1,0:T(8,128)(2,1)}, u32[]{:S(2)}) copy-start(bf16[128,768]{1,0:T(8,128)(2,1)} %copy-done.5) | copy-start | bytes 589828
  316.7 16.6 %copy-start.3 = (f32[128,768]{1,0:T(8,128)}, f32[128,768]{1,0:T(8,128)S(1)}, u32[]{:S(2)}) copy-start(f32[128,768]{1,0:T(8,128)S(1)} %multiply_subtract_fusion) | copy-start | bytes 1179652
  319.8 13.7 %copy-start.59 = (f32[3,512]{1,0:T(4,128)S(1)}, f32[3,512]{1,0:T(4,128)}, u32[]{:S(2)}) copy-start(f32[3,512]{1,0:T(4,128)} %copy-done.58) | copy-start | bytes 18436
  342.6 4.3 copy-start.34
  351.6 5.4 %copy-start.60 = (bf16[768]{0:T(1024)(128)(2,1)S(1)}, bf16[768]{0:T(1024)(128)(2,1)}, u32[]{:S(2)}) copy-start(bf16[768]{0:T(1024)(128)(2,1)} %get-tuple-element.75) | copy-start | bytes 4612
  443.5 5.0 %copy-start.47 = (f32[4,32,576]{2,1,0:T(8,128)S(1)}, f32[4,32,576]{2,1,0:T(8,128)}, u32[]{:S(2)}) copy-start(f32[4,32,576]{2,1,0:T(8,128)} %get-tuple-element.29) | copy-start | bytes 884740
  447.1 4.8 %copy-start.8 = (bf16[1,128,768]{2,1,0:T(8,128)(2,1)S(1)}, bf16[1,128,768]{2,1,0:T(8,128)(2,1)}, u32[]{:S(2)}) copy-start(bf16[1,128,768]{2,1,0:T(8,128)(2,1)} %param.13) | copy-start | bytes 589828
  447.1 4.8 %copy-start.28 = (f32[128,768]{1,0:T(8,128)S(1)}, f32[128,768]{1,0:T(8,128)}, u32[]{:S(2)}) copy-start(f32[128,768]{1,0:T(8,128)} %get-tuple-element.27) | copy-start | bytes 1179652
  448.5 4.5 copy-start.42
  448.5 4.5 copy-start.66
  448.9 6.5 %copy-start.50 = (f32[32,768]{1,0:T(8,128)S(1)}, f32[32,768]{1,0:T(8,128)}, u32[]{:S(2)}) copy-start(f32[32,768]{1,0:T(8,128)} %get-tuple-element.28) | copy-start | bytes 294916
  (46 other events, 105.2 us)

commit v2 on v1

--- a/solution.py
+++ b/solution.py
@@ -3,6 +3,7 @@
 
 import jax
 import jax.numpy as jnp
+import numpy as np
 from jax import lax
 from jax.experimental import pallas as pl
 from jax.experimental.pallas import tpu as pltpu
@@ -12,6 +13,8 @@
 EPSILON = 1e-05
 ROPE_BASE = 10000.0
 MASKED = -1e30
+NN, NT, TN = ((1,), (0,)), ((1,), (1,)), ((0,), (0,))
+FUSED_BYTES = 2 << 20
 GROUPS = 4
 MESH = pl.DeviceIdType.MESH
 DMA = pltpu.SemaphoreType.DMA
@@ -89,7 +92,7 @@
     remote(dst, dst, recv, recv, device).wait_recv()
 
 
-def gather_ctx(pos, src, out, sends, recv, local):
+def gather_ctx(pos, src, out, sends, recv, local, there=lambda slot: None):
     n = pos.columns
     me = pos.a * 2 + pos.b
     own = pltpu.make_async_copy(src, out.at[me], local)
@@ -98,16 +101,19 @@
         sends.start(src, out.at[me], recv.at[k], pos.column(k))
     sends.start(src, out.at[me], recv.at[n], pos.flip_b())
     yield
+    own.wait()
+    there(me)
     for k in range(1, n):
         slot = pos.at(n - k) * 2 + pos.b
         arrived(out.at[slot], recv.at[k], pos.column(k))
         sends.start(out.at[slot], out.at[slot], recv.at[n + k], pos.flip_b())
+        there(slot)
         yield
     for k in range(n):
         slot = pos.at(n - k) * 2 + 1 - pos.b
         arrived(out.at[slot], recv.at[n + k], pos.flip_b())
+        there(slot)
         yield
-    own.wait()
 
 
 def gather_ctx_sems(n):
@@ -197,90 +203,12 @@
     return [pos.column(k) for k in range(1, pos.columns)] + [pos.flip_b(), pos.flip_y(), pos.sibling()]
 
 
-def gather_start_kernel(columns, group_of, tokens, wq, wo, ffn, cot, o_tokens, o_wq, o_wo, o_ffn, o_cot, *sems):
-    pos = Place(columns)
-    greet(all_partners(pos))
-    s = [Sends(sems[3 * i]) for i in range(5)]
-    r = lambda i: (sems[3 * i + 1], sems[3 * i + 2])
-    streams = [
-        gather_ctx(pos, tokens, o_tokens, s[0], *r(0)),
-        gather_all(pos, wq, o_wq, s[1], *r(1), group_of=group_of),
-        gather_all(pos, wo, o_wo, s[2], *r(2)),
-        gather_fsdp(pos, ffn, o_ffn, s[3], *r(3)),
-    ]
-    drive(streams)
-    drive([gather_ctx(pos, cot, o_cot, s[4], *r(4))])
-    for x in s:
-        x.finish()
-
-
-def call(kernel, collective_id, ins, outs, scratch, name, space=pl.ANY, in_space=None):
-    return pl.pallas_call(
-        kernel,
-        out_shape=outs,
-        in_specs=[pl.BlockSpec(memory_space=in_space or space)] * len(ins),
-        out_specs=jax.tree.map(lambda _: pl.BlockSpec(memory_space=space), outs),
-        scratch_shapes=scratch,
-        compiler_params=pltpu.CompilerParams(
-            collective_id=collective_id, has_side_effects=True, vmem_limit_bytes=60 << 20
-        ),
-        name=name,
-    )(*ins)
-
-
 def shaped(shape, dtype=BF):
     return jax.ShapeDtypeStruct(tuple(shape), dtype)
 
 
-def gather_start(nc, tokens, wq, wo, ffn, cot):
-    n = nc // 2
-    group_of = lambda a: a // (n // GROUPS)
-    sems = gather_ctx_sems(n) + gather_all_sems(n) * 2 + gather_fsdp_sems(ffn.shape[0]) + gather_ctx_sems(n)
-    outs = (
-        shaped((nc,) + tokens.shape),
-        shaped((nc * 4,) + wq.shape[1:]),
-        shaped((nc * 4,) + wo.shape),
-        shaped((ffn.shape[0], 4) + ffn.shape[1:]),
-        shaped((nc,) + cot.shape),
-    )
-    return call(functools.partial(gather_start_kernel, n, group_of), 1, (tokens, wq, wo, ffn, cot), outs, sems, "gather_start")
-
-
-def gather_ctx_kernel(columns, src, out, send, recv, local):
-    pos = Place(columns)
-    greet([pos.column(k) for k in range(1, columns)] + [pos.flip_b()])
-    s = Sends(send)
-    drive([gather_ctx(pos, src, out, s, recv, local)])
-    s.finish()
-
-
-def gather_rows(nc, src, collective_id):
-    n = nc // 2
-    return call(functools.partial(gather_ctx_kernel, n), collective_id, (src,), shaped((nc,) + src.shape), gather_ctx_sems(n), "gather_rows")
-
-
-def swap_kernel(nc, src, out, send, recv, local):
-    per = nc // GROUPS
-    ctx = lax.axis_index("ctx")
-    group, place = ctx // per, ctx % per
-    peer = lambda k: lax.rem(group + k, GROUPS)
-    device = lambda k: {"ctx": peer(k) * per + place}
-    greet([device(k) for k in range(1, GROUPS)])
-    own = pltpu.make_async_copy(src.at[group], out.at[group], local)
-    own.start()
-    copies = []
-    for k in range(1, GROUPS):
-        copies.append(remote(src.at[peer(k)], out.at[group], send.at[k], recv.at[k], device(k)))
-        copies[-1].start()
-    for k in range(1, GROUPS):
-        arrived(out.at[peer(GROUPS - k)], recv.at[k], device(k))
-    own.wait()
-    for copy in copies:
-        copy.wait_send()
-
-
-def swap(nc, src, collective_id):
-    return call(functools.partial(swap_kernel, nc), collective_id, (src,), shaped(src.shape), [DMA((GROUPS,)), DMA((GROUPS,)), DMA], "swap")
+def dot(a, b, dims):
+    return lax.dot_general(a, b, (dims, ((), ())), preferred_element_type=F32)
 
 
 def add(acc, *others):
@@ -319,38 +247,17 @@
     return [v(n), v(n), v(n), DMA((2 * n,)), DMA((2 * n,)), DMA((n,))]
 
 
-def scatter_ctx_kernel(columns, part, out, acc, from_b, from_col, send, recv, local):
-    pos = Place(columns)
-    greet([pos.column(k) for k in range(1, columns)] + [pos.flip_b()])
-    s = Sends(send)
-    drive([scatter_ctx(pos, part, out, acc, from_b, from_col, s, recv, local)])
-    s.finish()
-
-
-def scatter_rows(nc, part, collective_id):
-    n = nc // 2
-    return pl.pallas_call(
-        functools.partial(scatter_ctx_kernel, n),
-        out_shape=shaped(part.shape[1:], F32),
-        in_specs=[pl.BlockSpec(memory_space=pl.ANY)],
-        out_specs=pl.BlockSpec(memory_space=pltpu.VMEM),
-        scratch_shapes=scatter_ctx_scratch(n, part.shape[1:]),
-        compiler_params=pltpu.CompilerParams(collective_id=collective_id, has_side_effects=True, vmem_limit_bytes=60 << 20),
-        name="scatter_rows",
-    )(part)
-
-
 def scatter_fsdp(pos, part, out, acc, from_sib, from_y, sends, recv, local):
-    parts = part.shape[0]
+    parts = len(part)
     loads = []
     mine = [(1 - pos.y) * 2 + pos.c, pos.y * 2 + pos.c]
     his = [(1 - pos.y) * 2 + 1 - pos.c, pos.y * 2 + 1 - pos.c]
     for t in range(2):
         for p in range(parts):
             i = t * parts + p
-            loads.append(pltpu.make_async_copy(part.at[p, mine[t]], acc.at[i], local.at[i]))
+            loads.append(pltpu.make_async_copy(part[p].at[mine[t]], acc.at[i], local.at[i]))
             loads[-1].start()
-            sends.start(part.at[p, his[t]], from_sib.at[i], recv.at[i], pos.sibling())
+            sends.start(part[p].at[his[t]], from_sib.at[i], recv.at[i], pos.sibling())
     yield
     for p in range(parts):
         loads[p].wait()
@@ -434,6 +341,622 @@
     return [v(4 * n), v(4 * n), v(2 * n), v(n), v(n), DMA((8 * n,)), DMA((8 * n,)), DMA((4 * n,))]
 
 
+class Sizes:
+    def __init__(self, nc, nf, rows, width, experts, hidden, owned, padded, capacity, top, docs):
+        self.nc, self.nf, self.rows, self.width = nc, nf, rows, width
+        self.experts, self.hidden, self.owned, self.padded = experts, hidden, owned, padded
+        self.capacity, self.top, self.docs = capacity, top, docs
+        self.columns, self.per = nc // 2, nc // GROUPS
+        self.heads = width // HEAD_DIM // GROUPS
+        self.share = self.heads * HEAD_DIM
+        self.slot = nc * rows
+        self.all = nc * nf
+
+
+def scalars(sz, lengths):
+    sizes = [lengths[0, d] for d in range(sz.docs)]
+    ends, total = [], 0
+    for size in sizes:
+        total = total + size
+        ends.append(total)
+    return sizes, ends
+
+
+def starts(index, sizes, ends):
+    low = jnp.zeros_like(index)
+    for size, end in zip(sizes, ends):
+        low = low + jnp.where(index >= end, size, 0)
+    return low
+
+
+def iota(shape, dim):
+    return lax.broadcasted_iota(jnp.int32, shape, dim)
+
+
+def mean_square(x, width):
+    return jnp.sum(x * x, axis=-1, keepdims=True) * (1.0 / width)
+
+
+def turn(value, cosine, sine):
+    half = HEAD_DIM // 2
+    lower, upper = value[:half], value[half:]
+    return jnp.concatenate([lower * cosine - upper * sine, upper * cosine + lower * sine], axis=0)
+
+
+def head(h):
+    return slice(h * HEAD_DIM, (h + 1) * HEAD_DIM)
+
+
+def blk(index, rows):
+    return pl.ds(pl.multiple_of(index * rows, rows), rows)
+
+
+class Copies:
+    def __init__(self, sems):
+        self.sems, self.made = sems, []
+
+    def start(self, src, dst):
+        self.made.append(pltpu.make_async_copy(src, dst, self.sems.at[len(self.made)]))
+        self.made[-1].start()
+
+    def finish(self):
+        for copy in self.made:
+            copy.wait()
+
+
+def swap_send(sz, group, place, src, out, sends, recv, local, h):
+    @pl.when(h == group)
+    def _():
+        pltpu.make_async_copy(src.at[h], out.at[h], local).start()
+
+    copy = remote(src.at[h], out.at[group], sends.at[h], recv.at[group], {"ctx": h * sz.per + place})
+
+    @pl.when(h != group)
+    def _():
+        copy.start()
+
+
+def swap_wait(sz, group, place, src, out, sends, recv, local):
+    for h in range(GROUPS):
+        copy = remote(src.at[h], out.at[h], sends.at[h], recv.at[h], {"ctx": h * sz.per + place})
+
+        @pl.when(h == group)
+        def _():
+            pltpu.make_async_copy(src.at[h], out.at[h], local).wait()
+
+        @pl.when(h != group)
+        def _():
+            copy.wait_send()
+            copy.wait_recv()
+
+
+def forward_kernel(
+    sz, lengths, inverse, tokens, cot, routes_t, wq_send, wo_send, ffn_send,
+    g_all, mix_all, cw_all, ffn_all, normed_o, qt_o, kt_o, vt_o, prob_o, wt_o, wo_o, small_o, attn_o, resid_o, mixed_o, route_o, table_o,
+    x_all, wq_all, wo_all, wq, wt, wo, small, normed, qt, kt, vt, prob, o_send, attn, resid, mixed, route, cw, g_own, table,
+    *sems,
+):
+    pos = Place(sz.columns)
+    ctx = lax.axis_index("ctx")
+    group, place = ctx // sz.per, ctx % sz.per
+    rows, width, share = sz.rows, sz.width, sz.share
+    sizes, ends = scalars(sz, lengths)
+    group_of = lambda a: a // (sz.columns // GROUPS)
+
+    greet(all_partners(pos))
+    s = [Sends(sems[3 * i]) for i in range(7)]
+    r = lambda i: (sems[3 * i + 1], sems[3 * i + 2])
+    swap_sems = sems[21:24]
+    out = Copies(sems[24])
+
+    early = [
+        gather_ctx(pos, tokens, x_all, s[0], *r(0)),
+        gather_all(pos, wq_send, wq_all, s[1], *r(1), group_of=group_of),
+        gather_all(pos, wo_send, wo_all, s[2], *r(2)),
+    ]
+    ffn = gather_fsdp(pos, ffn_send, ffn_all, s[3], *r(3))
+    for stream in early:
+        next(stream)
+    next(ffn)
+
+    own_rows = ctx * rows + iota((rows, 1), 0)
+    live = own_rows < ends[-1]
+    g_own[...] = jnp.where(live, cot[...].astype(F32), 0.0).astype(BF)
+    index = iota((1, sz.slot), 1)
+    position = index - jnp.where(index < ends[-1], starts(index, sizes, ends), 0)
+    angles = position.astype(F32) * inverse[:, :1]
+    table[0] = jnp.cos(angles)
+    table[1] = jnp.sin(angles)
+    live_t = (ctx * rows + iota((1, rows), 1)) < ends[-1]
+    before = (iota((rows, rows), 0) < iota((rows, rows), 1)).astype(BF)
+    base = jnp.zeros((8, 1), F32)
+    kept = jnp.zeros((8, rows), F32)
+    for k in range(sz.top):
+        hot = ((iota((8, rows), 0) == routes_t[k : k + 1, :]) & live_t).astype(F32)
+        earlier = base + dot(hot.astype(BF), before, NN)
+        kept = kept + jnp.where(earlier < sz.capacity, hot, 0.0)
+        base = base + jnp.sum(hot, axis=1, keepdims=True)
+
+    drive(early)
+    cots = gather_ctx(pos, g_own, g_all, s[4], *r(4))
+    next(cots)
+
+    owned = sz.owned
+    for i in range(sz.all):
+        wq[i * owned : (i + 1) * owned, :] = wq_all[i, :owned, :].astype(F32)
+        wo[i * owned : (i + 1) * owned, :] = wo_all[i, :owned, :].astype(F32)
+    extra = wo_all[0, owned:, :].astype(F32)
+    for i in range(1, sz.all):
+        extra = extra + wo_all[i, owned:, :].astype(F32)
+    small[...] = extra[:8]
+    wt[...] = wq[...].T.astype(BF)
+    gain_a, gain_m = small[0:1, :], small[1:2, :]
+
+    for d in range(sz.nc):
+        x = x_all[d].astype(F32)
+        inv = lax.rsqrt(mean_square(x, width) + EPSILON)
+        normed[d] = (x * inv * gain_a).astype(BF)
+        part = slice(d * rows, (d + 1) * rows)
+        kv = dot(wt[share:, :], normed[d], NT)
+        for h in range(sz.heads):
+            kt[head(h), part] = turn(kv[head(h)], table[0, :, part], table[1, :, part]).astype(BF)
+        vt[:, part] = kv[share:].astype(BF)
+
+    next(ffn)
+    next(cots)
+    for h_ in reversed(range(GROUPS)):
+        d = h_ * sz.per + place
+        part = blk(d, rows)
+        qq = dot(wt[:share, :], normed[d], NT)
+        keys = (h_ + 1) * sz.per * rows
+        index = d * rows + iota((rows, 1), 0)
+        low = starts(index, sizes, ends)
+        key = iota((rows, keys), 1)
+        allowed = (key >= low) & (key <= index)
+        for h in range(sz.heads):
+            q = turn(qq[head(h)], table[0, :, part], table[1, :, part]).astype(BF) * BF(1.0 / math.sqrt(HEAD_DIM))
+            qt[h_, head(h), :] = q
+            score = jnp.where(allowed, dot(q, kt[head(h), :keys], TN), MASKED)
+            expo = jnp.exp(score - jnp.max(score, axis=1, keepdims=True))
+            p = (expo * (1.0 / jnp.sum(expo, axis=1, keepdims=True))).astype(BF)
+            prob[h_, h, :, :keys] = p
+            o_send[h_, head(h), :] = dot(vt[head(h), :keys], p, NT).astype(BF)
+        swap_send(sz, group, place, o_send, attn, *swap_sems, h_)
+    drive([ffn, cots])
+    swap_wait(sz, group, place, o_send, attn, *swap_sems)
+
+    attn_t = attn[...].reshape(width, rows)
+    wo_b = wo[...].astype(BF)
+    res = tokens[...].astype(F32) + dot(attn_t, wo_b, TN)
+    resid[...] = res
+    inv = lax.rsqrt(mean_square(res, width) + EPSILON)
+    mixed[...] = (res * inv * gain_m).astype(BF)
+    row = iota((8, rows), 0)
+    logits = dot(small[...].astype(BF), mixed[...], NT)
+    logits = jnp.concatenate([logits[2:], logits[:2]], axis=0)
+    logits = jnp.where(row < sz.experts, logits, MASKED)
+    expo = jnp.exp(logits - jnp.max(logits, axis=0, keepdims=True))
+    router_prob = expo * (1.0 / jnp.sum(expo, axis=0, keepdims=True))
+    route[0] = router_prob
+    route[1] = kept
+    weight = router_prob * kept
+    high = weight.astype(BF).astype(F32)
+    high_row = jnp.where(row == sz.experts, 1.0, high)
+    cw[...] = jnp.concatenate([high_row, weight - high], axis=0).astype(BF)
+    late = [
+        gather_ctx(pos, cw, cw_all, s[5], *r(5)),
+        gather_ctx(pos, mixed, mix_all, s[6], *r(6)),
+    ]
+    for stream in late:
+        next(stream)
+    wo[...] = wo_b.astype(F32)
+    for src, dst in zip(
+        (normed, qt, kt, vt, prob, wt, wo, small, attn, resid, mixed, route, table),
+        (normed_o, qt_o, kt_o, vt_o, prob_o, wt_o, wo_o, small_o, attn_o, resid_o, mixed_o, route_o, table_o),
+    ):
+        out.start(src, dst)
+    drive(late)
+    out.finish()
+    for x in s:
+        x.finish()
+
+
+def forward(sz, collective_id, lengths, inverse, tokens, cot, routes_t, wq_send, wo_send, ffn_send):
+    n, nc, rows, width = sz.columns, sz.nc, sz.rows, sz.width
+    saved = [
+        ((nc, rows, width), BF),
+        ((GROUPS, sz.share, rows), BF),
+        ((sz.share, sz.slot), BF),
+        ((sz.share, sz.slot), BF),
+        ((GROUPS, sz.heads, rows, sz.slot), BF),
+        ((3 * sz.share, width), BF),
+        ((width, width), F32),
+        ((8, width), F32),
+        ((GROUPS, sz.share, rows), BF),
+        ((rows, width), F32),
+        ((rows, width), BF),
+        ((2, 8, rows), F32),
+        ((2, HEAD_DIM // 2, sz.slot), F32),
+    ]
+    outs = [
+        shaped((nc, rows, width)),
+        shaped((nc, rows, width)),
+        shaped((nc, 16, rows)),
+        shaped((ffn_send.shape[0], sz.nf) + ffn_send.shape[1:]),
+    ] + [shaped(*x) for x in saved]
+    v = lambda shape, dtype=BF: pltpu.VMEM(tuple(shape), dtype)
+    normed, qt, kt, vt, prob, wt, wo, small, attn, resid, mixed, route, table = (v(*x) for x in saved)
+    scratch = [
+        v((nc, rows, width)), v((sz.all,) + wq_send.shape[1:]), v((sz.all,) + wo_send.shape),
+        v((width, 3 * sz.share), F32), wt, wo, small, normed, qt, kt, vt, prob, v((GROUPS, sz.share, rows)),
+        attn, resid, mixed, route, v((16, rows)), v((rows, width)), table,
+    ]
+    sems = gather_ctx_sems(n) + gather_all_sems(n) * 2 + gather_fsdp_sems(ffn_send.shape[0]) + gather_ctx_sems(n) * 3
+    sems += [DMA((GROUPS,)), DMA((GROUPS,)), DMA, DMA((len(saved),))]
+    hbm, vmem = pl.BlockSpec(memory_space=pl.ANY), pl.BlockSpec(memory_space=pltpu.VMEM)
+    return pl.pallas_call(
+        functools.partial(forward_kernel, sz),
+        out_shape=outs,
+        in_specs=[pl.BlockSpec(memory_space=pltpu.SMEM), vmem, vmem, vmem, vmem, hbm, hbm, hbm],
+        out_specs=[hbm] * len(outs),
+        scratch_shapes=scratch + sems,
+        compiler_params=pltpu.CompilerParams(collective_id=collective_id, has_side_effects=True, vmem_limit_bytes=62 << 20),
+        name="forward",
+    )(lengths, inverse, tokens, cot, routes_t, wq_send, wo_send, ffn_send)
+
+
+def ffn_kernel(chunk, mix, cw, g, wg, wu, wd, spread, gm, yy, pair, dg_w, du_w, dd_w, hw_all, dg_all, du_all, wg_all, wu_all, wd_all, pair_acc):
+    j = pl.program_id(0)
+    hb = wg.shape[0]
+    nc, rows, width = mix.shape
+    per = chunk // rows
+    at = blk(j, hb) if hb < wg_all.shape[0] else pl.ds(0, hb)
+    wg_all[at, :] = wg[...]
+    wu_all[at, :] = wu[...]
+    wd_all[at, :] = wd[...]
+    sp = spread[...]
+    for m in range(nc // per):
+        part = slice(m * per, (m + 1) * per)
+        x = mix[part].reshape(chunk, width)
+        gate = dot(x, wg[...], NT)
+        up = dot(x, wu[...], NT)
+        back = dot(g[part].reshape(chunk, width), wd[...], NT)
+        weight = jnp.concatenate([dot(cw[m * per + i], sp[:16], TN) for i in range(per)], axis=0)
+        sig = 1.0 / (1.0 + jnp.exp(-gate))
+        act = gate * sig
+        hid = act * up
+        ms = slice(m * chunk, (m + 1) * chunk)
+        product = dot(sp[16:], (hid * back).astype(BF), NT)
+
+        @pl.when(j == 0)
+        def _():
+            pair_acc[:, ms] = product
+
+        @pl.when(j > 0)
+        def _():
+            pair_acc[:, ms] = pair_acc[:, ms] + product
+
+        hw_all[ms, at] = (hid * weight).astype(BF)
+        back = back * weight
+        dg_all[ms, at] = (back * up * sig * (1.0 + gate * (1.0 - sig))).astype(BF)
+        du_all[ms, at] = (back * act).astype(BF)
+    xs = mix[...].reshape(nc * rows, width)
+    dg_w[...] = dot(dg_all[:, at], xs, TN).astype(BF)
+    du_w[...] = dot(du_all[:, at], xs, TN).astype(BF)
+    dd_w[...] = dot(hw_all[:, at], g[...].reshape(nc * rows, width), TN).astype(BF)
+
+    @pl.when(j == pl.num_programs(0) - 1)
+    def _():
+        for m in range(nc // per):
+            ms = slice(m * chunk, (m + 1) * chunk)
+            part = slice(m * per, (m + 1) * per)
+            total = dot(dg_all[ms], wg_all[...], NN) + dot(du_all[ms], wu_all[...], NN)
+            gm[part] = total.astype(BF).reshape(per, rows, width)
+            yy[part] = dot(hw_all[ms], wd_all[...], NN).astype(BF).reshape(per, rows, width)
+        for d in range(nc):
+            pair[d] = pair_acc[:, d * rows : (d + 1) * rows].astype(BF)
+
+
+def feed_forward(mix, cw, g, w, spread):
+    nc, rows, width = mix.shape
+    units = w.shape[1]
+    block = math.gcd(units, 256) if units % 256 == 0 else units
+    chunk = 1024
+    once = pl.Buffered(1)
+    full = lambda a: pl.BlockSpec(a.shape, lambda j: (0,) * a.ndim, pipeline_mode=once)
+    of = lambda p: pl.BlockSpec((None, block, width), lambda j: (p, j, 0))
+    kept = lambda *shape: pl.BlockSpec(shape, lambda j: (0,) * len(shape), pipeline_mode=once)
+    grads = pl.BlockSpec((block, width), lambda j: (j, 0))
+    t = nc * rows
+    flops = 2 * t * units * width * 9
+    return pl.pallas_call(
+        functools.partial(ffn_kernel, chunk),
+        grid=(units // block,),
+        out_shape=(shaped(mix.shape), shaped(mix.shape), shaped((nc, 16, rows))) + (shaped((units, width)),) * 3,
+        in_specs=[full(mix), full(cw), full(g), of(0), of(1), of(2), pl.BlockSpec((32, block), lambda j: (0, j))],
+        out_specs=(kept(nc, rows, width), kept(nc, rows, width), kept(nc, 16, rows), grads, grads, grads),
+        scratch_shapes=[pltpu.VMEM((t, units), BF)] * 3 + [pltpu.VMEM((units, width), BF)] * 3 + [pltpu.VMEM((16, t), F32)],
+        compiler_params=pltpu.CompilerParams(vmem_limit_bytes=62 << 20),
+        cost_estimate=pl.CostEstimate(flops=flops, bytes_accessed=w.size * 4 + mix.size * 8, transcendentals=t * units),
+        name="feed_forward",
+    )(mix, cw, g, w, w, w, spread)
+
+
+def backward_kernel(
+    sz, lengths, tokens, cot, gm_part, pair_part, y_part, dg_w, du_w, dd_w,
+    normed_i, qt_i, kt_i, vt_i, prob_i, wt_i, wo_i, small_i, attn_i, resid_i, mixed_i, route_i, table_i,
+    o_out, o_tokens, o_wq, o_wo, o_ffn,
+    normed, qt, kt, vt, prob, wt, wo, small, attn, resid, mixed, route, table,
+    do_send, do, dkt, dvt, dqt_b, dkvt_b, normed_q, gn_part, wq_part, wo_part, gm_own, gp_own, gn_own, y_own,
+    *scratch,
+):
+    pos = Place(sz.columns)
+    ctx = lax.axis_index("ctx")
+    group, place = ctx // sz.per, ctx % sz.per
+    rows, width, share, n = sz.rows, sz.width, sz.share, sz.columns
+    sizes, ends = scalars(sz, lengths)
+    c_gm, c_gp, c_y, c_gn = (scratch[6 * i : 6 * i + 6] for i in range(4))
+    a_wq, a_wo = scratch[24:32], scratch[32:40]
+    f_ffn = scratch[40:46]
+    swap_sems, loads = scratch[46:49], Copies(scratch[49])
+    greet(all_partners(pos))
+    s = {x: Sends(scratch[i]) for x, i in (("gm", 3), ("gp", 9), ("y", 15), ("gn", 21), ("wq", 29), ("wo", 37), ("ffn", 43))}
+
+    def ctx_sum(name, part, out, x):
+        return scatter_ctx(pos, part, out, *x[:3], s[name], *x[4:])
+
+    early = [ctx_sum("gp", pair_part, gp_own, c_gp), ctx_sum("gm", gm_part, gm_own, c_gm)]
+    ffn = scatter_fsdp(pos, (dg_w, du_w, dd_w), o_ffn, *f_ffn[:3], s["ffn"], *f_ffn[4:])
+    for stream in early:
+        next(stream)
+    next(ffn)
+    for src, dst in zip(
+        (normed_i, qt_i, kt_i, vt_i, prob_i, wt_i, wo_i, small_i, attn_i, resid_i, mixed_i, route_i, table_i),
+        (normed, qt, kt, vt, prob, wt, wo, small, attn, resid, mixed, route, table),
+    ):
+        loads.start(src, dst)
+    drive(early)
+    loads.finish()
+    ys = ctx_sum("y", y_part, y_own, c_y)
+    next(ys)
+
+    gain_a, gain_m = small[0:1, :], small[1:2, :]
+    live = (ctx * rows + iota((rows, 1), 0)) < ends[-1]
+    router_prob, kept = route[0], route[1]
+    grad_prob = gp_own[:8, :] * kept
+    grad_logits = router_prob * (grad_prob - jnp.sum(router_prob * grad_prob, axis=0, keepdims=True))
+    shifted = jnp.concatenate([jnp.zeros((2, rows), F32), grad_logits[:6]], axis=0).astype(BF)
+    grad_small = dot(shifted, mixed[...], NN)
+    grad_mixed = gm_own[...] + dot(shifted, small[...].astype(BF), TN)
+    res = resid[...]
+    inv = lax.rsqrt(mean_square(res, width) + EPSILON)
+    w = grad_mixed * gain_m
+    inner = jnp.sum(w * res, axis=-1, keepdims=True) * (1.0 / width)
+    grad_resid = jnp.where(live, cot[...].astype(F32), 0.0) + inv * w - res * inner * inv * inv * inv
+    grad_gain_m = jnp.sum(grad_mixed * res * inv, axis=0, keepdims=True)
+    grad_resid_b = grad_resid.astype(BF)
+    resid[...] = res
+    wo_b = wo[...].astype(BF)
+    grad_attn_t = dot(wo_b, grad_resid_b, NT).astype(BF)
+    for h_ in range(GROUPS):
+        do_send[h_] = grad_attn_t[h_ * share : (h_ + 1) * share]
+    for h_ in range(GROUPS):
+        swap_send(sz, group, place, do_send, do, *swap_sems, h_)
+    next(ffn)
+    next(ys)
+    grad_wo = dot(attn[...].reshape(width, rows), grad_resid_b, NN)
+    for i in range(sz.all):
+        wo_part[i, : sz.owned, :] = grad_wo[i * sz.owned : (i + 1) * sz.owned].astype(BF)
+    for h_ in range(GROUPS):
+        normed_q[h_] = normed[h_ * sz.per + place]
+    next(ffn)
+    swap_wait(sz, group, place, do_send, do, *swap_sems)
+
+    for h_ in reversed(range(GROUPS)):
+        keys = (h_ + 1) * sz.per * rows
+        part = blk(h_ * sz.per + place, rows)
+        for h in range(sz.heads):
+            d_o = do[h_, head(h), :]
+            p = prob[h_, h, :, :keys]
+            pf = p.astype(F32)
+            grad_p = dot(d_o, vt[head(h), :keys], TN)
+            delta = jnp.sum(pf * grad_p, axis=1, keepdims=True)
+            grad_s = (pf * (grad_p - delta)).astype(BF)
+            dq = dot(kt[head(h), :keys], grad_s, NT) * (1.0 / math.sqrt(HEAD_DIM))
+            dqt_b[h_, head(h), :] = turn(dq, table[0, :, part], -table[1, :, part]).astype(BF)
+            dk = dot(qt[h_, head(h), :], grad_s, NN)
+            dv = dot(d_o, p, NN)
+            if h_ == GROUPS - 1:
+                dkt[head(h), :] = dk
+                dvt[head(h), :] = dv
+            else:
+                dkt[head(h), :keys] = dkt[head(h), :keys] + dk
+                dvt[head(h), :keys] = dvt[head(h), :keys] + dv
+        if h_ == 2:
+            next(ffn)
+            next(ys)
+    for h in range(sz.heads):
+        dkvt_b[head(h), :] = turn(dkt[head(h), :], table[0], -table[1]).astype(BF)
+    dkvt_b[share:, :] = dvt[...].astype(BF)
+
+    grad_gain_a = jnp.zeros((1, width), F32)
+    for step in range(sz.per):
+        for h_ in range(GROUPS):
+            other = lax.rem(place + 1 + step, sz.per)
+            d = h_ * sz.per + other
+            gn = dot(dkvt_b[:, blk(d, rows)], wt[share:, :], TN)
+            if step == sz.per - 1:
+                gn = gn + dot(dqt_b[h_], wt[:share, :], TN)
+            grad_gain_a = grad_gain_a + jnp.sum(gn * normed[d].astype(F32), axis=0, keepdims=True)
+            gn_part[d] = gn.astype(BF)
+    grad_gain_a = grad_gain_a / gain_a
+    gns = ctx_sum("gn", gn_part, gn_own, c_gn)
+    next(gns)
+    row = iota((8, width), 0)
+    grad_small = jnp.where(row == 0, grad_gain_a, jnp.where(row == 1, grad_gain_m, grad_small))
+    pad = jnp.zeros((sz.padded - sz.owned - 8, width), F32)
+    grad_small = jnp.concatenate([grad_small, pad], axis=0).astype(BF) if pad.shape[0] else grad_small.astype(BF)
+    for i in range(sz.all):
+        wo_part[i, sz.owned :, :] = grad_small
+    wos = scatter_all(pos, wo_part, o_wo, *a_wo[:5], s["wo"], *a_wo[6:])
+    next(wos)
+    grad_q = dot(dqt_b[0], normed_q[0], NN)
+    for h_ in range(1, GROUPS):
+        grad_q = grad_q + dot(dqt_b[h_], normed_q[h_], NN)
+    grad_kv = dot(dkvt_b[...], normed[...].reshape(sz.slot, width), NN)
+    grad_w = jnp.concatenate([grad_q, grad_kv], axis=0).T
+    wq_part[...] = jnp.zeros_like(wq_part)
+    for i in range(sz.all):
+        wq_part[i, : sz.owned, :] = grad_w[i * sz.owned : (i + 1) * sz.owned].astype(BF)
+    wqs = scatter_all(pos, wq_part, o_wq, *a_wq[:5], s["wq"], *a_wq[6:], per_group=True)
+    drive([gns, wqs, wos, ffn, ys])
+
+    o_out[...] = jnp.where(live, res + y_own[...], 0.0).astype(BF)
+    x = tokens[...].astype(F32)
+    inv = lax.rsqrt(mean_square(x, width) + EPSILON)
+    w = gn_own[...] * gain_a
+    inner = jnp.sum(w * x, axis=-1, keepdims=True) * (1.0 / width)
+    o_tokens[...] = grad_resid + inv * w - x * inner * inv * inv * inv
+    for x in s.values():
+        x.finish()
+
+
+def backward(sz, collective_id, lengths, tokens, cot, gm_part, pair_part, y_part, dg_w, du_w, dd_w, saved):
+    n, rows, width = sz.columns, sz.rows, sz.width
+    part = (3, sz.nf, dg_w.shape[1], width)
+    outs = [
+        shaped((rows, width)),
+        shaped((rows, width), F32),
+        shaped((GROUPS, sz.padded, 3 * sz.share), F32),
+        shaped((sz.padded, width), F32),
+        shaped((3,) + dg_w.shape[1:], F32),
+    ]
+    v = lambda shape, dtype=BF: pltpu.VMEM(tuple(shape), dtype)
+    scratch = [v(x.shape, x.dtype) for x in saved] + [
+        v((GROUPS, sz.share, rows)), v((GROUPS, sz.share, rows)), v((sz.share, sz.slot), F32), v((sz.share, sz.slot), F32),
+        v((GROUPS, sz.share, rows)), v((2 * sz.share, sz.slot)), v((GROUPS, rows, width)), v((sz.nc, rows, width)),
+        v((sz.all, sz.padded, 3 * sz.share)), v((sz.all, sz.padded, width)),
+        v((rows, width), F32), v((16, rows), F32), v((rows, width), F32), v((rows, width), F32),
+    ]
+    scratch += scatter_ctx_scratch(n, (rows, width)) + scatter_ctx_scratch(n, (16, rows)) + scatter_ctx_scratch(n, (rows, width)) * 2
+    scratch += scatter_all_scratch(n, (sz.padded, 3 * sz.share)) + scatter_all_scratch(n, (sz.padded, width))
+    scratch += scatter_fsdp_scratch(3, dg_w.shape[1:])
+    scratch += [DMA((GROUPS,)), DMA((GROUPS,)), DMA, DMA((len(saved),))]
+    hbm, vmem = pl.BlockSpec(memory_space=pl.ANY), pl.BlockSpec(memory_space=pltpu.VMEM)
+    return pl.pallas_call(
+        functools.partial(backward_kernel, sz),
+        out_shape=outs,
+        in_specs=[pl.BlockSpec(memory_space=pltpu.SMEM), vmem, vmem] + [hbm] * (6 + len(saved)),
+        out_specs=[vmem] * len(outs),
+        scratch_shapes=scratch,
+        compiler_params=pltpu.CompilerParams(collective_id=collective_id, has_side_effects=True, vmem_limit_bytes=62 << 20),
+        name="backward",
+    )(lengths, tokens, cot, gm_part, pair_part, y_part, dg_w, du_w, dd_w, *saved)
+
+
+def gather_start_kernel(columns, group_of, tokens, wq, wo, ffn, cot, o_tokens, o_wq, o_wo, o_ffn, o_cot, *sems):
+    pos = Place(columns)
+    greet(all_partners(pos))
+    s = [Sends(sems[3 * i]) for i in range(5)]
+    r = lambda i: (sems[3 * i + 1], sems[3 * i + 2])
+    streams = [
+        gather_ctx(pos, tokens, o_tokens, s[0], *r(0)),
+        gather_all(pos, wq, o_wq, s[1], *r(1), group_of=group_of),
+        gather_all(pos, wo, o_wo, s[2], *r(2)),
+        gather_fsdp(pos, ffn, o_ffn, s[3], *r(3)),
+    ]
+    drive(streams)
+    drive([gather_ctx(pos, cot, o_cot, s[4], *r(4))])
+    for x in s:
+        x.finish()
+
+
+def call(kernel, collective_id, ins, outs, scratch, name, space=pl.ANY, in_space=None):
+    return pl.pallas_call(
+        kernel,
+        out_shape=outs,
+        in_specs=[pl.BlockSpec(memory_space=in_space or space)] * len(ins),
+        out_specs=jax.tree.map(lambda _: pl.BlockSpec(memory_space=space), outs),
+        scratch_shapes=scratch,
+        compiler_params=pltpu.CompilerParams(
+            collective_id=collective_id, has_side_effects=True, vmem_limit_bytes=60 << 20
+        ),
+        name=name,
+    )(*ins)
+
+
+def gather_start(nc, tokens, wq, wo, ffn, cot):
+    n = nc // 2
+    group_of = lambda a: a // (n // GROUPS)
+    sems = gather_ctx_sems(n) + gather_all_sems(n) * 2 + gather_fsdp_sems(ffn.shape[0]) + gather_ctx_sems(n)
+    outs = (
+        shaped((nc,) + tokens.shape),
+        shaped((nc * 4,) + wq.shape[1:]),
+        shaped((nc * 4,) + wo.shape),
+        shaped((ffn.shape[0], 4) + ffn.shape[1:]),
+        shaped((nc,) + cot.shape),
+    )
+    return call(functools.partial(gather_start_kernel, n, group_of), 1, (tokens, wq, wo, ffn, cot), outs, sems, "gather_start")
+
+
+def gather_ctx_kernel(columns, src, out, send, recv, local):
+    pos = Place(columns)
+    greet([pos.column(k) for k in range(1, columns)] + [pos.flip_b()])
+    s = Sends(send)
+    drive([gather_ctx(pos, src, out, s, recv, local)])
+    s.finish()
+
+
+def gather_rows(nc, src, collective_id):
+    n = nc // 2
+    return call(functools.partial(gather_ctx_kernel, n), collective_id, (src,), shaped((nc,) + src.shape), gather_ctx_sems(n), "gather_rows")
+
+
+def swap_kernel(nc, src, out, send, recv, local):
+    per = nc // GROUPS
+    ctx = lax.axis_index("ctx")
+    group, place = ctx // per, ctx % per
+    peer = lambda k: lax.rem(group + k, GROUPS)
+    device = lambda k: {"ctx": peer(k) * per + place}
+    greet([device(k) for k in range(1, GROUPS)])
+    own = pltpu.make_async_copy(src.at[group], out.at[group], local)
+    own.start()
+    copies = []
+    for k in range(1, GROUPS):
+        copies.append(remote(src.at[peer(k)], out.at[group], send.at[k], recv.at[k], device(k)))
+        copies[-1].start()
+    for k in range(1, GROUPS):
+        arrived(out.at[peer(GROUPS - k)], recv.at[k], device(k))
+    own.wait()
+    for copy in copies:
+        copy.wait_send()
+
+
+def swap(nc, src, collective_id):
+    return call(functools.partial(swap_kernel, nc), collective_id, (src,), shaped(src.shape), [DMA((GROUPS,)), DMA((GROUPS,)), DMA], "swap")
+
+
+def scatter_ctx_kernel(columns, part, out, acc, from_b, from_col, send, recv, local):
+    pos = Place(columns)
+    greet([pos.column(k) for k in range(1, columns)] + [pos.flip_b()])
+    s = Sends(send)
+    drive([scatter_ctx(pos, part, out, acc, from_b, from_col, s, recv, local)])
+    s.finish()
+
+
+def scatter_rows(nc, part, collective_id):
+    n = nc // 2
+    return pl.pallas_call(
+        functools.partial(scatter_ctx_kernel, n),
+        out_shape=shaped(part.shape[1:], F32),
+        in_specs=[pl.BlockSpec(memory_space=pl.ANY)],
+        out_specs=pl.BlockSpec(memory_space=pltpu.VMEM),
+        scratch_shapes=scatter_ctx_scratch(n, part.shape[1:]),
+        compiler_params=pltpu.CompilerParams(collective_id=collective_id, has_side_effects=True, vmem_limit_bytes=60 << 20),
+        name="scatter_rows",
+    )(part)
+
+
 def scatter_end_kernel(columns, gn, wq, wo, ffn, yy, o_gn, o_wq, o_wo, o_ffn, o_yy, *scratch):
     pos = Place(columns)
     greet(all_partners(pos))
@@ -442,7 +965,7 @@
     drive(
         [
             scatter_ctx(pos, gn, o_gn, *c1[:-3], s[0], *c1[-2:]),
-            scatter_fsdp(pos, ffn, o_ffn, *f1[:-3], s[3], *f1[-2:]),
+            scatter_fsdp(pos, [ffn.at[p] for p in range(ffn.shape[0])], o_ffn, *f1[:-3], s[3], *f1[-2:]),
             scatter_all(pos, wq, o_wq, *a1[:-3], s[1], *a1[-2:], per_group=True),
             scatter_all(pos, wo, o_wo, *a2[:-3], s[2], *a2[-2:]),
             scatter_ctx(pos, yy, o_yy, *c2[:-3], s[4], *c2[-2:]),
@@ -515,15 +1038,11 @@
     return kept
 
 
-def dot(a, b, dims):
-    return lax.dot_general(a, b, (dims, ((), ())), preferred_element_type=F32)
-
-
 def pad_rows(x, rows):
     return jnp.pad(x, [(0, rows - x.shape[0])] + [(0, 0)] * (x.ndim - 1))
 
 
-def body(tokens, doc_lengths, routes, cotangent, attn_gain, w_qkv, w_out, mlp_gain, router, expert_in, expert_out, shared_in, shared_out):
+def body_wide(tokens, doc_lengths, routes, cotangent, attn_gain, w_qkv, w_out, mlp_gain, router, expert_in, expert_out, shared_in, shared_out):
     nc = lax.axis_size("ctx")
     nf = lax.axis_size("fsdp")
     rows, width = tokens.shape[1:]
@@ -687,6 +1206,68 @@
     )
 
 
+def body(tokens, doc_lengths, routes, cotangent, attn_gain, w_qkv, w_out, mlp_gain, router, expert_in, expert_out, shared_in, shared_out):
+    nc, nf = lax.axis_size("ctx"), lax.axis_size("fsdp")
+    rows, width = tokens.shape[1:]
+    experts, hidden, top = expert_in.shape[1], expert_in.shape[0], routes.shape[2]
+    owned = w_out.shape[0]
+    if 2 * nc * rows * width > FUSED_BYTES:
+        return body_wide(
+            tokens, doc_lengths, routes, cotangent, attn_gain, w_qkv, w_out, mlp_gain, router, expert_in, expert_out, shared_in, shared_out
+        )
+    padded = -(-(owned + 8) // 16) * 16
+    sz = Sizes(nc, nf, rows, width, experts, hidden, owned, padded, 5 * top * rows // (4 * experts), top, doc_lengths.shape[1])
+    share = sz.share
+    device = lax.axis_index("ctx") * nf + lax.axis_index("fsdp")
+
+    wq_send = w_qkv.reshape(owned, 3, GROUPS, share).transpose(2, 0, 1, 3).reshape(GROUPS, owned, 3 * share)
+    wq_send = jnp.pad(wq_send, ((0, 0), (0, padded - owned), (0, 0)))
+    small = jnp.concatenate([attn_gain[None], mlp_gain[None], router.T], axis=0)
+    small = lax.dynamic_update_slice(jnp.zeros((padded - owned, width), BF), small, (0, device * owned))
+    wo_send = jnp.concatenate([w_out, small], axis=0)
+    gate_up = jnp.concatenate([expert_in.transpose(2, 1, 0, 3), shared_in.transpose(1, 0, 2)[:, None]], axis=1)
+    down = jnp.concatenate([expert_out.transpose(1, 0, 2), shared_out[None]], axis=0)
+    ffn_send = jnp.concatenate([gate_up, down[None]], axis=0).reshape(3, (experts + 1) * hidden, width)
+
+    half = HEAD_DIM // 2
+    inverse = (ROPE_BASE ** (-2.0 * np.arange(half) / HEAD_DIM)).astype(np.float32)
+    inverse = jnp.asarray(np.broadcast_to(inverse[:, None], (half, 128)))
+    routes_t = jnp.pad(routes[0].T, ((0, 8 - top), (0, 0)))
+
+    units = nf * (experts + 1) * hidden
+    of = np.arange(units) // hidden % (experts + 1)
+    spread = np.zeros((32, units), np.float32)
+    for e in range(experts + 1):
+        spread[e] = of == e
+    for e in range(experts):
+        spread[8 + e] = of == e
+        spread[16 + e] = of == e
+
+    g_all, mix_all, cw_all, ffn_all, *saved = forward(sz, 1, doc_lengths, inverse, tokens[0], cotangent[0], routes_t, wq_send, wo_send, ffn_send)
+    gm_part, y_part, pair_part, dg_w, du_w, dd_w = feed_forward(mix_all, cw_all, g_all, ffn_all.reshape(3, units, width), jnp.asarray(spread, BF))
+    by_owner = lambda v: v.reshape(nf, (experts + 1) * hidden, width)
+    layer_out, grad_tokens, wq_own, wo_own, ffn_own = backward(
+        sz, 2, doc_lengths, tokens[0], cotangent[0], gm_part, pair_part, y_part, by_owner(dg_w), by_owner(du_w), by_owner(dd_w), saved
+    )
+
+    grad_w_qkv = wq_own[:, :owned].reshape(GROUPS, owned, 3, share).transpose(1, 2, 0, 3).reshape(owned, 3 * width)
+    small = lax.dynamic_slice(wo_own[owned:], (0, device * owned), (2 + experts, owned))
+    out = ffn_own.reshape(3, experts + 1, hidden, width)
+    return (
+        layer_out[None],
+        grad_tokens[None],
+        small[0],
+        grad_w_qkv,
+        wo_own[:owned],
+        small[1],
+        small[2:].T,
+        out[:2, :experts].transpose(2, 1, 0, 3),
+        out[2, :experts].transpose(1, 0, 2),
+        out[:2, experts].transpose(1, 0, 2),
+        out[2, experts],
+    )
+
+
 def solution(mesh):
     rows = P("fsdp", "ctx", None)
     flat = ("ctx", "fsdp")

time: 462 us -> 253 us (0.55)
  matrix products: 90.5 us -> 0 us
  local copies, waits for them, and re-layouts: 82.3 us -> 22.6 us
  other arithmetic: 43.9 us -> 5.04 us
  Pallas kernels: 239 us -> 224 us
    dot_general x29 -> x0, matrix products: 84.3 us -> none  [the longest x22 58.5 us: dot(): return lax.dot_general(a, b, (dims, ((), ())), preferred_element_type=F32)]
    dot_general x5 -> x0, local copies, waits for them, and re-layouts: 15.4 us -> none  [dot(): return lax.dot_general(a, b, (dims, ((), ())), preferred_element_type=F32)]
    pallas_call x6 -> x3, Pallas kernels: 239 us -> 224 us  [the longest x1 110 us: forward(): pl.pallas_call(functools.partial(forward_kernel, sz), out_shape=outs, in_...]
    slice x8 -> x1, local copies, waits for them, and re-layouts: 15.1 us -> 0.89 us  [body(): wo_own[owned:]]
    convert_element_type x15 -> x0, other arithmetic: 10.7 us -> none  [the longest x1 3.6 us: body(): gn_part = gn.reshape(nc, rows, width).astype(BF)]
    another operation x2 -> x1, local copies, waits for them, and re-layouts: 8.84 us -> 0.68 us  [body(): unit_weight = jnp.tile(jnp.repeat(unit_weight, hidden, axis=1), (1, nf))]
    reduce_sum x9 -> x0, other arithmetic: 6.7 us -> none  [the longest x1 2.88 us: body(): (hid * back).reshape(slot, nf, experts + 1, hidden).sum(axis=(1, 3))]
    sub x1 -> x0, matrix products: 6.27 us -> none  [body(): expo = jnp.exp(scores - jnp.max(scores, axis=-1, keepdims=True))]
where the time goes in v2:
time: 253 us
  Pallas kernels  224 us (89%)
  local copies, waits for them, and re-layouts  22.6 us (9%)
  other arithmetic  5.04 us (2%)
    pallas_call x1, Pallas kernels, forward(): pl.pallas_call(functools.partial(forward_kernel, sz), out_shape=outs, in_...  110 us
    pallas_call x1, Pallas kernels, backward(): pl.pallas_call(functools.partial(backward_kernel, sz), out_shape=outs, in...  85 us
    pallas_call x1, Pallas kernels, feed_forward(): pl.pallas_call(functools.partial(ffn_kernel, chunk), grid=(units // block...  29.7 us
    unnamed x19, local copies, waits for them, and re-layouts  6.25 us

profile of v2, /device:TPU:0, one launch (start us, length us, event | category | flops | bytes accessed | tf_op | source)
XLA Modules:
  0.0 252.7 jit_solution(1139581036824358429)
XLA Ops:
  0.7 0.8 pad_maximum_fusion.4
  1.4 1.3 pad.8.routes_t
  2.7 0.2 dynamic_update_slice.3
  2.9 1.4 pad_maximum_fusion.3.wo_send
  4.3 1.1 reshape.53
  5.5 0.2 reshape.54
  5.7 0.7 pad.9.wq_send
  6.3 1.0 copy.46
  7.4 0.4 pad_maximum_fusion.2
  7.8 0.1 copy.47
  7.9 1.3 pad_maximum_fusion.1
  9.2 0.1 copy.45
  9.3 1.2 pad_maximum_fusion.ffn_send
  10.6 0.7 jit_solution_.3.inverse
  11.2 109.5 %forward.1 = (bf16[8,128,768]{2,1,0:T(8,128)(2,1)}, bf16[8,128,768]{2,1,0:T(8,128)(2,1)}, bf16[8,16,128]{2,1,0:T(8,128)(2,1)}, bf16[3,4,320,768]{3,2,1,0:T(8,128...) custom-call(s32[1,4]{1,0:T(1,128)} %lengths.3, ...), custom_call_target="tpu_custom_call" | custom-call | tf_op jit(solution)/shard_map/forward/pallas_call | solution.py:597
  120.8 29.7 %feed_forward.1 = (bf16[8,128,768]{2,1,0:T(8,128)(2,1)}, bf16[8,128,768]{2,1,0:T(8,128)(2,1)}, bf16[8,16,128]{2,1,0:T(8,128)(2,1)}, bf16[1280,768]{1,0:T(8,128)(...) custom-call(bf16[8,128,768]{2,1,0:T(8,128)(2,1)} %get-tuple-element.39.mix, ...), custom_call_target="tpu_custom_call" | custom-call | flops 18119393280 | bytes 18087936 | tf_op jit(solution)/shard_map/feed_forward/pallas_call | solution.py:672
  150.5 85.0 %backward.1 = (bf16[128,768]{1,0:T(8,128)(2,1)}, f32[128,768]{1,0:T(8,128)}, f32[4,32,576]{2,1,0:T(8,128)}, f32[32,768]{1,0:T(8,128)}, f32[3,320,768]{2,1,0:T(8,128)}) custom-call(s32[1,4]{1,0:T(1,128)} %lengths.3, bf16[128,768]{1,0:T(8,128)(2,1)} %bitcast.58, bf16[128,768]{1,0:T(8,128)(2,1)} %bitcast.60, bf16[8,128,768]{2,1,0:T(8,128)(2,1)} %get-tuple-element.43.gm_part, ...), custom_call_target="tpu_custom_call" | custom-call | tf_op jit(solution)/shard_map/backward/pallas_call | solution.py:846
  235.5 0.9 slice.30
  236.4 1.5 slice.33
  238.0 0.5 slice_bitcast_fusion.5
  238.5 0.6 slice_bitcast_fusion.4
  239.1 1.6 slice_bitcast_fusion.3
  240.7 1.7 slice.32
  242.4 1.1 reshape.59
  243.5 0.9 copy.48
  244.4 1.8 reshape.60
  246.3 1.1 copy.51
  247.4 0.1 slice_bitcast_fusion
  247.5 2.4 copy.49
  249.9 1.4 copy.50
  251.3 0.7 copy.57
  252.0 0.7 copy.58
  (19 shorter events, 0.3 us)
Async XLA Ops:
  0.6 6.7 %copy-start.3 = (bf16[64,4,768]{2,1,0:T(4,128)(2,1)S(1)}, bf16[64,4,768]{2,1,0:T(4,128)(2,1)}, u32[]{:S(2)}) copy-start(bf16[64,4,768]{2,1,0:T(4,128)(2,1)} %param.25) | copy-start | bytes 1179652
  5.6 2.3 copy-start.1
  5.6 2.3 copy-start.5
  9.3 1.3 copy-start.6
  235.5 10.7 %copy-start = (f32[3,320,768]{2,1,0:T(8,128)S(1)}, f32[3,320,768]{2,1,0:T(8,128)}, u32[]{:S(2)}) copy-start(f32[3,320,768]{2,1,0:T(8,128)} %get-tuple-element.66) | copy-start | bytes 8847364
  247.5 3.8 %copy-start.4 = (bf16[128,768]{1,0:T(8,128)(2,1)S(1)}, bf16[128,768]{1,0:T(8,128)(2,1)}, u32[]{:S(2)}) copy-start(bf16[128,768]{1,0:T(8,128)(2,1)} %get-tuple-element.62) | copy-start | bytes 589828
  249.9 2.1 copy-start.2

commit v3 on v2

--- a/solution.py
+++ b/solution.py
@@ -23,14 +23,14 @@
 
 
 class Place:
-    def __init__(self, columns):
+    def __init__(self, columns, balanced=True):
         ctx, fsdp = lax.axis_index("ctx"), lax.axis_index("fsdp")
         self.columns = columns
         self.a, self.b = ctx // 2, ctx % 2
         self.y, self.c = fsdp // 2, fsdp % 2
         flip_b = (1 - self.b, self.y)
         flip_y = (self.b, 1 - self.y)
-        core = self.c == 0
+        core = (self.c == 0) if balanced else (self.c >= 0)
         self.first = tuple(jnp.where(core, p, q) for p, q in zip(flip_b, flip_y))
         self.second = tuple(jnp.where(core, q, p) for p, q in zip(flip_b, flip_y))
         self.plane = [(self.b, self.y), self.first, self.second, (1 - self.b, 1 - self.y)]
@@ -122,23 +122,28 @@
 
 def gather_fsdp(pos, src, out, sends, recv, local):
     parts = src.shape[0]
+    if len(out.shape) == 3:
+        out = [out.at[p] for p in range(parts)]
+        at = lambda p, f: out[p].at[pl.ds(pl.multiple_of(f * src.shape[1], src.shape[1]), src.shape[1])]
+    else:
+        at = lambda p, f: out.at[p, f]
     me = pos.y * 2 + pos.c
     other = (1 - pos.y) * 2 + pos.c
     own = []
     for p in range(parts):
-        own.append(pltpu.make_async_copy(src.at[p], out.at[p, me], local.at[p]))
+        own.append(pltpu.make_async_copy(src.at[p], at(p, me), local.at[p]))
         own[-1].start()
-        sends.start(src.at[p], out.at[p, me], recv.at[p], pos.flip_y())
+        sends.start(src.at[p], at(p, me), recv.at[p], pos.flip_y())
     for p in range(parts):
-        sends.start(src.at[p], out.at[p, me], recv.at[parts + p], pos.sibling())
+        sends.start(src.at[p], at(p, me), recv.at[parts + p], pos.sibling())
     yield
     for p in range(parts):
-        arrived(out.at[p, other], recv.at[p], pos.flip_y())
-        sends.start(out.at[p, other], out.at[p, other], recv.at[2 * parts + p], pos.sibling())
+        arrived(at(p, other), recv.at[p], pos.flip_y())
+        sends.start(at(p, other), at(p, other), recv.at[2 * parts + p], pos.sibling())
         yield
     for p in range(parts):
-        arrived(out.at[p, pos.y * 2 + 1 - pos.c], recv.at[parts + p], pos.sibling())
-        arrived(out.at[p, (1 - pos.y) * 2 + 1 - pos.c], recv.at[2 * parts + p], pos.sibling())
+        arrived(at(p, pos.y * 2 + 1 - pos.c), recv.at[parts + p], pos.sibling())
+        arrived(at(p, (1 - pos.y) * 2 + 1 - pos.c), recv.at[2 * parts + p], pos.sibling())
         own[p].wait()
 
 
@@ -341,6 +346,218 @@
     return [v(4 * n), v(4 * n), v(2 * n), v(n), v(n), DMA((8 * n,)), DMA((8 * n,)), DMA((4 * n,))]
 
 
+class GatherLine:
+    def __init__(self, pos, bufs, send, recv, parts=2):
+        self.pos, self.bufs, self.send, self.recv, self.parts = pos, bufs, send, recv, parts
+        self.made = []
+
+    def cut(self, ref, p):
+        rows = ref.shape[0] // self.parts
+        return ref.at[pl.ds(p * rows, rows)]
+
+    def copy(self, i, p, src, a, kind, device):
+        out = self.bufs[i][1]
+        n = self.pos.columns
+        dst = self.cut(out.at[2 * a + self.pos.b], p)
+        at = ((i * 2 + kind) * n + a) * self.parts + p
+        made = remote(dst if src is None else self.cut(src, p), dst, self.send.at[len(self.made)], self.recv.at[at], device)
+        return made
+
+    def go(self, i, p, src, a, kind, device, when=None):
+        made = self.copy(i, p, src, a, kind, device)
+        self.made.append((made, when))
+        if when is None:
+            made.start()
+        else:
+            pl.when(when)(made.start)
+
+    def start(self):
+        pos, n = self.pos, self.pos.columns
+        up, down = pos.device(a=jnp.minimum(pos.a + 1, n - 1)), pos.device(a=jnp.maximum(pos.a - 1, 0))
+        self.up, self.down = up, down
+        for p in range(self.parts):
+            for i, (src, _) in enumerate(self.bufs):
+                self.go(i, p, src, pos.a, 0, up, pos.a < n - 1)
+                self.go(i, p, src, pos.a, 0, down, pos.a > 0)
+                self.go(i, p, src, pos.a, 1, pos.flip_b())
+
+    def here(self, i, p, a, kind, device):
+        b = self.pos.b if kind == 0 else 1 - self.pos.b
+        out = self.bufs[i][1]
+        at = ((i * 2 + kind) * self.pos.columns + a) * self.parts + p
+        arrived(self.cut(out.at[2 * a + b], p), self.recv.at[at], device)
+
+    def relay(self, d):
+        pos, n = self.pos, self.pos.columns
+        for p in range(self.parts):
+            for sign, device, end in ((-1, self.up, pos.a < n - 1), (1, self.down, pos.a > 0)):
+                a = pos.a + sign * d
+                there = (a >= 0) & (a < n)
+                a = jnp.clip(a, 0, n - 1)
+                for i in range(len(self.bufs)):
+                    pl.when(there)(functools.partial(self.here, i, p, a, 0, device))
+                    if d < n - 1:
+                        self.go(i, p, None, a, 0, device, there & end)
+                    self.go(i, p, None, a, 1, pos.flip_b(), there)
+
+    def across(self, a):
+        for p in range(self.parts):
+            for i in range(len(self.bufs)):
+                self.here(i, p, a, 1, self.pos.flip_b())
+
+    def finish(self):
+        for made, when in self.made:
+            if when is None:
+                made.wait_send()
+            else:
+                pl.when(when)(made.wait_send)
+
+
+def gather_line_sems(n, bufs=1, parts=2):
+    return [DMA((parts * bufs * (3 + 4 * (n - 1)),)), DMA((2 * bufs * n * parts,))]
+
+
+def gather_tree(pos, src, out, sends, recv, local, group_of=None):
+    n = pos.columns
+    b, y = pos.plane[0]
+    part = (lambda a: src) if group_of is None else (lambda a: src.at[group_of(a)])
+    first, second, sibling = pos.device(plane=pos.first), pos.device(plane=pos.second), pos.sibling()
+    mine = out.at[pos.c, b, y, pos.a]
+    own = pltpu.make_async_copy(part(pos.a), mine, local)
+    own.start()
+    for k in range(1, n):
+        sends.start(part(pos.at(k)), mine, recv.at[k], pos.column(k))
+    yield
+    for k in range(1, n):
+        arrived(out.at[pos.c, b, y, pos.at(n - k)], recv.at[k], first)
+    own.wait()
+    column = out.at[pos.c, b, y]
+    sends.start(column, column, recv.at[n], first)
+    sends.start(column, column, recv.at[n + 1], second)
+    yield
+    column = out.at[pos.c, pos.first[0], pos.first[1]]
+    arrived(column, recv.at[n], first)
+    sends.start(column, column, recv.at[n + 2], second)
+    yield
+    for r in range(2):
+        arrived(out.at[pos.c, pos.plane[2 + r][0], pos.plane[2 + r][1]], recv.at[n + 1 + r], second)
+    sends.start(out.at[pos.c], out.at[pos.c], recv.at[n + 3], sibling)
+    yield
+    arrived(out.at[1 - pos.c], recv.at[n + 3], sibling)
+
+
+def gather_tree_sems(n):
+    return [DMA((n + 4,)), DMA((n + 4,)), DMA]
+
+
+def scatter_tree(pos, part, out, from_sib, from_2, from_1, from_col, sends, recv, per_group=False):
+    n = pos.columns
+    c = pos.c
+    first, second, sibling = pos.device(plane=pos.first), pos.device(plane=pos.second), pos.sibling()
+    sends.start(part.at[1 - c], from_sib, recv.at[0], sibling)
+    yield
+    arrived(from_sib, recv.at[0], sibling)
+    at = lambda r: (c, pos.plane[r][0], pos.plane[r][1])
+    sib = lambda r: (pos.plane[r][0], pos.plane[r][1])
+    for r in (3, 2):
+        part[at(r)] = (part[at(r)].astype(F32) + from_sib[sib(r)].astype(F32)).astype(BF)
+        sends.start(part.at[at(r)], from_2.at[r - 2], recv.at[1 + r - 2], second)
+    yield
+    arrived(from_2.at[1], recv.at[2], second)
+    part[at(1)] = (part[at(1)].astype(F32) + from_sib[sib(1)].astype(F32) + from_2[1].astype(F32)).astype(BF)
+    sends.start(part.at[at(1)], from_1, recv.at[3], first)
+    arrived(from_2.at[0], recv.at[1], second)
+    yield
+    arrived(from_1, recv.at[3], first)
+    total = part[at(0)].astype(F32) + from_sib[sib(0)].astype(F32) + from_2[0].astype(F32) + from_1[...].astype(F32)
+    part[at(0)] = total.astype(BF)
+    mine = part.at[at(0)]
+    for k in range(1, n):
+        sends.start(mine.at[pos.at(k)], from_col.at[k], recv.at[3 + k], pos.column(k))
+    yield
+    total = mine[pos.a].astype(F32)
+    if per_group:
+        out[pos.a // (n // GROUPS)] = total
+    for k in range(1, n):
+        arrived(from_col.at[k], recv.at[3 + k], pos.column(k))
+        if per_group:
+            out[pos.at(n - k) // (n // GROUPS)] = from_col[k].astype(F32)
+        else:
+            total = total + from_col[k].astype(F32)
+    if not per_group:
+        out[...] = total
+
+
+def scatter_tree_scratch(n, shape):
+    v = lambda *lead: pltpu.VMEM(lead + tuple(shape), BF)
+    return [v(2, 2, n), v(2, n), v(n), v(n), DMA((n + 4,)), DMA((n + 4,))]
+
+
+class SumCtx:
+    def __init__(self, pos, parts, send, recv):
+        self.pos, self.parts, self.send, self.recv = pos, parts, send, recv
+
+    def copies(self, a, way):
+        pos, n = self.pos, self.pos.columns
+        for i, (part, from_b, from_col) in enumerate(self.parts):
+            base = 2 * n * i
+            if way == "b":
+                yield remote(part.at[2 * a + 1 - pos.b], from_b.at[a], self.send.at[base + a], self.recv.at[base + a], pos.flip_b())
+            else:
+                device = pos.device(a=a)
+                yield remote(part.at[2 * a + pos.b], from_col.at[pos.a], self.send.at[base + n + a], self.recv.at[base + n + pos.a], device)
+
+    def push(self, a):
+        for copy in self.copies(a, "b"):
+            copy.start()
+
+    def pass_on(self, a, other=None):
+        pos = self.pos
+        for copy, (part, from_b, _) in zip(self.copies(a, "b"), self.parts):
+            copy.wait_recv()
+
+        def send():
+            for copy, (part, from_b, _) in zip(self.copies(a, "column"), self.parts):
+                at = 2 * a + pos.b
+                part[at] = (part[at].astype(F32) + from_b[a].astype(F32)).astype(BF)
+                copy.start()
+
+        if other is None:
+            pl.when(a != pos.a)(send)
+        elif other:
+            send()
+
+    def total(self):
+        pos, n = self.pos, self.pos.columns
+        sums = []
+        for i, (part, from_b, from_col) in enumerate(self.parts):
+            total = part[2 * pos.a + pos.b].astype(F32) + from_b[pos.a].astype(F32)
+            for k in range(1, n):
+                a = pos.at(k)
+                sem = self.recv.at[2 * n * i + n + a]
+                arrived(from_col.at[a], sem, pos.column(k))
+                total = total + from_col[a].astype(F32)
+            sums.append(total)
+        return sums
+
+    def finish(self):
+        pos, n = self.pos, self.pos.columns
+        for a in range(n):
+            for copy in self.copies(a, "b"):
+                copy.wait_send()
+        for k in range(1, n):
+            for copy in self.copies(pos.at(k), "column"):
+                copy.wait_send()
+
+
+def sum_ctx_scratch(n, *shapes):
+    v = lambda shape: pltpu.VMEM((n,) + tuple(shape), BF)
+    out = []
+    for shape in shapes:
+        out += [v(shape), v(shape)]
+    return out + [DMA((2 * n * len(shapes),)), DMA((2 * n * len(shapes),))]
+
+
 class Sizes:
     def __init__(self, nc, nf, rows, width, experts, hidden, owned, padded, capacity, top, docs):
         self.nc, self.nf, self.rows, self.width = nc, nf, rows, width
@@ -431,79 +648,93 @@
 
 
 def forward_kernel(
-    sz, lengths, inverse, tokens, cot, routes_t, wq_send, wo_send, ffn_send,
-    g_all, mix_all, cw_all, ffn_all, normed_o, qt_o, kt_o, vt_o, prob_o, wt_o, wo_o, small_o, attn_o, resid_o, mixed_o, route_o, table_o,
-    x_all, wq_all, wo_all, wq, wt, wo, small, normed, qt, kt, vt, prob, o_send, attn, resid, mixed, route, cw, g_own, table,
+    sz, lengths, tokens, cot, routes, small_own, spread, wq_send, wo_own, ffn_send,
+    gm_o, gp_o, y_o, dw_o, normed_o, qt_o, kt_o, vt_o, prob_o, wt_o, wo_o, small_o, attn_o, resid_o, mixed_o, route_o, table_o,
+    x_all, wq_all, wo_all, wo_send, wq, wt, wo, small, normed, qt, kt, vt, prob, o_send, attn, resid, route, g_own, table,
+    g_all, mix_all, cw_all, ffn_w, hw, dg, du, gm_part, gp_part, y_part, dw,
     *sems,
 ):
-    pos = Place(sz.columns)
+    pos, pos_b = Place(sz.columns), Place(sz.columns, balanced=False)
     ctx = lax.axis_index("ctx")
     group, place = ctx // sz.per, ctx % sz.per
-    rows, width, share = sz.rows, sz.width, sz.share
+    rows, width, share, n = sz.rows, sz.width, sz.share, sz.columns
     sizes, ends = scalars(sz, lengths)
-    group_of = lambda a: a // (sz.columns // GROUPS)
+    group_of = lambda a: a // (n // GROUPS)
+
+    owned = sz.owned
+    me = ctx * sz.nf + lax.axis_index("fsdp")
+    place_of = (iota((owned, width), 1) == me * owned + iota((owned, width), 0)).astype(BF)
+    wo_send[:owned, :] = wo_own[...]
+    wo_send[owned:, :] = dot(small_own[...], place_of, NN).astype(BF)
 
     greet(all_partners(pos))
-    s = [Sends(sems[3 * i]) for i in range(7)]
+    s = [Sends(sems[3 * i]) for i in range(3)]
     r = lambda i: (sems[3 * i + 1], sems[3 * i + 2])
-    swap_sems = sems[21:24]
-    out = Copies(sems[24])
-
-    early = [
-        gather_ctx(pos, tokens, x_all, s[0], *r(0)),
-        gather_all(pos, wq_send, wq_all, s[1], *r(1), group_of=group_of),
-        gather_all(pos, wo_send, wo_all, s[2], *r(2)),
-    ]
-    ffn = gather_fsdp(pos, ffn_send, ffn_all, s[3], *r(3))
-    for stream in early:
-        next(stream)
+    swap_sems, out = sems[9:12], Copies(sems[12])
+    gm_sum = SumCtx(pos, [(gm_part, sems[13], sems[14]), (gp_part, sems[15], sems[16])], sems[17], sems[18])
+    toks = GatherLine(pos, [(tokens, x_all)], sems[19], sems[20])
+    cots = GatherLine(pos, [(None, g_all)], sems[21], sems[22])
+    mixes = GatherLine(pos, [(None, mix_all)], sems[23], sems[24])
+    weights = GatherLine(pos, [(None, cw_all)], sems[25], sems[26], parts=1)
+
+    wqs = gather_tree(pos_b, wq_send, wq_all, s[0], *r(0), group_of=group_of)
+    wos = gather_tree(pos_b, wo_send, wo_all, s[1], *r(1))
+    ffn = gather_fsdp(pos, ffn_send, ffn_w, s[2], *r(2))
+    next(wqs)
+    toks.start()
     next(ffn)
+    x_all[ctx] = tokens[...]
 
     own_rows = ctx * rows + iota((rows, 1), 0)
     live = own_rows < ends[-1]
-    g_own[...] = jnp.where(live, cot[...].astype(F32), 0.0).astype(BF)
+    g_all[ctx] = jnp.where(live, cot[...].astype(F32), 0.0).astype(BF)
     index = iota((1, sz.slot), 1)
     position = index - jnp.where(index < ends[-1], starts(index, sizes, ends), 0)
-    angles = position.astype(F32) * inverse[:, :1]
+    half = HEAD_DIM // 2
+    inverse = jnp.exp(iota((half, 1), 0).astype(F32) * (-2.0 * math.log(ROPE_BASE) / HEAD_DIM))
+    angles = position.astype(F32) * inverse
     table[0] = jnp.cos(angles)
     table[1] = jnp.sin(angles)
-    live_t = (ctx * rows + iota((1, rows), 1)) < ends[-1]
     before = (iota((rows, rows), 0) < iota((rows, rows), 1)).astype(BF)
+    same = (iota((rows, rows), 0) == iota((rows, rows), 1)).astype(BF)
     base = jnp.zeros((8, 1), F32)
     kept = jnp.zeros((8, rows), F32)
     for k in range(sz.top):
-        hot = ((iota((8, rows), 0) == routes_t[k : k + 1, :]) & live_t).astype(F32)
-        earlier = base + dot(hot.astype(BF), before, NN)
+        hot = ((iota((rows, 8), 1) == routes[:, k : k + 1]) & live).astype(BF)
+        earlier = base + dot(hot, before, TN)
+        hot = dot(hot, same, TN)
         kept = kept + jnp.where(earlier < sz.capacity, hot, 0.0)
         base = base + jnp.sum(hot, axis=1, keepdims=True)
-
-    drive(early)
-    cots = gather_ctx(pos, g_own, g_all, s[4], *r(4))
-    next(cots)
-
-    owned = sz.owned
+    route[1] = kept
+    step(wqs)
+    for k in range(1, n):
+        toks.relay(k)
+        step(wqs)
+    cots.start()
+    step(wos)
+    for k in range(n):
+        toks.across(k)
+    drive([wqs])
+
+    def spot(i):
+        a_b, y_c = divmod(i, sz.nf)
+        return y_c % 2, a_b % 2, y_c // 2, a_b // 2
+
     for i in range(sz.all):
-        wq[i * owned : (i + 1) * owned, :] = wq_all[i, :owned, :].astype(F32)
-        wo[i * owned : (i + 1) * owned, :] = wo_all[i, :owned, :].astype(F32)
-    extra = wo_all[0, owned:, :].astype(F32)
-    for i in range(1, sz.all):
-        extra = extra + wo_all[i, owned:, :].astype(F32)
-    small[...] = extra[:8]
+        wq[i * owned : (i + 1) * owned, :] = wq_all[spot(i)][:owned, :].astype(F32)
     wt[...] = wq[...].T.astype(BF)
-    gain_a, gain_m = small[0:1, :], small[1:2, :]
-
     for d in range(sz.nc):
         x = x_all[d].astype(F32)
         inv = lax.rsqrt(mean_square(x, width) + EPSILON)
-        normed[d] = (x * inv * gain_a).astype(BF)
+        normed[d] = (x * inv).astype(BF)
         part = slice(d * rows, (d + 1) * rows)
         kv = dot(wt[share:, :], normed[d], NT)
         for h in range(sz.heads):
             kt[head(h), part] = turn(kv[head(h)], table[0, :, part], table[1, :, part]).astype(BF)
         vt[:, part] = kv[share:].astype(BF)
-
-    next(ffn)
-    next(cots)
+    step(wos, ffn)
+    cots.relay(1)
+
     for h_ in reversed(range(GROUPS)):
         d = h_ * sz.per + place
         part = blk(d, rows)
@@ -522,49 +753,131 @@
             prob[h_, h, :, :keys] = p
             o_send[h_, head(h), :] = dot(vt[head(h), :keys], p, NT).astype(BF)
         swap_send(sz, group, place, o_send, attn, *swap_sems, h_)
-    drive([ffn, cots])
+        step(wos)
+        if h_ in (1, 2):
+            cots.relay(n - h_)
+            step(ffn)
+    for i in range(sz.all):
+        wo[i * owned : (i + 1) * owned, :] = wo_all[spot(i)][:owned, :].astype(F32)
+    drive([wos])
+    extra = wo_all[spot(0)][owned:, :].astype(F32)
+    for i in range(1, sz.all):
+        extra = extra + wo_all[spot(i)][owned:, :].astype(F32)
+    small[...] = extra[:8]
+    gain_m = small[1:2, :]
+    wo_b = wo[...].astype(BF)
     swap_wait(sz, group, place, o_send, attn, *swap_sems)
 
     attn_t = attn[...].reshape(width, rows)
-    wo_b = wo[...].astype(BF)
     res = tokens[...].astype(F32) + dot(attn_t, wo_b, TN)
     resid[...] = res
     inv = lax.rsqrt(mean_square(res, width) + EPSILON)
-    mixed[...] = (res * inv * gain_m).astype(BF)
+    mixed = (res * inv * gain_m).astype(BF)
+    mix_all[ctx] = mixed
     row = iota((8, rows), 0)
-    logits = dot(small[...].astype(BF), mixed[...], NT)
+    logits = dot(small[...].astype(BF), mixed, NT)
     logits = jnp.concatenate([logits[2:], logits[:2]], axis=0)
     logits = jnp.where(row < sz.experts, logits, MASKED)
     expo = jnp.exp(logits - jnp.max(logits, axis=0, keepdims=True))
     router_prob = expo * (1.0 / jnp.sum(expo, axis=0, keepdims=True))
     route[0] = router_prob
-    route[1] = kept
     weight = router_prob * kept
     high = weight.astype(BF).astype(F32)
     high_row = jnp.where(row == sz.experts, 1.0, high)
-    cw[...] = jnp.concatenate([high_row, weight - high], axis=0).astype(BF)
-    late = [
-        gather_ctx(pos, cw, cw_all, s[5], *r(5)),
-        gather_ctx(pos, mixed, mix_all, s[6], *r(6)),
-    ]
-    for stream in late:
-        next(stream)
+    cw_all[ctx] = jnp.concatenate([high_row, weight - high], axis=0).astype(BF)
+
+    weights.start()
+    mixes.start()
     wo[...] = wo_b.astype(F32)
     for src, dst in zip(
-        (normed, qt, kt, vt, prob, wt, wo, small, attn, resid, mixed, route, table),
+        (normed, qt, kt, vt, prob, wt, wo, small, attn, resid, mix_all.at[ctx], route, table),
         (normed_o, qt_o, kt_o, vt_o, prob_o, wt_o, wo_o, small_o, attn_o, resid_o, mixed_o, route_o, table_o),
     ):
         out.start(src, dst)
-    drive(late)
+    drive([ffn])
+
+    block = 256
+    chunk = 2 * rows
+
+    def hidden_units(a):
+        at_rows = blk(a, chunk)
+        x = mix_all[pl.ds(2 * a, 2)].reshape(chunk, width)
+        g = g_all[pl.ds(2 * a, 2)].reshape(chunk, width)
+
+        def units(j, pair):
+            at = blk(j, block)
+            gate = dot(x, ffn_w[0, at, :], NT)
+            up = dot(x, ffn_w[1, at, :], NT)
+            back = dot(g, ffn_w[2, at, :], NT)
+            weight = jnp.concatenate([dot(cw_all[2 * a + i], spread[:16, at], TN) for i in range(2)], axis=0)
+            sig = 1.0 / (1.0 + jnp.exp(-gate))
+            act = gate * sig
+            hid = act * up
+            pair = pair + dot(spread[16:, at], (hid * back).astype(BF), NT)
+            hw[at_rows, at] = (hid * weight).astype(BF)
+            back = back * weight
+            dg[at_rows, at] = (back * up * sig * (1.0 + gate * (1.0 - sig))).astype(BF)
+            du[at_rows, at] = (back * act).astype(BF)
+            return pair
+
+        pair = lax.fori_loop(0, ffn_w.shape[1] // block, units, jnp.zeros((16, chunk), F32))
+        for i in range(2):
+            gp_part[2 * a + i] = pair[:, i * rows : (i + 1) * rows].astype(BF)
+
+    def input_grad(a):
+        at_rows = blk(a, chunk)
+        total = dot(dg[at_rows, :], ffn_w[0], NN) + dot(du[at_rows, :], ffn_w[1], NN)
+        gm_part[pl.ds(2 * a, 2)] = total.astype(BF).reshape(2, rows, width)
+        gm_sum.push(a)
+
+    near = [pos.a, jnp.where(pos.a == 0, 1, jnp.where(pos.a == 1, 0, jnp.where(pos.a == 2, 3, 2)))]
+    near += [jnp.where(pos.a < 2, 2, 1), jnp.where(pos.a < 2, 3, 0)]
+    for i in range(n):
+        if i + 1 < n:
+            weights.relay(i + 1)
+            mixes.relay(i + 1)
+        for stream in (cots, weights, mixes):
+            stream.across(near[i])
+        hidden_units(near[i])
+        input_grad(near[i])
+        if i > 1:
+            gm_sum.pass_on(near[i - 1], other=True)
+    xs = mix_all[...].reshape(sz.slot, width)
+    gs = g_all[...].reshape(sz.slot, width)
+    total_units = ffn_w.shape[1]
+
+    def unit_grads(j, _):
+        at = blk(j, block)
+        dw[0, at, :] = dot(dg[:, at], xs, TN).astype(BF)
+        dw[1, at, :] = dot(du[:, at], xs, TN).astype(BF)
+        dw[2, at, :] = dot(hw[:, at], gs, TN).astype(BF)
+        return 0
+
+    lax.fori_loop(0, total_units // block // 2, unit_grads, 0)
+    gm_sum.pass_on(near[-1], other=True)
+    gm_sum.pass_on(pos.a, other=False)
+    lax.fori_loop(total_units // block // 2, total_units // block, unit_grads, 0)
+    out.start(dw, dw_o)
+    for a in range(n):
+        part = slice(a * chunk, (a + 1) * chunk)
+        y_part[2 * a : 2 * a + 2] = dot(hw[part, :], ffn_w[2], NN).astype(BF).reshape(2, rows, width)
+    out.start(y_part, y_o)
+    gm_o[...], gp_o[...] = gm_sum.total()
     out.finish()
-    for x in s:
+    gm_sum.finish()
+    for x in (*s, toks, cots, mixes, weights):
         x.finish()
 
 
-def forward(sz, collective_id, lengths, inverse, tokens, cot, routes_t, wq_send, wo_send, ffn_send):
-    n, nc, rows, width = sz.columns, sz.nc, sz.rows, sz.width
-    saved = [
-        ((nc, rows, width), BF),
+def step(*streams):
+    for stream in streams:
+        next(stream, None)
+
+
+def saved_shapes(sz):
+    rows, width = sz.rows, sz.width
+    return [
+        ((sz.nc, rows, width), BF),
         ((GROUPS, sz.share, rows), BF),
         ((sz.share, sz.slot), BF),
         ((sz.share, sz.slot), BF),
@@ -578,149 +891,78 @@
         ((2, 8, rows), F32),
         ((2, HEAD_DIM // 2, sz.slot), F32),
     ]
+
+
+def forward(sz, collective_id, lengths, tokens, cot, routes, small_own, spread, wq_send, wo_own, ffn_send):
+    n, nc, rows, width = sz.columns, sz.nc, sz.rows, sz.width
+    units = sz.nf * ffn_send.shape[1]
+    saved = saved_shapes(sz)
     outs = [
+        shaped((rows, width), F32),
+        shaped((16, rows), F32),
         shaped((nc, rows, width)),
-        shaped((nc, rows, width)),
-        shaped((nc, 16, rows)),
-        shaped((ffn_send.shape[0], sz.nf) + ffn_send.shape[1:]),
+        shaped((3, units, width)),
     ] + [shaped(*x) for x in saved]
     v = lambda shape, dtype=BF: pltpu.VMEM(tuple(shape), dtype)
     normed, qt, kt, vt, prob, wt, wo, small, attn, resid, mixed, route, table = (v(*x) for x in saved)
+    tree = (2, 2, 2, n)
     scratch = [
-        v((nc, rows, width)), v((sz.all,) + wq_send.shape[1:]), v((sz.all,) + wo_send.shape),
+        v((nc, rows, width)), v(tree + wq_send.shape[1:]), v(tree + (sz.padded, width)), v((sz.padded, width)),
         v((width, 3 * sz.share), F32), wt, wo, small, normed, qt, kt, vt, prob, v((GROUPS, sz.share, rows)),
-        attn, resid, mixed, route, v((16, rows)), v((rows, width)), table,
+        attn, resid, route, v((rows, width)), table,
+        v((nc, rows, width)), v((nc, rows, width)), v((nc, 16, rows)), v((3, units, width)),
+        v((sz.slot, units)), v((sz.slot, units)), v((sz.slot, units)),
+        v((nc, rows, width)), v((nc, 16, rows)), v((nc, rows, width)), v((3, units, width)),
     ]
-    sems = gather_ctx_sems(n) + gather_all_sems(n) * 2 + gather_fsdp_sems(ffn_send.shape[0]) + gather_ctx_sems(n) * 3
-    sems += [DMA((GROUPS,)), DMA((GROUPS,)), DMA, DMA((len(saved),))]
+    sems = gather_tree_sems(n) * 2 + gather_fsdp_sems(3)
+    sems += [DMA((GROUPS,)), DMA((GROUPS,)), DMA, DMA((len(saved) + 2,))]
+    sems += sum_ctx_scratch(n, (rows, width), (16, rows)) + gather_line_sems(n) * 3 + gather_line_sems(n, parts=1)
     hbm, vmem = pl.BlockSpec(memory_space=pl.ANY), pl.BlockSpec(memory_space=pltpu.VMEM)
     return pl.pallas_call(
         functools.partial(forward_kernel, sz),
         out_shape=outs,
-        in_specs=[pl.BlockSpec(memory_space=pltpu.SMEM), vmem, vmem, vmem, vmem, hbm, hbm, hbm],
-        out_specs=[hbm] * len(outs),
+        in_specs=[pl.BlockSpec(memory_space=pltpu.SMEM), vmem, vmem, vmem, vmem, vmem, hbm, vmem, hbm],
+        out_specs=[vmem, vmem] + [hbm] * (len(outs) - 2),
         scratch_shapes=scratch + sems,
         compiler_params=pltpu.CompilerParams(collective_id=collective_id, has_side_effects=True, vmem_limit_bytes=62 << 20),
         name="forward",
-    )(lengths, inverse, tokens, cot, routes_t, wq_send, wo_send, ffn_send)
-
-
-def ffn_kernel(chunk, mix, cw, g, wg, wu, wd, spread, gm, yy, pair, dg_w, du_w, dd_w, hw_all, dg_all, du_all, wg_all, wu_all, wd_all, pair_acc):
-    j = pl.program_id(0)
-    hb = wg.shape[0]
-    nc, rows, width = mix.shape
-    per = chunk // rows
-    at = blk(j, hb) if hb < wg_all.shape[0] else pl.ds(0, hb)
-    wg_all[at, :] = wg[...]
-    wu_all[at, :] = wu[...]
-    wd_all[at, :] = wd[...]
-    sp = spread[...]
-    for m in range(nc // per):
-        part = slice(m * per, (m + 1) * per)
-        x = mix[part].reshape(chunk, width)
-        gate = dot(x, wg[...], NT)
-        up = dot(x, wu[...], NT)
-        back = dot(g[part].reshape(chunk, width), wd[...], NT)
-        weight = jnp.concatenate([dot(cw[m * per + i], sp[:16], TN) for i in range(per)], axis=0)
-        sig = 1.0 / (1.0 + jnp.exp(-gate))
-        act = gate * sig
-        hid = act * up
-        ms = slice(m * chunk, (m + 1) * chunk)
-        product = dot(sp[16:], (hid * back).astype(BF), NT)
-
-        @pl.when(j == 0)
-        def _():
-            pair_acc[:, ms] = product
-
-        @pl.when(j > 0)
-        def _():
-            pair_acc[:, ms] = pair_acc[:, ms] + product
-
-        hw_all[ms, at] = (hid * weight).astype(BF)
-        back = back * weight
-        dg_all[ms, at] = (back * up * sig * (1.0 + gate * (1.0 - sig))).astype(BF)
-        du_all[ms, at] = (back * act).astype(BF)
-    xs = mix[...].reshape(nc * rows, width)
-    dg_w[...] = dot(dg_all[:, at], xs, TN).astype(BF)
-    du_w[...] = dot(du_all[:, at], xs, TN).astype(BF)
-    dd_w[...] = dot(hw_all[:, at], g[...].reshape(nc * rows, width), TN).astype(BF)
-
-    @pl.when(j == pl.num_programs(0) - 1)
-    def _():
-        for m in range(nc // per):
-            ms = slice(m * chunk, (m + 1) * chunk)
-            part = slice(m * per, (m + 1) * per)
-            total = dot(dg_all[ms], wg_all[...], NN) + dot(du_all[ms], wu_all[...], NN)
-            gm[part] = total.astype(BF).reshape(per, rows, width)
-            yy[part] = dot(hw_all[ms], wd_all[...], NN).astype(BF).reshape(per, rows, width)
-        for d in range(nc):
-            pair[d] = pair_acc[:, d * rows : (d + 1) * rows].astype(BF)
-
-
-def feed_forward(mix, cw, g, w, spread):
-    nc, rows, width = mix.shape
-    units = w.shape[1]
-    block = math.gcd(units, 256) if units % 256 == 0 else units
-    chunk = 1024
-    once = pl.Buffered(1)
-    full = lambda a: pl.BlockSpec(a.shape, lambda j: (0,) * a.ndim, pipeline_mode=once)
-    of = lambda p: pl.BlockSpec((None, block, width), lambda j: (p, j, 0))
-    kept = lambda *shape: pl.BlockSpec(shape, lambda j: (0,) * len(shape), pipeline_mode=once)
-    grads = pl.BlockSpec((block, width), lambda j: (j, 0))
-    t = nc * rows
-    flops = 2 * t * units * width * 9
-    return pl.pallas_call(
-        functools.partial(ffn_kernel, chunk),
-        grid=(units // block,),
-        out_shape=(shaped(mix.shape), shaped(mix.shape), shaped((nc, 16, rows))) + (shaped((units, width)),) * 3,
-        in_specs=[full(mix), full(cw), full(g), of(0), of(1), of(2), pl.BlockSpec((32, block), lambda j: (0, j))],
-        out_specs=(kept(nc, rows, width), kept(nc, rows, width), kept(nc, 16, rows), grads, grads, grads),
-        scratch_shapes=[pltpu.VMEM((t, units), BF)] * 3 + [pltpu.VMEM((units, width), BF)] * 3 + [pltpu.VMEM((16, t), F32)],
-        compiler_params=pltpu.CompilerParams(vmem_limit_bytes=62 << 20),
-        cost_estimate=pl.CostEstimate(flops=flops, bytes_accessed=w.size * 4 + mix.size * 8, transcendentals=t * units),
-        name="feed_forward",
-    )(mix, cw, g, w, w, w, spread)
+    )(lengths, tokens, cot, routes, small_own, spread, wq_send, wo_own, ffn_send)
 
 
 def backward_kernel(
-    sz, lengths, tokens, cot, gm_part, pair_part, y_part, dg_w, du_w, dd_w,
+    sz, lengths, tokens, cot, gm_own, gp_own, y_part, dw,
     normed_i, qt_i, kt_i, vt_i, prob_i, wt_i, wo_i, small_i, attn_i, resid_i, mixed_i, route_i, table_i,
-    o_out, o_tokens, o_wq, o_wo, o_ffn,
+    o_out, o_tokens, o_wq, o_wo, o_in, o_down,
     normed, qt, kt, vt, prob, wt, wo, small, attn, resid, mixed, route, table,
-    do_send, do, dkt, dvt, dqt_b, dkvt_b, normed_q, gn_part, wq_part, wo_part, gm_own, gp_own, gn_own, y_own,
+    do_send, do, dkt, dvt, dqt_b, dkvt_b, normed_q, gn_part, wq_part, wo_part, y_own, ffn_own,
     *scratch,
 ):
     pos = Place(sz.columns)
     ctx = lax.axis_index("ctx")
     group, place = ctx // sz.per, ctx % sz.per
     rows, width, share, n = sz.rows, sz.width, sz.share, sz.columns
+    owned = sz.owned
     sizes, ends = scalars(sz, lengths)
-    c_gm, c_gp, c_y, c_gn = (scratch[6 * i : 6 * i + 6] for i in range(4))
-    a_wq, a_wo = scratch[24:32], scratch[32:40]
-    f_ffn = scratch[40:46]
-    swap_sems, loads = scratch[46:49], Copies(scratch[49])
+    c_y, g_sum, t_wq, t_wo, f_ffn = scratch[:6], scratch[6:10], scratch[10:16], scratch[16:22], scratch[22:28]
+    swap_sems, first, later = scratch[28:31], Copies(scratch[31]), Copies(scratch[32])
+    saved = (normed_i, qt_i, kt_i, vt_i, prob_i, wt_i, wo_i, small_i, attn_i, resid_i, mixed_i, route_i, table_i)
+    held = (normed, qt, kt, vt, prob, wt, wo, small, attn, resid, mixed, route, table)
+    for i in (7, 6, 9, 10, 11):
+        first.start(saved[i], held[i])
+    for i in (8, 0, 2, 3, 1, 4, 5, 12):
+        later.start(saved[i], held[i])
     greet(all_partners(pos))
-    s = {x: Sends(scratch[i]) for x, i in (("gm", 3), ("gp", 9), ("y", 15), ("gn", 21), ("wq", 29), ("wo", 37), ("ffn", 43))}
-
-    def ctx_sum(name, part, out, x):
-        return scatter_ctx(pos, part, out, *x[:3], s[name], *x[4:])
-
-    early = [ctx_sum("gp", pair_part, gp_own, c_gp), ctx_sum("gm", gm_part, gm_own, c_gm)]
-    ffn = scatter_fsdp(pos, (dg_w, du_w, dd_w), o_ffn, *f_ffn[:3], s["ffn"], *f_ffn[4:])
-    for stream in early:
-        next(stream)
-    next(ffn)
-    for src, dst in zip(
-        (normed_i, qt_i, kt_i, vt_i, prob_i, wt_i, wo_i, small_i, attn_i, resid_i, mixed_i, route_i, table_i),
-        (normed, qt, kt, vt, prob, wt, wo, small, attn, resid, mixed, route, table),
-    ):
-        loads.start(src, dst)
-    drive(early)
-    loads.finish()
-    ys = ctx_sum("y", y_part, y_own, c_y)
-    next(ys)
-
-    gain_a, gain_m = small[0:1, :], small[1:2, :]
+    s = {x: Sends(y) for x, y in (("y", c_y[3]), ("wq", t_wq[4]), ("wo", t_wo[4]), ("ffn", f_ffn[3]))}
+    ys = scatter_ctx(pos, y_part, y_own, *c_y[:3], s["y"], *c_y[4:])
+    by_owner = [dw.at[p] for p in range(3)]
+    ffn = scatter_fsdp(pos, by_owner, ffn_own, *f_ffn[:3], s["ffn"], *f_ffn[4:])
+    wos = scatter_tree(pos, wo_part, o_wo, *t_wo[:4], s["wo"], t_wo[5])
+    wqs = scatter_tree(pos, wq_part, o_wq, *t_wq[:4], s["wq"], t_wq[5], per_group=True)
+    gn_sum = SumCtx(pos, [(gn_part, g_sum[0], g_sum[1])], g_sum[2], g_sum[3])
+    step(ffn)
+    first.finish()
+
+    gain_m = small[1:2, :]
     live = (ctx * rows + iota((rows, 1), 0)) < ends[-1]
     router_prob, kept = route[0], route[1]
     grad_prob = gp_own[:8, :] * kept
@@ -735,25 +977,36 @@
     grad_resid = jnp.where(live, cot[...].astype(F32), 0.0) + inv * w - res * inner * inv * inv * inv
     grad_gain_m = jnp.sum(grad_mixed * res * inv, axis=0, keepdims=True)
     grad_resid_b = grad_resid.astype(BF)
-    resid[...] = res
-    wo_b = wo[...].astype(BF)
-    grad_attn_t = dot(wo_b, grad_resid_b, NT).astype(BF)
+    grad_attn_t = dot(wo[...].astype(BF), grad_resid_b, NT).astype(BF)
     for h_ in range(GROUPS):
         do_send[h_] = grad_attn_t[h_ * share : (h_ + 1) * share]
     for h_ in range(GROUPS):
         swap_send(sz, group, place, do_send, do, *swap_sems, h_)
-    next(ffn)
-    next(ys)
+    step(ys)
+
+    later.finish()
     grad_wo = dot(attn[...].reshape(width, rows), grad_resid_b, NN)
+    row = iota((sz.padded - owned, width), 0)
+    grad_small = jnp.where(row == 1, grad_gain_m, jnp.concatenate([grad_small] * ((sz.padded - owned) // 8), axis=0)).astype(BF)
+
+    def spot(i):
+        a_b, y_c = divmod(i, sz.nf)
+        return y_c % 2, a_b % 2, y_c // 2, a_b // 2
+
     for i in range(sz.all):
-        wo_part[i, : sz.owned, :] = grad_wo[i * sz.owned : (i + 1) * sz.owned].astype(BF)
+        wo_part[spot(i) + (slice(0, owned),)] = grad_wo[i * owned : (i + 1) * owned].astype(BF)
+        wo_part[spot(i) + (slice(owned, None),)] = grad_small
+    step(wos)
     for h_ in range(GROUPS):
         normed_q[h_] = normed[h_ * sz.per + place]
-    next(ffn)
+    step(ffn)
     swap_wait(sz, group, place, do_send, do, *swap_sems)
 
+    dkt[...] = jnp.zeros_like(dkt)
+    dvt[...] = jnp.zeros_like(dvt)
     for h_ in reversed(range(GROUPS)):
         keys = (h_ + 1) * sz.per * rows
+        done = slice(h_ * sz.per * rows, keys)
         part = blk(h_ * sz.per + place, rows)
         for h in range(sz.heads):
             d_o = do[h_, head(h), :]
@@ -764,42 +1017,21 @@
             grad_s = (pf * (grad_p - delta)).astype(BF)
             dq = dot(kt[head(h), :keys], grad_s, NT) * (1.0 / math.sqrt(HEAD_DIM))
             dqt_b[h_, head(h), :] = turn(dq, table[0, :, part], -table[1, :, part]).astype(BF)
-            dk = dot(qt[h_, head(h), :], grad_s, NN)
-            dv = dot(d_o, p, NN)
-            if h_ == GROUPS - 1:
-                dkt[head(h), :] = dk
-                dvt[head(h), :] = dv
-            else:
-                dkt[head(h), :keys] = dkt[head(h), :keys] + dk
-                dvt[head(h), :keys] = dvt[head(h), :keys] + dv
-        if h_ == 2:
-            next(ffn)
-            next(ys)
-    for h in range(sz.heads):
-        dkvt_b[head(h), :] = turn(dkt[head(h), :], table[0], -table[1]).astype(BF)
-    dkvt_b[share:, :] = dvt[...].astype(BF)
-
-    grad_gain_a = jnp.zeros((1, width), F32)
-    for step in range(sz.per):
-        for h_ in range(GROUPS):
-            other = lax.rem(place + 1 + step, sz.per)
-            d = h_ * sz.per + other
+            dkt[head(h), :keys] = dkt[head(h), :keys] + dot(qt[h_, head(h), :], grad_s, NN)
+            dvt[head(h), :keys] = dvt[head(h), :keys] + dot(d_o, p, NN)
+        for h in range(sz.heads):
+            dkvt_b[head(h), done] = turn(dkt[head(h), done], table[0, :, done], -table[1, :, done]).astype(BF)
+        dkvt_b[share:, done] = dvt[:, done].astype(BF)
+        for t in range(2):
+            d = h_ * sz.per + lax.rem(place + 1 + t, 2)
             gn = dot(dkvt_b[:, blk(d, rows)], wt[share:, :], TN)
-            if step == sz.per - 1:
+            if t == 1:
                 gn = gn + dot(dqt_b[h_], wt[:share, :], TN)
-            grad_gain_a = grad_gain_a + jnp.sum(gn * normed[d].astype(F32), axis=0, keepdims=True)
             gn_part[d] = gn.astype(BF)
-    grad_gain_a = grad_gain_a / gain_a
-    gns = ctx_sum("gn", gn_part, gn_own, c_gn)
-    next(gns)
-    row = iota((8, width), 0)
-    grad_small = jnp.where(row == 0, grad_gain_a, jnp.where(row == 1, grad_gain_m, grad_small))
-    pad = jnp.zeros((sz.padded - sz.owned - 8, width), F32)
-    grad_small = jnp.concatenate([grad_small, pad], axis=0).astype(BF) if pad.shape[0] else grad_small.astype(BF)
-    for i in range(sz.all):
-        wo_part[i, sz.owned :, :] = grad_small
-    wos = scatter_all(pos, wo_part, o_wo, *a_wo[:5], s["wo"], *a_wo[6:])
-    next(wos)
+        gn_sum.push(h_)
+        if h_ < GROUPS - 1:
+            gn_sum.pass_on(h_ + 1)
+        step(wos, ffn, ys)
     grad_q = dot(dqt_b[0], normed_q[0], NN)
     for h_ in range(1, GROUPS):
         grad_q = grad_q + dot(dqt_b[h_], normed_q[h_], NN)
@@ -807,51 +1039,56 @@
     grad_w = jnp.concatenate([grad_q, grad_kv], axis=0).T
     wq_part[...] = jnp.zeros_like(wq_part)
     for i in range(sz.all):
-        wq_part[i, : sz.owned, :] = grad_w[i * sz.owned : (i + 1) * sz.owned].astype(BF)
-    wqs = scatter_all(pos, wq_part, o_wq, *a_wq[:5], s["wq"], *a_wq[6:], per_group=True)
-    drive([gns, wqs, wos, ffn, ys])
-
+        wq_part[spot(i) + (slice(0, owned),)] = grad_w[i * owned : (i + 1) * owned].astype(BF)
+    step(wqs)
+    gn_sum.pass_on(0)
+    drive([wqs, wos, ys, ffn])
+    o_in[...] = ffn_own[:2]
+    o_down[...] = ffn_own[2]
     o_out[...] = jnp.where(live, res + y_own[...], 0.0).astype(BF)
     x = tokens[...].astype(F32)
     inv = lax.rsqrt(mean_square(x, width) + EPSILON)
-    w = gn_own[...] * gain_a
+    (gn_own,) = gn_sum.total()
+    w = gn_own
     inner = jnp.sum(w * x, axis=-1, keepdims=True) * (1.0 / width)
     o_tokens[...] = grad_resid + inv * w - x * inner * inv * inv * inv
+    gn_sum.finish()
     for x in s.values():
         x.finish()
 
 
-def backward(sz, collective_id, lengths, tokens, cot, gm_part, pair_part, y_part, dg_w, du_w, dd_w, saved):
+def backward(sz, collective_id, lengths, tokens, cot, gm_own, gp_own, y_part, dw, saved):
     n, rows, width = sz.columns, sz.rows, sz.width
-    part = (3, sz.nf, dg_w.shape[1], width)
+    units = dw.shape[2]
     outs = [
         shaped((rows, width)),
         shaped((rows, width), F32),
         shaped((GROUPS, sz.padded, 3 * sz.share), F32),
         shaped((sz.padded, width), F32),
-        shaped((3,) + dg_w.shape[1:], F32),
+        shaped((2, units, width), F32),
+        shaped((units, width), F32),
     ]
     v = lambda shape, dtype=BF: pltpu.VMEM(tuple(shape), dtype)
+    tree = (2, 2, 2, n)
     scratch = [v(x.shape, x.dtype) for x in saved] + [
         v((GROUPS, sz.share, rows)), v((GROUPS, sz.share, rows)), v((sz.share, sz.slot), F32), v((sz.share, sz.slot), F32),
         v((GROUPS, sz.share, rows)), v((2 * sz.share, sz.slot)), v((GROUPS, rows, width)), v((sz.nc, rows, width)),
-        v((sz.all, sz.padded, 3 * sz.share)), v((sz.all, sz.padded, width)),
-        v((rows, width), F32), v((16, rows), F32), v((rows, width), F32), v((rows, width), F32),
+        v(tree + (sz.padded, 3 * sz.share)), v(tree + (sz.padded, width)), v((rows, width), F32), v((3, units, width), F32),
     ]
-    scratch += scatter_ctx_scratch(n, (rows, width)) + scatter_ctx_scratch(n, (16, rows)) + scatter_ctx_scratch(n, (rows, width)) * 2
-    scratch += scatter_all_scratch(n, (sz.padded, 3 * sz.share)) + scatter_all_scratch(n, (sz.padded, width))
-    scratch += scatter_fsdp_scratch(3, dg_w.shape[1:])
-    scratch += [DMA((GROUPS,)), DMA((GROUPS,)), DMA, DMA((len(saved),))]
+    scratch += scatter_ctx_scratch(n, (rows, width)) + sum_ctx_scratch(n, (rows, width))
+    scratch += scatter_tree_scratch(n, (sz.padded, 3 * sz.share)) + scatter_tree_scratch(n, (sz.padded, width))
+    scratch += scatter_fsdp_scratch(3, dw.shape[2:])
+    scratch += [DMA((GROUPS,)), DMA((GROUPS,)), DMA, DMA((len(saved),)), DMA((len(saved),))]
     hbm, vmem = pl.BlockSpec(memory_space=pl.ANY), pl.BlockSpec(memory_space=pltpu.VMEM)
     return pl.pallas_call(
         functools.partial(backward_kernel, sz),
         out_shape=outs,
-        in_specs=[pl.BlockSpec(memory_space=pltpu.SMEM), vmem, vmem] + [hbm] * (6 + len(saved)),
+        in_specs=[pl.BlockSpec(memory_space=pltpu.SMEM)] + [vmem] * 4 + [hbm] * (2 + len(saved)),
         out_specs=[vmem] * len(outs),
         scratch_shapes=scratch,
         compiler_params=pltpu.CompilerParams(collective_id=collective_id, has_side_effects=True, vmem_limit_bytes=62 << 20),
         name="backward",
-    )(lengths, tokens, cot, gm_part, pair_part, y_part, dg_w, du_w, dd_w, *saved)
+    )(lengths, tokens, cot, gm_own, gp_own, y_part, dw, *saved)
 
 
 def gather_start_kernel(columns, group_of, tokens, wq, wo, ffn, cot, o_tokens, o_wq, o_wo, o_ffn, o_cot, *sems):
@@ -1211,7 +1448,7 @@
     rows, width = tokens.shape[1:]
     experts, hidden, top = expert_in.shape[1], expert_in.shape[0], routes.shape[2]
     owned = w_out.shape[0]
-    if 2 * nc * rows * width > FUSED_BYTES:
+    if nc != 2 * GROUPS or 2 * nc * rows * width > FUSED_BYTES:
         return body_wide(
             tokens, doc_lengths, routes, cotangent, attn_gain, w_qkv, w_out, mlp_gain, router, expert_in, expert_out, shared_in, shared_out
         )
@@ -1220,19 +1457,13 @@
     share = sz.share
     device = lax.axis_index("ctx") * nf + lax.axis_index("fsdp")
 
-    wq_send = w_qkv.reshape(owned, 3, GROUPS, share).transpose(2, 0, 1, 3).reshape(GROUPS, owned, 3 * share)
+    gain = attn_gain.astype(F32)[:, None]
+    wq_send = (w_qkv.astype(F32) * gain).astype(BF).reshape(owned, 3, GROUPS, share).transpose(2, 0, 1, 3).reshape(GROUPS, owned, 3 * share)
     wq_send = jnp.pad(wq_send, ((0, 0), (0, padded - owned), (0, 0)))
-    small = jnp.concatenate([attn_gain[None], mlp_gain[None], router.T], axis=0)
-    small = lax.dynamic_update_slice(jnp.zeros((padded - owned, width), BF), small, (0, device * owned))
-    wo_send = jnp.concatenate([w_out, small], axis=0)
+    small = jnp.concatenate([attn_gain[None], mlp_gain[None], router.T, jnp.zeros((padded - owned - 2 - experts, owned), BF)], axis=0)
     gate_up = jnp.concatenate([expert_in.transpose(2, 1, 0, 3), shared_in.transpose(1, 0, 2)[:, None]], axis=1)
     down = jnp.concatenate([expert_out.transpose(1, 0, 2), shared_out[None]], axis=0)
     ffn_send = jnp.concatenate([gate_up, down[None]], axis=0).reshape(3, (experts + 1) * hidden, width)
-
-    half = HEAD_DIM // 2
-    inverse = (ROPE_BASE ** (-2.0 * np.arange(half) / HEAD_DIM)).astype(np.float32)
-    inverse = jnp.asarray(np.broadcast_to(inverse[:, None], (half, 128)))
-    routes_t = jnp.pad(routes[0].T, ((0, 8 - top), (0, 0)))
 
     units = nf * (experts + 1) * hidden
     of = np.arange(units) // hidden % (experts + 1)
@@ -1243,28 +1474,32 @@
         spread[8 + e] = of == e
         spread[16 + e] = of == e
 
-    g_all, mix_all, cw_all, ffn_all, *saved = forward(sz, 1, doc_lengths, inverse, tokens[0], cotangent[0], routes_t, wq_send, wo_send, ffn_send)
-    gm_part, y_part, pair_part, dg_w, du_w, dd_w = feed_forward(mix_all, cw_all, g_all, ffn_all.reshape(3, units, width), jnp.asarray(spread, BF))
-    by_owner = lambda v: v.reshape(nf, (experts + 1) * hidden, width)
-    layer_out, grad_tokens, wq_own, wo_own, ffn_own = backward(
-        sz, 2, doc_lengths, tokens[0], cotangent[0], gm_part, pair_part, y_part, by_owner(dg_w), by_owner(du_w), by_owner(dd_w), saved
+    gm_own, gp_own, y_part, dw, *saved = forward(
+        sz, 1, doc_lengths, tokens[0], cotangent[0], routes[0], small, jnp.asarray(spread, BF), wq_send, w_out, ffn_send
     )
-
-    grad_w_qkv = wq_own[:, :owned].reshape(GROUPS, owned, 3, share).transpose(1, 2, 0, 3).reshape(owned, 3 * width)
+    dw = dw.reshape(3, nf, (experts + 1) * hidden, width)
+    layer_out, grad_tokens, wq_own, wo_own, grad_in, grad_down = backward(
+        sz, 2, doc_lengths, tokens[0], cotangent[0], gm_own, gp_own, y_part, dw, saved
+    )
+
+    grad_w = wq_own[:, :owned].reshape(GROUPS, owned, 3, share).transpose(1, 2, 0, 3).reshape(owned, 3 * width)
+    gain_a = jnp.sum(grad_w * w_qkv.astype(F32), axis=1)
+    grad_w_qkv = grad_w * gain
     small = lax.dynamic_slice(wo_own[owned:], (0, device * owned), (2 + experts, owned))
-    out = ffn_own.reshape(3, experts + 1, hidden, width)
+    grad_in = grad_in.reshape(2, experts + 1, hidden, width)
+    grad_down = grad_down.reshape(experts + 1, hidden, width)
     return (
         layer_out[None],
         grad_tokens[None],
-        small[0],
+        gain_a,
         grad_w_qkv,
         wo_own[:owned],
         small[1],
         small[2:].T,
-        out[:2, :experts].transpose(2, 1, 0, 3),
-        out[2, :experts].transpose(1, 0, 2),
-        out[:2, experts].transpose(1, 0, 2),
-        out[2, experts],
+        grad_in[:, :experts].transpose(2, 1, 0, 3),
+        grad_down[:experts].transpose(1, 0, 2),
+        grad_in[:, experts].transpose(1, 0, 2),
+        grad_down[experts],
     )
 
 

time: 253 us -> 239 us (0.945)
  Pallas kernels: 224 us -> 216 us
  local copies, waits for them, and re-layouts: 22.6 us -> 15 us
    pallas_call x1 -> x0, Pallas kernels: 29.7 us -> none  [feed_forward(): pl.pallas_call(functools.partial(ffn_kernel, chunk), grid=(units // block...]
    pallas_call x1, Pallas kernels: 110 us -> 132 us  [forward(): pl.pallas_call(functools.partial(forward_kernel, sz), out_shape=outs, in_...]
    slice x0 -> x5, local copies, waits for them, and re-layouts: none -> 4.71 us  [the longest x1 1.56 us: body(): grad_in[:, :experts].transpose(2, 1, 0, 3)]
    reshape x2, local copies, waits for them, and re-layouts: 2.95 us -> 0.36 us  [body(): wq_own[:, :owned].reshape(GROUPS, owned, 3, share).transpose(1, 2, 0, 3)]
    unnamed x19 -> x33, local copies, waits for them, and re-layouts: 6.25 us -> 6.34 us
where the time goes in v3:
time: 239 us; the launch traced here: 238 us
  Pallas kernels  216 us (90%)
  local copies, waits for them, and re-layouts  15 us (6%)
  other arithmetic  6.66 us (3%)
    pallas_call x1, Pallas kernels, forward(): pl.pallas_call(functools.partial(forward_kernel, sz), out_shape=outs, in_...  132 us
    pallas_call x1, Pallas kernels, backward(): pl.pallas_call(functools.partial(backward_kernel, sz), out_shape=outs, in...  84.2 us
    unnamed x33, local copies, waits for them, and re-layouts  6.34 us

profile of v3, /device:TPU:0, one launch (start us, length us, event | category | flops | bytes accessed | tf_op | source)
XLA Modules:
  0.0 238.4 jit_solution(13965180133105306237)
XLA Ops:
  0.7 0.7 convert_element_type.13
  1.4 1.0 fusion
  2.4 0.2 reshape.49
  2.6 0.2 reshape.50
  2.8 0.7 pad.4.wq_send
  3.5 1.3 pad_maximum_fusion.1
  4.8 0.1 copy.47
  4.9 0.2 copy.48
  5.1 0.7 copy-done.4
  5.8 0.4 pad_maximum_fusion.2
  6.2 0.1 copy.49
  6.3 1.2 pad_maximum_fusion.ffn_send
  7.6 0.7 copy.44
  8.3 0.1 pad.14.clone
  8.4 0.7 maximum_maximum_fusion.small_own
  9.0 131.7 %forward.1 = (f32[128,768]{1,0:T(8,128)}, f32[16,128]{1,0:T(8,128)}, bf16[8,128,768]{2,1,0:T(8,128)(2,1)}, bf16[3,1280,768]{2,1,0:T(8,128)(2,1)}, bf16[8,128,768...) custom-call(s32[1,4]{1,0:T(1,128)} %lengths.3, ...), custom_call_target="tpu_custom_call" | custom-call | tf_op jit(solution)/shard_map/forward/pallas_call | solution.py:921
  140.8 84.2 %backward.1 = (bf16[128,768]{1,0:T(8,128)(2,1)}, f32[128,768]{1,0:T(8,128)}, f32[4,32,576]{2,1,0:T(8,128)}, f32[32,768]{1,0:T(8,128)}, f32[2,320,768]{2,1,0:T(8,128)}, /*index=5*/f32[320,768]{1,0:T(8,128)}) custom-call(s32[1,4]{1,0:T(1,128)} %lengths.3, bf16[128,768]{1,0:T(8,128)(2,1)} %bitcast.49, bf16[128,768]{1,0:T(8,128)(2,1)} %bitcast.51, ...), custom_call_target="tpu_custom_call" | custom-call | tf_op jit(solution)/shard_map/backward/pallas_call | solution.py:1083
  225.0 1.6 slice.41
  226.5 2.4 copy.60
  229.0 1.4 copy.61
  230.4 0.2 reshape.52
  230.6 0.2 copy.50
  230.8 0.2 reshape.53
  231.0 1.4 broadcast_multiply_fusion
  232.4 1.0 slice.42
  233.4 1.1 copy.62
  234.5 0.7 slice.40
  235.2 0.6 slice.32
  235.9 0.6 slice_bitcast_fusion
  236.5 0.5 slice_bitcast_fusion.1
  237.0 0.7 copy.66
  237.6 0.7 copy.67
  (33 shorter events, 0.3 us)
Async XLA Ops:
  0.6 2.9 %copy-start.6 = (bf16[64,2,768]{2,1,0:T(2,128)(2,1)S(1)}, bf16[64,2,768]{2,1,0:T(2,128)(2,1)}, u32[]{:S(2)}) copy-start(bf16[64,2,768]{2,1,0:T(2,128)(2,1)} %param.25) | copy-start | bytes 589828
  0.7 2.8 %copy-start.1 = (bf16[64,4,2,768]{3,2,1,0:T(2,128)(2,1)S(1)}, bf16[64,4,2,768]{3,2,1,0:T(2,128)(2,1)}, u32[]{:S(2)}) copy-start(bf16[64,4,2,768]{3,2,1,0:T(2,128)(2,1)} %param.23) | copy-start | bytes 2359300
  3.5 1.4 copy-start.9
  4.8 1.0 copy-start.4
  6.3 1.3 copy-start.10
  6.3 2.1 copy-start.11
  6.3 2.1 copy-start.12
  6.3 2.1 copy-start.13
  226.5 2.4 copy-start
  228.9 1.5 copy-start.7
  229.0 2.0 copy-start.2
  230.8 4.4 %copy-start.8 = (f32[32,768]{1,0:T(8,128)S(1)}, f32[32,768]{1,0:T(8,128)}, u32[]{:S(2)}) copy-start(f32[32,768]{1,0:T(8,128)} %get-tuple-element.54) | copy-start | bytes 294916
  230.8 6.2 %copy-start.5 = (bf16[128,768]{1,0:T(8,128)(2,1)S(1)}, bf16[128,768]{1,0:T(8,128)(2,1)}, u32[]{:S(2)}) copy-start(bf16[128,768]{1,0:T(8,128)(2,1)} %get-tuple-element.51) | copy-start | bytes 589828
  231.0 6.7 %copy-start.3 = (f32[128,768]{1,0:T(8,128)S(1)}, f32[128,768]{1,0:T(8,128)}, u32[]{:S(2)}) copy-start(f32[128,768]{1,0:T(8,128)} %get-tuple-element.52) | copy-start | bytes 1179652
